TPU v7x, 128 devices: a whole 4x4x4 slice. The times are simulated.
128 devices in a mesh: row: 16 (over z, x), col: 8 (over y, core).
Axes of the slice: x: 4, y: 4, z: 4, core: 2. Of those that a mesh axis runs over, the one named last changes fastest.
Arguments:
- charges: bfloat16 [65536, 512], P(('row', 'col')), may hold values from -6 to 6
- send_order: int32 [128, 512], P(('row', 'col')), may hold values from 0 to 511, each once within a row
- near_rows: int32 [128, 160], P(('row', 'col')), may hold values from 0 to 15, as said below
- near_cols: int32 [128, 160], P(('row', 'col')), may hold values from 0 to 31, as said below
- near_count: int32 [128], P(('row', 'col')), may hold values from 40 to 160, as said below
- near_blocks: bfloat16 [128, 160, 256, 256], P(('row', 'col')), may hold values from -0.0625 to 0.0625
- far_rows: int32 [128, 64], P(('row', 'col')), may hold values from 0 to 15, as said below
- far_cols: int32 [128, 64], P(('row', 'col')), may hold values from 0 to 31, as said below
- far_count: int32 [128], P(('row', 'col')), may hold values from 32 to 64, as said below
- couplings: bfloat16 [128, 64, 32, 32], P(('row', 'col')), may hold values from -0.25 to 0.25
- row_basis: bfloat16 [256, 32, 256], P('row'), may hold values from -1 to 1
- col_basis: bfloat16 [256, 32, 256], P(('row', 'col')), may hold values from -0.375 to 0.375
Outputs:
- potential: bfloat16 [65536, 512], P(('row', 'col'))
Inputs may be any that keep to these rules, and one draw needn't show every extreme that they name: `send_order`: each row j orders the 512 panels of device j once; its places d * 4 to (d + 1) * 4 - 1 are the panels bound for device d. `near_rows`: the live slots of one device name distinct pairs with near_cols, and slots at or beyond the count hold target 0 and column r * 2. On device r * 8 + c, near_cols // 2 differs from r by at most 2. `near_count`: some devices hold the full 160. `far_rows`: every slot of one device names a distinct pair with far_cols. On device r * 8 + c, far_cols // 2 differs from r by more than 2. `far_count`: some device holds the full 64.
All inputs are finite; a program needn't handle non-finite values.
Results may differ from a plain program's by a relative error of at most 0.017.
Values may be sent and summed in bfloat16 or wider, within the bound.
No kernel may reach another device: no remote copies, remote signals or barrier semaphores. Data moves between devices by JAX's collectives and lax.ppermute only.
A program may use at most 128 MiB of HBM per device.

v0:
```python
import jax
import jax.numpy as jnp
from jax import lax
from jax.sharding import PartitionSpec as P

slot_group = 8


def shards(
    charges,
    send_order,
    near_rows,
    near_cols,
    near_count,
    near_blocks,
    far_rows,
    far_cols,
    far_count,
    couplings,
    row_basis,
    col_basis,
):
    row_count = lax.axis_size("row")
    col_count = lax.axis_size("col")
    device_count = row_count * col_count
    panels, excitations = charges.shape
    segment = panels // device_count
    owned_clusters, rank_size, leaf_size = col_basis.shape
    target_clusters = row_basis.shape[0]
    outgoing = jnp.take(charges, send_order[0], axis=0)
    incoming = lax.all_to_all(
        outgoing.reshape(device_count, segment, excitations),
        ("row", "col"),
        split_axis=0,
        concat_axis=0,
        tiled=True,
    )
    own_slab = incoming.reshape(owned_clusters, leaf_size, excitations)
    moments = jnp.einsum(
        "gkb,gbr->gkr", col_basis, own_slab, preferred_element_type=jnp.float32
    ).astype(jnp.bfloat16)
    sources, source_moments = (
        lax.all_gather(own_slab, "row", axis=0, tiled=True),
        lax.all_gather(moments, "row", axis=0, tiled=True),
    )
    local_cols = near_cols[0]
    live_near = near_count[0]
    target_rows = near_rows[0]
    blocks = near_blocks[0]

    def near_step(group_index, running):
        first_slot = group_index * slot_group
        block_tile = lax.dynamic_slice_in_dim(blocks, first_slot, slot_group, 0)
        slot_cols = lax.dynamic_slice_in_dim(local_cols, first_slot, slot_group, 0)
        slot_rows = lax.dynamic_slice_in_dim(target_rows, first_slot, slot_group, 0)
        live_slots = first_slot + jnp.arange(slot_group, dtype=jnp.int32) < live_near
        gathered = jnp.take(sources, slot_cols, axis=0)
        product = jnp.einsum(
            "sij,sjr->sir", block_tile, gathered, preferred_element_type=jnp.float32
        )
        product = jnp.where(live_slots[:, None, None], product, 0.0)
        return running.at[slot_rows].add(product)

    group_total = (live_near + slot_group - 1) // slot_group
    near_part = lax.fori_loop(
        0, group_total, near_step, jnp.zeros((target_clusters, leaf_size, excitations), jnp.float32)
    )
    far_slots = far_cols[0]
    far_live = jnp.arange(far_slots.shape[0], dtype=jnp.int32) < far_count[0]
    far_gathered = jnp.take(source_moments, far_slots, axis=0)
    coupled = jnp.einsum(
        "pkl,plr->pkr", couplings[0], far_gathered, preferred_element_type=jnp.float32
    )
    coupled = jnp.where(far_live[:, None, None], coupled, 0.0)
    far_part = (
        jnp.zeros((target_clusters, rank_size, excitations), jnp.float32)
        .at[far_rows[0]]
        .add(coupled)
    )
    expanded = jnp.einsum(
        "gkb,gkr->gbr", row_basis.astype(jnp.float32), far_part, precision=lax.Precision.HIGHEST
    )
    result = lax.psum_scatter(
        (near_part + expanded).astype(jnp.bfloat16), "col", scatter_dimension=0, tiled=True
    ).astype(jnp.float32)
    return result.reshape(panels, excitations).astype(jnp.bfloat16)


def solution(mesh):
    placed = (
        P(("row", "col"), None),
        P(("row", "col"), None),
        P(("row", "col"), None),
        P(("row", "col"), None),
        P(("row", "col")),
        P(("row", "col"), None, None, None),
        P(("row", "col"), None),
        P(("row", "col"), None),
        P(("row", "col")),
        P(("row", "col"), None, None, None),
        P("row", None, None),
        P(("row", "col"), None, None),
    )
    return jax.shard_map(
        shards, mesh=mesh, in_specs=placed, out_specs=P(("row", "col"), None), check_vma=False
    )
```

profile of v0, /device:TPU:1, one launch (start us, length us, event | category | flops | bytes accessed | tf_op | source)
XLA Modules:
  0.0 614.7 jit_solution(6248720853515782450)
XLA Ops:
  6.5 0.8 compare_select_fusion.3
  7.3 0.3 copy-done
  7.6 2.0 gather_fusion.1
  9.6 0.1 gather.15
  9.7 0.5 broadcast.121
  10.2 0.7 reduce.3
  10.9 0.1 squeeze.35
  11.0 0.3 broadcast_select_fusion
  11.4 24.8 %all_to_all.5 = bf16[128,4,512]{2,1,0:T(4,128)(2,1)S(1)} all-to-all(bf16[128,4,512]{2,1,0:T(4,128)(2,1)S(1)} %broadcast_select_fusion), channel_id=1, replica_groups=mesh['row'=16,'col'=8] {'row','col'}, dimensions={0} | all-to-all | bytes 1048576 | tf_op jit(solution)/shard_map/all_to_all | solution.py:31
  36.2 0.1 reshape.122
  36.3 0.8 fusion.9
  37.2 0.7 all-gather.3.cloned.1.call-update
  39.3 0.8 copy.16
  40.2 34.9 %all-gather.5.cloned.1.call-done = bf16[32,32,512]{2,1,0:T(8,128)(2,1)} async-done(((bf16[2,32,512]{2,1,0:T(8,128)(2,1)}), bf16[32,32,512]{2,1,0:T(8,128)(2,1)}) %all-gather.5.cloned.1.call-update) | async-done | bytes 1048592 | tf_op jit(solution)/shard_map/all_gather | solution.py:44
  75.0 1.9 gather_fusion.2
  77.0 2.7 select_bitcast_fusion
  79.7 0.1 broadcast_in_dim.71
  79.8 8.9 %scatter_fusion.1 = f32[16,32,512]{2,1,0:T(8,128)S(1)} fusion(f32[16,32,512]{2,1,0:T(8,128)S(1)} %broadcast_in_dim.71, s32[64]{0:T(128)S(1)} %fusion.11, f32[64,32,512]{2,1,0:T(8,128)} %select_bitcast_fusion), kind=kCustom, calls=%fused_computation.4 | custom fusion | flops 1048576 | bytes 12583168 | tf_op jit(solution)/shard_map/scatter-add | solution.py:78
  88.7 60.1 %all-gather.3.cloned.1.call-done = bf16[32,256,512]{2,1,0:T(8,128)(2,1)} async-done(((bf16[2,256,512]{2,1,0:T(8,128)(2,1)}), bf16[32,256,512]{2,1,0:T(8,128)(2,1)}) %all-gather.3.cloned.1.call-update) | async-done | bytes 8388624 | tf_op jit(solution)/shard_map/all_gather | solution.py:43
  148.8 4.3 broadcast_in_dim.68
  153.1 181.3 %while.10 = (s32[]{:T(128)}, f32[16,256,512]{2,1,0:T(8,128)}, s32[]{:T(128)}, s32[160]{0:T(256)S(1)}, s32[]{:T(128)}, /*index=5*/bf16[160,256,256]{2,1,0:T(8,128...) while((s32[]{:T(128)}, f32[16,256,512]{2,1,0:T(8,128)}, ...), condition=%wide.region_2.3_spmd, body=%wide.region_0.0_spmd.sunk | while | flops 540017728 | bytes 24121784 | solution.py:65
  153.1 0.7 compare_and_fusion.4
  153.9 5.4 gather_fusion
  159.3 4.7 convolution_select_fusion.2
  163.9 0.1 compare_select_fusion.9
  164.0 9.3 %scatter_fusion = f32[16,256,512]{2,1,0:T(8,128)} fusion(f32[16,256,512]{2,1,0:T(8,128)} %get-tuple-element.139, s32[8]{0:T(128)S(1)} %compare_select_fusion.9, f32[8,256,512]{2,1,0:T(8,128)} %convolution_select_fusion.2), kind=kCustom, calls=%fused_computation.3.clone.1 | custom fusion | flops 1048576 | bytes 12582944 | tf_op jit(solution)/shard_map/while/body/scatter-add | solution.py:62
  173.3 0.7 compare_and_fusion.4
  174.0 5.4 gather_fusion
  179.4 4.7 convolution_select_fusion.2
  184.0 0.1 compare_select_fusion.9
  184.1 9.6 %scatter_fusion = f32[16,256,512]{2,1,0:T(8,128)} fusion(f32[16,256,512]{2,1,0:T(8,128)} %get-tuple-element.139, s32[8]{0:T(128)S(1)} %compare_select_fusion.9, f32[8,256,512]{2,1,0:T(8,128)} %convolution_select_fusion.2), kind=kCustom, calls=%fused_computation.3.clone.1 | custom fusion | flops 1048576 | bytes 12582944 | tf_op jit(solution)/shard_map/while/body/scatter-add | solution.py:62
  193.7 0.7 compare_and_fusion.4
  194.4 5.4 gather_fusion
  199.8 4.7 convolution_select_fusion.2
  204.5 9.3 %scatter_fusion = f32[16,256,512]{2,1,0:T(8,128)} fusion(f32[16,256,512]{2,1,0:T(8,128)} %get-tuple-element.139, s32[8]{0:T(128)S(1)} %compare_select_fusion.9, f32[8,256,512]{2,1,0:T(8,128)} %convolution_select_fusion.2), kind=kCustom, calls=%fused_computation.3.clone.1 | custom fusion | flops 1048576 | bytes 12582944 | tf_op jit(solution)/shard_map/while/body/scatter-add | solution.py:62
  213.8 0.7 compare_and_fusion.4
  214.5 5.4 gather_fusion
  219.9 4.7 convolution_select_fusion.2
  224.6 9.1 %scatter_fusion = f32[16,256,512]{2,1,0:T(8,128)} fusion(f32[16,256,512]{2,1,0:T(8,128)} %get-tuple-element.139, s32[8]{0:T(128)S(1)} %compare_select_fusion.9, f32[8,256,512]{2,1,0:T(8,128)} %convolution_select_fusion.2), kind=kCustom, calls=%fused_computation.3.clone.1 | custom fusion | flops 1048576 | bytes 12582944 | tf_op jit(solution)/shard_map/while/body/scatter-add | solution.py:62
  233.7 0.7 compare_and_fusion.4
  234.4 5.4 gather_fusion
  239.8 4.7 convolution_select_fusion.2
  244.6 9.4 %scatter_fusion = f32[16,256,512]{2,1,0:T(8,128)} fusion(f32[16,256,512]{2,1,0:T(8,128)} %get-tuple-element.139, s32[8]{0:T(128)S(1)} %compare_select_fusion.9, f32[8,256,512]{2,1,0:T(8,128)} %convolution_select_fusion.2), kind=kCustom, calls=%fused_computation.3.clone.1 | custom fusion | flops 1048576 | bytes 12582944 | tf_op jit(solution)/shard_map/while/body/scatter-add | solution.py:62
  254.0 0.7 compare_and_fusion.4
  254.7 5.4 gather_fusion
  260.1 4.7 convolution_select_fusion.2
  264.8 0.1 compare_select_fusion.9
  264.8 9.4 %scatter_fusion = f32[16,256,512]{2,1,0:T(8,128)} fusion(f32[16,256,512]{2,1,0:T(8,128)} %get-tuple-element.139, s32[8]{0:T(128)S(1)} %compare_select_fusion.9, f32[8,256,512]{2,1,0:T(8,128)} %convolution_select_fusion.2), kind=kCustom, calls=%fused_computation.3.clone.1 | custom fusion | flops 1048576 | bytes 12582944 | tf_op jit(solution)/shard_map/while/body/scatter-add | solution.py:62
  274.2 0.7 compare_and_fusion.4
  275.0 5.4 gather_fusion
  280.4 4.7 convolution_select_fusion.2
  285.1 9.3 %scatter_fusion = f32[16,256,512]{2,1,0:T(8,128)} fusion(f32[16,256,512]{2,1,0:T(8,128)} %get-tuple-element.139, s32[8]{0:T(128)S(1)} %compare_select_fusion.9, f32[8,256,512]{2,1,0:T(8,128)} %convolution_select_fusion.2), kind=kCustom, calls=%fused_computation.3.clone.1 | custom fusion | flops 1048576 | bytes 12582944 | tf_op jit(solution)/shard_map/while/body/scatter-add | solution.py:62
  294.4 0.7 compare_and_fusion.4
  295.1 5.4 gather_fusion
  300.5 4.7 convolution_select_fusion.2
  305.2 9.5 %scatter_fusion = f32[16,256,512]{2,1,0:T(8,128)} fusion(f32[16,256,512]{2,1,0:T(8,128)} %get-tuple-element.139, s32[8]{0:T(128)S(1)} %compare_select_fusion.9, f32[8,256,512]{2,1,0:T(8,128)} %convolution_select_fusion.2), kind=kCustom, calls=%fused_computation.3.clone.1 | custom fusion | flops 1048576 | bytes 12582944 | tf_op jit(solution)/shard_map/while/body/scatter-add | solution.py:62
  314.7 0.7 compare_and_fusion.4
  315.5 5.4 gather_fusion
  320.8 4.7 convolution_select_fusion.2
  325.6 8.8 %scatter_fusion = f32[16,256,512]{2,1,0:T(8,128)} fusion(f32[16,256,512]{2,1,0:T(8,128)} %get-tuple-element.139, s32[8]{0:T(128)S(1)} %compare_select_fusion.9, f32[8,256,512]{2,1,0:T(8,128)} %convolution_select_fusion.2), kind=kCustom, calls=%fused_computation.3.clone.1 | custom fusion | flops 1048576 | bytes 12582944 | tf_op jit(solution)/shard_map/while/body/scatter-add | solution.py:62
  334.4 9.3 %copy.17 = f32[16,256,512]{1,2,0:T(8,128)} copy(f32[16,256,512]{2,1,0:T(8,128)} %get-tuple-element.48) | data formatting | bytes 16777216 | tf_op jit(solution)/shard_map/while | solution.py:65
  343.8 7.5 %fusion.6 = bf16[16,256,512]{1,2,0:T(8,128)(2,1)} fusion(f32[16,256,512]{1,2,0:T(8,128)} %copy.17, f32[16,32,512]{2,1,0:T(8,128)S(1)} %scatter_fusion.1, bf16[16,32,256]{2,1,0:T(8,128)(2,1)S(1)} %copy-done.4), kind=kOutput, calls=%fused_computation.18 | convolution fusion | flops 809500672 | bytes 13893632 | tf_op jit(solution)/shard_map/gkb,gkr->gbr/dot_general | solution.py:80
  351.2 254.9 %reduce-scatter.2.cloned.1.call-done = bf16[2,256,512]{1,2,0:T(8,128)(2,1)} async-done(((bf16[16,256,512]{1,2,0:T(8,128)(2,1)}), bf16[2,256,512]{1,2,0:T(8,128)(2,1)}) %reduce-scatter.2.cloned.1.call-update) | async-done | bytes 524304 | tf_op jit(solution)/shard_map/reduce_scatter | solution.py:83
  606.2 2.0 copy.18
  (47 shorter events, 0.7 us)
Async XLA Ops:
  6.5 1.1 copy-start
  6.5 3.7 copy-start.6
  6.5 68.5 %all-gather.5.cloned.1.call-start = ((), (), s32[]{:S(2)}) async-start(), calls=%async_computation.3 | async-start | bytes 1114112 | tf_op jit(solution)/shard_map/all_gather | solution.py:44
  7.6 28.7 %copy-start.5 = (bf16[2,32,256]{2,1,0:T(8,128)(2,1)S(1)}, bf16[2,32,256]{2,1,0:T(8,128)(2,1)}, u32[]{:S(2)}) copy-start(bf16[2,32,256]{2,1,0:T(8,128)(2,1)} %param.25) | copy-start | bytes 98308
  7.6 31.7 %copy-start.3 = (bf16[1,64,32,32]{1,3,2,0:T(8,128)(2,1)S(1)}, bf16[1,64,32,32]{1,3,2,0:T(8,128)(2,1)}, u32[]{:S(2)}) copy-start(bf16[1,64,32,32]{1,3,2,0:T(8,128)(2,1)} %param.23) | copy-start | bytes 393220
  9.6 30.5 %copy-start.8 = (s32[1,64]{1,0:T(1,128)S(1)}, s32[1,64]{1,0:T(1,128)}, u32[]{:S(2)}) copy-start(s32[1,64]{1,0:T(1,128)} %param.21) | copy-start | bytes 772
  9.6 30.6 %copy-start.10 = (s32[1,64]{1,0:T(1,128)S(1)}, s32[1,64]{1,0:T(1,128)}, u32[]{:S(2)}) copy-start(s32[1,64]{1,0:T(1,128)} %param.20) | copy-start | bytes 772
  36.3 0.9 copy-start.2
  37.2 111.6 %all-gather.3.cloned.1.call-start = ((), (), s32[]{:S(2)}) async-start(), calls=%async_computation.2 | async-start | bytes 8912896 | tf_op jit(solution)/shard_map/all_gather | solution.py:43
  37.9 568.2 %reduce-scatter.2.cloned.1.call-start = ((), (), s32[]{:S(2)}) async-start(), calls=%async_computation.4 | async-start | bytes 4718592 | tf_op jit(solution)/shard_map/reduce_scatter | solution.py:83
  148.8 4.3 copy-start.7
  148.8 4.3 copy-start.9
  334.4 9.3 %copy-start.4 = (bf16[16,32,256]{2,1,0:T(8,128)(2,1)S(1)}, bf16[16,32,256]{2,1,0:T(8,128)(2,1)}, u32[]{:S(2)}) copy-start(bf16[16,32,256]{2,1,0:T(8,128)(2,1)} %param.24) | copy-start | bytes 786436
  343.7 264.5 %copy-start.1 = (bf16[512,512]{1,0:T(8,128)(2,1)S(1)}, bf16[512,512]{1,0:T(8,128)(2,1)}, u32[]{:S(2)}) copy-start(bf16[512,512]{1,0:T(8,128)(2,1)} %param.14) | copy-start | bytes 1572868
Sparse Core Ops, SparseCore 0:
  37.3 37.6 all-gather.4
  77.2 71.5 all-gather.2
  351.4 254.7 reduce-scatter.1
where the time goes:
time: 619 us; the launch traced here: 615 us
  waiting for transfers between devices  351 us (57%)
  other arithmetic  102 us (16%)
  local copies, waits for them, and re-layouts  70.1 us (11%)
  matrix products  52.9 us (9%)
  blocking collectives  24.8 us (4%)
  between operations  14.6 us (2%)
    reduce_scatter x1, waiting for transfers between devices, shards(): lax.psum_scatter((near_part + expanded).astype(jnp.bfloat16), 'col', scat...  255 us
    scatter-add x9, other arithmetic, near_step(): return running.at[slot_rows].add(product)  83.6 us
    all_gather x1, waiting for transfers between devices, shards(): lax.all_gather(own_slab, 'row', axis=0, tiled=True)  60.1 us
    gather x9, local copies, waits for them, and re-layouts, near_step(): gathered = jnp.take(sources, slot_cols, axis=0)  48.5 us
    dot_general x9, matrix products, near_step(): jnp.einsum('sij,sjr->sir', block_tile, gathered, preferred_element_type=j...  41.9 us
    all_gather x1, waiting for transfers between devices, shards(): lax.all_gather(moments, 'row', axis=0, tiled=True)  34.9 us
    all_to_all x1, blocking collectives, shards(): lax.all_to_all(outgoing.reshape(device_count, segment, excitations), ('ro...  24.8 us
  transfers between devices with their start and end apart: 3, of which 3 were waited for; matrix products, arithmetic and copies ran while one was open for 2% of the time, Pallas kernels for 0%

commit v1 on v0

v1 whole, which is shorter than its diff:
```python
import jax
import jax.numpy as jnp
from jax import lax
from jax.experimental import pallas as pl
from jax.experimental.pallas import tpu as pltpu
from jax.sharding import PartitionSpec as P

reach = 2


def far_kernel(cols_ref, moments_ref, coupling_ref, rows_ref, out_ref, gathered, spread):
    slots = cols_ref.shape[0]
    rank = coupling_ref.shape[0]
    targets = out_ref.shape[0]

    def pick(slot, carry):
        source = pl.multiple_of(cols_ref[slot] * rank, rank)
        place = pl.multiple_of(slot * rank, rank)
        gathered[pl.ds(place, rank), :] = moments_ref[pl.ds(source, rank), :]
        return carry

    lax.fori_loop(0, slots, pick, 0)
    couplings = coupling_ref[...]
    rows = rows_ref[...]
    for target in range(targets):
        spread[target * rank : (target + 1) * rank, :] = jnp.where(
            rows == target, couplings, jnp.zeros_like(couplings)
        )
    incoming = jnp.dot(spread[...], gathered[...], preferred_element_type=jnp.float32)
    high = incoming.astype(jnp.bfloat16)
    rest = incoming - high.astype(jnp.float32)
    middle = rest.astype(jnp.bfloat16)
    low = (rest - middle.astype(jnp.float32)).astype(jnp.bfloat16)
    for target in range(targets):
        own = slice(target * rank, (target + 1) * rank)
        out_ref[target, 0:rank, :] = high[own]
        out_ref[target, rank : 2 * rank, :] = middle[own]
        out_ref[target, 2 * rank : 3 * rank, :] = low[own]


def far_incoming(far_cols, moments, coupling_rows, slot_rows, targets):
    rank, width = coupling_rows.shape
    excitations = moments.shape[1]
    return pl.pallas_call(
        far_kernel,
        grid_spec=pltpu.PrefetchScalarGridSpec(
            num_scalar_prefetch=1,
            grid=(1,),
            in_specs=[
                pl.BlockSpec(moments.shape, lambda i, *_: (0, 0)),
                pl.BlockSpec(coupling_rows.shape, lambda i, *_: (0, 0)),
                pl.BlockSpec(slot_rows.shape, lambda i, *_: (0, 0)),
            ],
            out_specs=pl.BlockSpec((targets, 3 * rank, excitations), lambda i, *_: (0, 0, 0)),
            scratch_shapes=[
                pltpu.VMEM((width, excitations), jnp.bfloat16),
                pltpu.VMEM((targets * rank, width), jnp.bfloat16),
            ],
        ),
        out_shape=jax.ShapeDtypeStruct((targets, 3 * rank, excitations), jnp.bfloat16),
        compiler_params=pltpu.CompilerParams(vmem_limit_bytes=32 * 2**20),
        cost_estimate=pl.CostEstimate(
            flops=2 * targets * rank * width * excitations,
            bytes_accessed=8 * 2**20,
            transcendentals=0,
        ),
        name="far_incoming",
    )(far_cols, moments, coupling_rows, slot_rows)


def near_kernel(
    place_ref, target_ref, blocks_ref, *rest
):
    parts = rest[: 2 * reach + 1]
    far_ref, basis_ref, out_ref = rest[2 * reach + 1 : 2 * reach + 4]
    held, sources, far, basis, result = rest[2 * reach + 4 : 2 * reach + 9]
    held_sem, source_sem, far_sem, basis_sem, result_sem = rest[2 * reach + 9 :]
    count = target_ref.shape[0]
    size = blocks_ref.shape[1]
    per_target = sources.shape[0] // size
    part_rows = parts[0].shape[0]

    def block_copy(step, source):
        slot = place_ref[target_ref[step] * per_target + source]
        return slot, pltpu.make_async_copy(
            blocks_ref.at[jnp.maximum(slot, 0)],
            held.at[step, :, pl.ds(source * size, size)],
            held_sem.at[step, source],
        )

    def far_copies(step):
        target = target_ref[step]
        return (
            pltpu.make_async_copy(far_ref.at[target], far.at[step], far_sem.at[step]),
            pltpu.make_async_copy(basis_ref.at[target], basis.at[step], basis_sem.at[step]),
        )

    def source_copy(index):
        return pltpu.make_async_copy(
            parts[index],
            sources.at[pl.ds(index * part_rows, part_rows), :],
            source_sem.at[index],
        )

    def result_copy(step):
        return pltpu.make_async_copy(result.at[step], out_ref.at[step], result_sem.at[step])

    for index in range(len(parts)):
        source_copy(index).start()

    def begin(step, carry):
        for copy in far_copies(step):
            copy.start()
        for source in range(per_target):
            slot, copy = block_copy(step, source)

            @pl.when(slot >= 0)
            def _():
                copy.start()

            @pl.when(slot < 0)
            def _():
                held[step, :, source * size : (source + 1) * size] = jnp.zeros(
                    (size, size), held.dtype
                )

        return carry

    lax.fori_loop(0, count, begin, 0)
    for index in range(len(parts)):
        source_copy(index).wait()

    def work(step, carry):
        for copy in far_copies(step):
            copy.wait()
        for source in range(per_target):
            slot, copy = block_copy(step, source)

            @pl.when(slot >= 0)
            def _():
                copy.wait()

        total = jnp.dot(held[step], sources[...], preferred_element_type=jnp.float32)
        total = total + jnp.dot(basis[step], far[step], preferred_element_type=jnp.float32)
        result[step] = total.astype(result.dtype)
        result_copy(step).start()
        return carry

    lax.fori_loop(0, count, work, 0)

    def finish(step, carry):
        result_copy(step).wait()
        return carry

    lax.fori_loop(0, count, finish, 0)


def near_terms(place, targets, blocks, parts, far, basis):
    count = targets.shape[0]
    size = blocks.shape[1]
    part_rows, excitations = parts[0].shape
    depth = part_rows * len(parts)
    anywhere = pl.BlockSpec(memory_space=pl.ANY)
    return pl.pallas_call(
        near_kernel,
        grid_spec=pltpu.PrefetchScalarGridSpec(
            num_scalar_prefetch=2,
            grid=(1,),
            in_specs=[anywhere] * (3 + len(parts)),
            out_specs=anywhere,
            scratch_shapes=[
                pltpu.VMEM((count, size, depth), jnp.bfloat16),
                pltpu.VMEM((depth, excitations), jnp.bfloat16),
                pltpu.VMEM((count,) + far.shape[1:], jnp.bfloat16),
                pltpu.VMEM((count,) + basis.shape[1:], jnp.bfloat16),
                pltpu.VMEM((count, size, excitations), jnp.bfloat16),
                pltpu.SemaphoreType.DMA((count, depth // size)),
                pltpu.SemaphoreType.DMA((len(parts),)),
                pltpu.SemaphoreType.DMA((count,)),
                pltpu.SemaphoreType.DMA((count,)),
                pltpu.SemaphoreType.DMA((count,)),
            ],
        ),
        out_shape=jax.ShapeDtypeStruct((count, size, excitations), jnp.bfloat16),
        compiler_params=pltpu.CompilerParams(vmem_limit_bytes=40 * 2**20),
        cost_estimate=pl.CostEstimate(
            flops=2 * count * size * depth * excitations,
            bytes_accessed=2 * (count * size * depth + depth * excitations),
            transcendentals=0,
        ),
        name="near_terms",
    )(place, targets, blocks, *parts, far, basis)


def add(*terms):
    total = terms[0].astype(jnp.float32)
    for term in terms[1:]:
        total = total + term.astype(jnp.float32)
    return total.astype(jnp.bfloat16)


def shards(
    charges,
    send_order,
    near_rows,
    near_cols,
    near_count,
    near_blocks,
    far_rows,
    far_cols,
    far_count,
    couplings,
    row_basis,
    col_basis,
):
    row_count = lax.axis_size("row")
    col_count = lax.axis_size("col")
    device_count = row_count * col_count
    panels, excitations = charges.shape
    segment = panels // device_count
    owned, rank, leaf = col_basis.shape
    targets = row_basis.shape[0]
    window = (2 * reach + 1) * owned
    row = lax.axis_index("row")
    col = lax.axis_index("col")

    slots = jnp.arange(near_rows.shape[1], dtype=jnp.int32)
    pair = near_rows[0] * window + near_cols[0] - (row - reach) * owned
    pair = jnp.where(slots < near_count[0], pair, -1)
    wanted = jnp.arange(targets * window, dtype=jnp.int32)
    place = jnp.max(jnp.where(pair[None, :] == wanted[:, None], slots[None, :], -1), axis=1)

    far_slots = far_rows.shape[1]
    far_target = jnp.where(
        jnp.arange(far_slots, dtype=jnp.int32) < far_count[0], far_rows[0], -1
    )
    slot_rows = jnp.repeat(far_target, rank)[None, :]
    coupling_rows = couplings[0].transpose(1, 0, 2).reshape(rank, far_slots * rank)
    basis = jnp.tile(row_basis.transpose(0, 2, 1), (1, 1, 3))

    outgoing = jnp.take(charges, send_order[0], axis=0)
    incoming = lax.all_to_all(
        outgoing.reshape(device_count, segment, excitations),
        ("row", "col"),
        split_axis=0,
        concat_axis=0,
        tiled=True,
    )
    slab = incoming.reshape(panels, excitations)
    moments = (
        jnp.einsum(
            "gkb,gbr->gkr",
            col_basis,
            slab.reshape(owned, leaf, excitations),
            preferred_element_type=jnp.float32,
        )
        .astype(jnp.bfloat16)
        .reshape(owned * rank, excitations)
    )

    def row_shift(value, step):
        return lax.ppermute(value, "row", [(i, (i + step) % row_count) for i in range(row_count)])

    all_moments = lax.all_gather(moments, "row", axis=0, tiled=True)
    below, above = [slab], [slab]
    for _ in range(reach):
        below.append(row_shift(below[-1], 1))
        above.append(row_shift(above[-1], -1))
    parts = below[:0:-1] + above
    far = far_incoming(far_cols[0], all_moments, coupling_rows, slot_rows, targets)

    chips = col_count // 2
    chip, core = col // 2, col % 2
    each = jnp.arange(owned, dtype=jnp.int32)

    def clusters(chip_step, which):
        return (((chip + chip_step) % chips) * 2 + which) * owned + each

    def order(*chip_steps):
        return jnp.concatenate(
            [clusters(step, 1 - core) for step in chip_steps]
            + [clusters(step, core) for step in chip_steps]
        )

    def other_core(value):
        return lax.ppermute(value, "col", [(i, i ^ 1) for i in range(col_count)])

    def chip_shift(value, step):
        return lax.ppermute(
            value, "col", [(i, (i + 2 * step) % col_count) for i in range(col_count)]
        )

    def both_cores(terms):
        half = terms.shape[0] // 2
        return terms[half:], other_core(terms[:half])

    opposite = add(*both_cores(near_terms(place, order(2), near_blocks[0], parts, far, basis)))
    opposite, place = lax.optimization_barrier((opposite, place))
    from_below = chip_shift(opposite[:1], 1)
    from_above = chip_shift(opposite[1:], -1)
    kept, got = both_cores(near_terms(place, order(1, -1), near_blocks[0], parts, far, basis))
    zero = jnp.zeros_like(from_below)
    passing = jnp.concatenate([from_below, zero, zero, from_above])
    sides = add(kept, got, passing)
    sides, place = lax.optimization_barrier((sides, place))
    side_below = chip_shift(sides[:owned], 1)
    side_above = chip_shift(sides[owned:], -1)
    kept, got = both_cores(near_terms(place, order(0), near_blocks[0], parts, far, basis))
    return add(kept, got, side_below, side_above).reshape(panels, excitations)


def solution(mesh):
    placed = (
        P(("row", "col"), None),
        P(("row", "col"), None),
        P(("row", "col"), None),
        P(("row", "col"), None),
        P(("row", "col")),
        P(("row", "col"), None, None, None),
        P(("row", "col"), None),
        P(("row", "col"), None),
        P(("row", "col")),
        P(("row", "col"), None, None, None),
        P("row", None, None),
        P(("row", "col"), None, None),
    )
    return jax.shard_map(
        shards, mesh=mesh, in_specs=placed, out_specs=P(("row", "col"), None), check_vma=False
    )
```

time: 619 us -> 163 us (0.26)
  waiting for transfers between devices: 351 us -> 58.7 us
  other arithmetic: 102 us -> 7.35 us
  local copies, waits for them, and re-layouts: 70.1 us -> 12.1 us
  matrix products: 52.9 us -> 0.82 us
  Pallas kernels: 0 us -> 28.5 us
  starting transfers between devices: 0.08 us -> 15.1 us
    reduce_scatter x1 -> x0, waiting for transfers between devices: 255 us -> none  [shards(): lax.psum_scatter((near_part + expanded).astype(jnp.bfloat16), 'col', scat...]
    scatter-add x10 -> x0, other arithmetic: 92.5 us -> none  [the longest x9 83.6 us: near_step(): return running.at[slot_rows].add(product)]
    all_gather x2 -> x1, waiting for transfers between devices: 95 us -> 30 us  [shards(): all_moments = lax.all_gather(moments, 'row', axis=0, tiled=True)]
    dot_general x12 -> x1, matrix products: 52.9 us -> 0.82 us  [shards(): jnp.einsum('gkb,gbr->gkr', col_basis, slab.reshape(owned, leaf, excitatio...]
    gather x10 -> x0, local copies, waits for them, and re-layouts: 50.4 us -> none  [the longest x9 48.5 us: near_step(): gathered = jnp.take(sources, slot_cols, axis=0)]
    ppermute x0 -> x11, waiting for transfers between devices: none -> 28.7 us  [the longest x4 18.6 us: chip_shift(): lax.ppermute(value, 'col', [(i, (i + 2 * step) % col_count) for i in rang...]
    pallas_call x0 -> x4, Pallas kernels: none -> 28.5 us  [the longest x3 26.1 us: near_terms(): pl.pallas_call(near_kernel, grid_spec=pltpu.PrefetchScalarGridSpec(num_sc...]
    ppermute x0 -> x11, starting transfers between devices: none -> 15.1 us  [the longest x4 6.03 us: row_shift(): lax.ppermute(value, 'row', [(i, (i + step) % row_count) for i in range(ro...]
  transfers between devices with their start and end apart: 3 -> 12, of which waited for: 3 -> 6; matrix products, arithmetic and copies ran while one was open for 2% -> 2% of each run, Pallas kernels for 0% -> 1%
where the time goes in v1:
time: 163 us; the launch traced here: 162 us
  waiting for transfers between devices  58.7 us (36%)
  Pallas kernels  28.5 us (17%)
  blocking collectives  24.8 us (15%)
  starting transfers between devices  15.1 us (9%)
  between operations  15 us (9%)
  local copies, waits for them, and re-layouts  12.1 us (7%)
  other arithmetic  7.35 us (5%)
    all_gather x1, waiting for transfers between devices, shards(): all_moments = lax.all_gather(moments, 'row', axis=0, tiled=True)  30 us
    pallas_call x3, Pallas kernels, near_terms(): pl.pallas_call(near_kernel, grid_spec=pltpu.PrefetchScalarGridSpec(num_sc...  26.1 us
    all_to_all x1, blocking collectives, shards(): lax.all_to_all(outgoing.reshape(device_count, segment, excitations), ('ro...  24.8 us
    ppermute x4, waiting for transfers between devices, chip_shift(): lax.ppermute(value, 'col', [(i, (i + 2 * step) % col_count) for i in rang...  18.6 us
    ppermute x4, waiting for transfers between devices, row_shift(): lax.ppermute(value, 'row', [(i, (i + step) % row_count) for i in range(ro...  8.3 us
    ppermute x4, starting transfers between devices, row_shift(): lax.ppermute(value, 'row', [(i, (i + step) % row_count) for i in range(ro...  6.03 us
    ppermute x4, starting transfers between devices, chip_shift(): lax.ppermute(value, 'col', [(i, (i + 2 * step) % col_count) for i in rang...  5.44 us
    unnamed x31, local copies, waits for them, and re-layouts  5.2 us
  transfers between devices with their start and end apart: 12, of which 6 were waited for; matrix products, arithmetic and copies ran while one was open for 2% of the time, Pallas kernels for 1%

profile of v1, /device:TPU:1, one launch (start us, length us, event | category | flops | bytes accessed | tf_op | source)
XLA Modules:
  0.0 162.5 jit_solution(4459966823452638957)
XLA Ops:
  6.5 0.7 compare_select_fusion.1
  7.3 0.5 broadcast.59
  7.8 1.3 reduce.3
  9.1 0.1 squeeze.29
  9.3 2.0 %gather_fusion = bf16[512,512]{1,0:T(8,128)(2,1)S(1)} fusion(bf16[512,512]{1,0:T(8,128)(2,1)S(1)} %copy-done, s32[1024]{0:T(1024)S(1)} %pad_clamp_fusion), kind=kCustom, calls=%fused_computation | custom fusion | bytes 1050624 | tf_op jit(solution)/shard_map/jit(_take)/gather | solution.py:241
  11.3 0.0 copy-start.11
  11.3 0.1 gather.7
  11.4 0.3 broadcast_select_fusion
  11.8 0.0 copy-start.14
  11.8 0.0 copy-start.9
  11.8 24.8 %all_to_all.5 = bf16[128,4,512]{2,1,0:T(4,128)(2,1)S(1)} all-to-all(bf16[128,4,512]{2,1,0:T(4,128)(2,1)S(1)} %broadcast_select_fusion), channel_id=1, replica_groups=mesh['row'=16,'col'=8] {'row','col'}, dimensions={0} | all-to-all | bytes 1048576 | tf_op jit(solution)/shard_map/all_to_all | solution.py:242
  36.6 0.1 reshape_reshape.3
  36.7 0.8 convolution_convert_fusion
  37.6 0.0 all-gather.2.cloned.1.call-update
  37.6 0.1 reshape.64.rest_2_
  37.7 0.0 copy-start.1
  37.7 1.1 collective-permute-start.2
  38.8 0.4 collective-permute-start
  40.6 0.1 broadcast_in_dim.42
  40.7 0.1 broadcast_in_dim_reshape.3.rows_ref
  40.8 0.0 copy-start.12
  40.8 0.0 copy-start.13
  40.8 0.0 copy-start.8
  40.8 0.3 copy.19
  41.1 0.5 reshape.66.coupling_ref
  41.6 0.1 tile.4
  41.7 0.7 copy.20.rest_6_
  42.4 8.2 %collective-permute-done.2.rest_3_ = bf16[512,512]{1,0:T(8,128)(2,1)} collective-permute-done((bf16[512,512]{1,0:T(8,128)(2,1)S(1)}, bf16[512,512]{1,0:T(8,128)(2,1)}, u32[]{:S(2)}, u32[]{:S(2)}) %collective-permute-start.2) | collective-permute-done | bytes 524320 | tf_op jit(solution)/shard_map/ppermute | solution.py:262
  50.6 4.5 %collective-permute-start.3 = (bf16[512,512]{1,0:T(8,128)(2,1)}, bf16[512,512]{1,0:T(8,128)(2,1)}, u32[]{:S(2)}, u32[]{:S(2)}) collective-permute-start(bf16[512,512]{1,0:T(8,128)(2,1)} %collective-permute-done.2.rest_3_), channel_id=1, source_target_pairs={{0,120},{8,0},{16,8},{24,16},{32,24},{40,32},{48,40},{56,48},{64,5... | collective-permute-start | bytes 1572872 | tf_op jit(solution)/shard_map/ppermute | solution.py:262
  55.1 0.1 collective-permute-done.rest_1_
  55.2 0.1 pad_add_fusion.target_ref
  55.3 0.1 select_reduce_fusion.place_ref
  55.4 30.0 %all-gather.2.cloned.1.call-done.moments_ref = bf16[1024,512]{1,0:T(8,128)(2,1)} async-done(((bf16[64,512]{1,0:T(8,128)(2,1)}), bf16[1024,512]{1,0:T(8,128)(2,1)}) %all-gather.2.cloned.1.call-update) | async-done | bytes 1048592 | tf_op jit(solution)/shard_map/all_gather | solution.py:264
  85.4 1.3 copy-done.7
  86.7 2.4 %far_incoming.1.rest_5_ = bf16[16,96,512]{2,1,0:T(8,128)(2,1)S(1)} custom-call(s32[64]{0:T(128)S(1)} %bitcast.23, bf16[1024,512]{1,0:T(8,128)(2,1)S(1)} %copy-done.7, bf16[32,2048]{1,0:T(8,128)(2,1)S(1)} %reshape.66.coupling_ref, s32[1,2048]{1,0:T(1,128)S(1)} %broadcast_in_dim_reshape.3.rows_ref), custom_call_target="tpu_custom_call" | custom-call | flops 1073741824 | bytes 8388608 | tf_op jit(solution)/shard_map/far_incoming/pallas_call | solution.py:44
  89.1 0.0 collective-permute-done.3.rest_4_
  89.1 0.0 collective-permute-done.1.rest_0_
  89.1 6.7 %near_terms.3 = bf16[4,256,512]{2,1,0:T(8,128)(2,1)S(1)} custom-call(s32[160]{0:T(256)S(1)} %select_reduce_fusion.place_ref, s32[4]{0:T(128)S(1)} %pad_add_fusion.target_ref, bf16[160,256,256]{2,1,0:T(8,128)(2,1)} %bitcast.24, bf16[512,512]{1,0:T(8,128)(2,1)} %collective-permute-done.1.rest_0_, bf16[512,512]{1,0:T(8,128)(2,1)} %collective-permute-done.rest_1_, ...), custom_call_target="tpu_custom_call" | custom-call | flops 2684354560 | bytes 7864320 | tf_op jit(solution)/shard_map/near_terms/pallas_call | solution.py:164
  95.8 1.0 copy-done.6
  96.8 0.8 slice.43
  97.6 2.2 %collective-permute-start.4 = (bf16[2,256,512]{2,1,0:T(8,128)(2,1)}, bf16[2,256,512]{2,1,0:T(8,128)(2,1)}, u32[]{:S(2)}, u32[]{:S(2)}) collective-permute-start(bf16[2,256,512]{2,1,0:T(8,128)(2,1)} %slice.43), channel_id=1, source_target_pairs={{0,1},{1,0},{2,3},{3,2},{4,5},{5,4},{6,7},{7,6},{8,9},{9,8},{10,11... | collective-permute-start | bytes 1572872 | tf_op jit(solution)/shard_map/ppermute | solution.py:286
  99.9 0.1 pad_add_fusion.1.target_ref
  100.0 1.8 %collective-permute-done.4 = bf16[2,256,512]{2,1,0:T(8,128)(2,1)} collective-permute-done((bf16[2,256,512]{2,1,0:T(8,128)(2,1)}, bf16[2,256,512]{2,1,0:T(8,128)(2,1)}, u32[]{:S(2)}, u32[]{:S(2)}) %collective-permute-start.4) | collective-permute-done | bytes 524320 | tf_op jit(solution)/shard_map/ppermute | solution.py:286
  101.7 1.3 add_convert_fusion.2
  103.1 0.0 copy-start.3
  103.1 1.0 copy-done.3
  104.1 12.7 %near_terms.4 = bf16[8,256,512]{2,1,0:T(8,128)(2,1)S(1)} custom-call(s32[160]{0:T(256)S(1)} %select_reduce_fusion.place_ref, s32[8]{0:T(128)S(1)} %pad_add_fusion.1.target_ref, bf16[160,256,256]{2,1,0:T(8,128)(2,1)} %bitcast.25, bf16[512,512]{1,0:T(8,128)(2,1)} %collective-permute-done.1.rest_0_, bf16[512,512]{1,0:T(8,128)(2,1)} %collective-permute-done.rest_1_, ...), custom_call_target="tpu_custom_call" | custom-call | flops 5368709120 | bytes 13107200 | tf_op jit(solution)/shard_map/near_terms/pallas_call | solution.py:164
  116.9 1.3 copy-done.5
  118.2 1.0 slice.45
  119.2 0.4 collective-permute-start.5
  119.7 0.7 fusion.1
  120.4 1.1 collective-permute-start.6
  121.4 1.6 %collective-permute-start.7 = (bf16[1,256,512]{2,1,0:T(8,128)(2,1)S(1)}, bf16[1,256,512]{2,1,0:T(8,128)(2,1)}, u32[]{:S(2)}, u32[]{:S(2)}) collective-permute-start(bf16[1,256,512]{2,1,0:T(8,128)(2,1)S(1)} %get-tuple-element.16), channel_id=1, source_target_pairs={{0,6},{1,7},{2,0},{3,1},{4,2},{5,3},{6,4},{7,5},{8,14},{9,15},{10,... | collective-permute-start | bytes 786440 | tf_op jit(solution)/shard_map/ppermute | solution.py:289
  123.1 0.1 pad.3.clone
  123.2 0.1 pad_add_fusion.2.target_ref
  123.3 6.6 %collective-permute-done.6 = bf16[1,256,512]{2,1,0:T(8,128)(2,1)} collective-permute-done((bf16[1,256,512]{2,1,0:T(8,128)(2,1)}, bf16[1,256,512]{2,1,0:T(8,128)(2,1)}, u32[]{:S(2)}, u32[]{:S(2)}) %collective-permute-start.6) | collective-permute-done | bytes 262176 | tf_op jit(solution)/shard_map/ppermute | solution.py:289
  129.8 2.1 %add_convert_fusion = bf16[4,256,512]{2,1,0:T(8,128)(2,1)S(1)} fusion(bf16[4,256,512]{2,1,0:T(8,128)(2,1)} %collective-permute-done.5, bf16[8,256,512]{2,1,0:T(8,128)(2,1)} %copy-done.5, bf16[1,256,512]{2,1,0:T(8,128)(2,1)} %collective-permute-done.7, bf16[1,256,512]{2,1,0:T(8,128)(2,1)} %collective-permute-done.6, bf16[4]{0:T(256)(128)(2,1)S(1)} %pad.3.clone), kind=kLoop, calls=%fused_computation.1 | loop fusion | flops 4194304 | bytes 3670024 | tf_op jit(solution)/shard_map/convert_element_type | solution.py:199
  132.0 6.7 %near_terms.5 = bf16[4,256,512]{2,1,0:T(8,128)(2,1)S(1)} custom-call(s32[160]{0:T(256)S(1)} %select_reduce_fusion.place_ref, s32[4]{0:T(128)S(1)} %pad_add_fusion.2.target_ref, bf16[160,256,256]{2,1,0:T(8,128)(2,1)} %bitcast.26, bf16[512,512]{1,0:T(8,128)(2,1)} %collective-permute-done.1.rest_0_, bf16[512,512]{1,0:T(8,128)(2,1)} %collective-permute-done.rest_1_, ...), custom_call_target="tpu_custom_call" | custom-call | flops 2684354560 | bytes 7864320 | tf_op jit(solution)/shard_map/near_terms/pallas_call | solution.py:164
  138.7 0.9 collective-permute-start.8
  139.7 0.1 fusion
  139.7 1.0 collective-permute-start.9
  140.8 1.7 %collective-permute-start.10 = (bf16[2,256,512]{2,1,0:T(8,128)(2,1)S(1)}, bf16[2,256,512]{2,1,0:T(8,128)(2,1)S(1)}, u32[]{:S(2)}, u32[]{:S(2)}) collective-permute-start(bf16[2,256,512]{2,1,0:T(8,128)(2,1)S(1)} %get-tuple-element.14), channel_id=1, source_target_pairs={{0,6},{1,7},{2,0},{3,1},{4,2},{5,3},{6,4},{7,5},{8,14},{9,15},{10,... | collective-permute-start | bytes 1572872 | tf_op jit(solution)/shard_map/ppermute | solution.py:289
  142.5 12.1 %collective-permute-done.9 = bf16[2,256,512]{2,1,0:T(8,128)(2,1)S(1)} collective-permute-done((bf16[2,256,512]{2,1,0:T(8,128)(2,1)S(1)}, bf16[2,256,512]{2,1,0:T(8,128)(2,1)S(1)}, u32[]{:S(2)}, u32[]{:S(2)}) %collective-permute-start.9) | collective-permute-done | bytes 524320 | tf_op jit(solution)/shard_map/ppermute | solution.py:289
  154.5 1.1 add_convert_fusion.1
  (34 shorter events, 0.1 us)
Async XLA Ops:
  6.5 2.8 %copy-start = (bf16[512,512]{1,0:T(8,128)(2,1)S(1)}, bf16[512,512]{1,0:T(8,128)(2,1)}, u32[]{:S(2)}) copy-start(bf16[512,512]{1,0:T(8,128)(2,1)} %param.12) | copy-start | bytes 1572868
  6.5 78.9 %all-gather.2.cloned.1.call-start = ((), (), s32[]{:S(2)}) async-start(), calls=%async_computation.1 | async-start | bytes 1114112 | tf_op jit(solution)/shard_map/all_gather | solution.py:264
  11.3 25.4 %copy-start.11 = (bf16[2,32,256]{2,1,0:T(8,128)(2,1)S(1)}, bf16[2,32,256]{2,1,0:T(8,128)(2,1)}, u32[]{:S(2)}) copy-start(bf16[2,32,256]{2,1,0:T(8,128)(2,1)} %param.23) | copy-start | bytes 98308
  11.8 28.8 %copy-start.14 = (s32[1,64]{1,0:T(1,128)S(1)}, s32[1,64]{1,0:T(1,128)}, u32[]{:S(2)}) copy-start(s32[1,64]{1,0:T(1,128)} %param.18) | copy-start | bytes 772
  11.8 29.0 %copy-start.9 = (bf16[1,64,32,32]{1,3,2,0:T(8,128)(2,1)S(1)}, bf16[1,64,32,32]{1,3,2,0:T(8,128)(2,1)}, u32[]{:S(2)}) copy-start(bf16[1,64,32,32]{1,3,2,0:T(8,128)(2,1)} %param.21) | copy-start | bytes 393220
  36.6 5.0 %copy-start.10 = (bf16[16,32,256]{2,1,0:T(8,128)(2,1)S(1)}, bf16[16,32,256]{2,1,0:T(8,128)(2,1)}, u32[]{:S(2)}) copy-start(bf16[16,32,256]{2,1,0:T(8,128)(2,1)} %param.22) | copy-start | bytes 786436
  37.7 4.7 %copy-start.1 = (bf16[512,512]{1,0:T(8,128)(2,1)}, bf16[512,512]{1,0:T(8,128)(2,1)S(1)}, u32[]{:S(2)}) copy-start(bf16[512,512]{1,0:T(8,128)(2,1)S(1)} %reshape.64.rest_2_) | copy-start | bytes 1572868
  37.7 12.9 %collective-permute-start.2 = (bf16[512,512]{1,0:T(8,128)(2,1)S(1)}, bf16[512,512]{1,0:T(8,128)(2,1)}, u32[]{:S(2)}, u32[]{:S(2)}) collective-permute-start(bf16[512,512]{1,0:T(8,128)(2,1)S(1)} %reshape.64.rest_2_), channel_id=1, source_target_pairs={{0,120},{8,0},{16,8},{24,16},{32,24},{40,32},{48,40},{56,48},{64,5... | collective-permute-start | bytes 1572872 | tf_op jit(solution)/shard_map/ppermute | solution.py:262
  38.8 16.4 %collective-permute-start = (bf16[512,512]{1,0:T(8,128)(2,1)S(1)}, bf16[512,512]{1,0:T(8,128)(2,1)}, u32[]{:S(2)}, u32[]{:S(2)}) collective-permute-start(bf16[512,512]{1,0:T(8,128)(2,1)S(1)} %reshape.64.rest_2_), channel_id=1, source_target_pairs={{0,8},{8,16},{16,24},{24,32},{32,40},{40,48},{48,56},{56,64},{64,7... | collective-permute-start | bytes 1572872 | tf_op jit(solution)/shard_map/ppermute | solution.py:262
  40.8 14.5 %copy-start.12 = (s32[1,160]{1,0:T(1,128)S(1)}, s32[1,160]{1,0:T(1,128)}, u32[]{:S(2)}) copy-start(s32[1,160]{1,0:T(1,128)} %param.15) | copy-start | bytes 1924
  40.8 14.5 %copy-start.13 = (s32[1,160]{1,0:T(1,128)S(1)}, s32[1,160]{1,0:T(1,128)}, u32[]{:S(2)}) copy-start(s32[1,160]{1,0:T(1,128)} %param.14) | copy-start | bytes 1924
  40.8 44.6 %copy-start.8 = (s32[1,64]{1,0:T(1,128)S(1)}, s32[1,64]{1,0:T(1,128)}, u32[]{:S(2)}) copy-start(s32[1,64]{1,0:T(1,128)} %param.19) | copy-start | bytes 772
  50.6 38.5 %collective-permute-start.3 = (bf16[512,512]{1,0:T(8,128)(2,1)}, bf16[512,512]{1,0:T(8,128)(2,1)}, u32[]{:S(2)}, u32[]{:S(2)}) collective-permute-start(bf16[512,512]{1,0:T(8,128)(2,1)} %collective-permute-done.2.rest_3_), channel_id=1, source_target_pairs={{0,120},{8,0},{16,8},{24,16},{32,24},{40,32},{48,40},{56,48},{64,5... | collective-permute-start | bytes 1572872 | tf_op jit(solution)/shard_map/ppermute | solution.py:262
  55.2 33.9 %collective-permute-start.1 = (bf16[512,512]{1,0:T(8,128)(2,1)}, bf16[512,512]{1,0:T(8,128)(2,1)}, u32[]{:S(2)}, u32[]{:S(2)}) collective-permute-start(bf16[512,512]{1,0:T(8,128)(2,1)} %collective-permute-done.rest_1_), channel_id=1, source_target_pairs={{0,8},{8,16},{16,24},{24,32},{32,40},{40,48},{48,56},{56,64},{64,7... | collective-permute-start | bytes 1572872 | tf_op jit(solution)/shard_map/ppermute | solution.py:262
  85.4 3.7 %copy-start.2 = (bf16[512,512]{1,0:T(8,128)(2,1)S(1)}, bf16[512,512]{1,0:T(8,128)(2,1)}, u32[]{:S(2)}) copy-start(bf16[512,512]{1,0:T(8,128)(2,1)} %copy-done.1) | copy-start | bytes 1572868
  85.4 1.3 copy-start.7
  95.8 1.0 copy-start.6
  97.6 4.1 %collective-permute-start.4 = (bf16[2,256,512]{2,1,0:T(8,128)(2,1)}, bf16[2,256,512]{2,1,0:T(8,128)(2,1)}, u32[]{:S(2)}, u32[]{:S(2)}) collective-permute-start(bf16[2,256,512]{2,1,0:T(8,128)(2,1)} %slice.43), channel_id=1, source_target_pairs={{0,1},{1,0},{2,3},{3,2},{4,5},{5,4},{6,7},{7,6},{8,9},{9,8},{10,11... | collective-permute-start | bytes 1572872 | tf_op jit(solution)/shard_map/ppermute | solution.py:286
  103.1 1.0 copy-start.3
  116.9 1.3 copy-start.5
  119.2 10.6 %collective-permute-start.5 = (bf16[4,256,512]{2,1,0:T(8,128)(2,1)}, bf16[4,256,512]{2,1,0:T(8,128)(2,1)}, u32[]{:S(2)}, u32[]{:S(2)}) collective-permute-start(bf16[4,256,512]{2,1,0:T(8,128)(2,1)} %slice.45), channel_id=1, source_target_pairs={{0,1},{1,0},{2,3},{3,2},{4,5},{5,4},{6,7},{7,6},{8,9},{9,8},{10,11... | collective-permute-start | bytes 3145736 | tf_op jit(solution)/shard_map/ppermute | solution.py:286
  120.4 9.4 %collective-permute-start.6 = (bf16[1,256,512]{2,1,0:T(8,128)(2,1)}, bf16[1,256,512]{2,1,0:T(8,128)(2,1)}, u32[]{:S(2)}, u32[]{:S(2)}) collective-permute-start(bf16[1,256,512]{2,1,0:T(8,128)(2,1)} %get-tuple-element.15), channel_id=1, source_target_pairs={{0,2},{1,3},{2,4},{3,5},{4,6},{5,7},{6,0},{7,1},{8,10},{9,11},{10,... | collective-permute-start | bytes 786440 | tf_op jit(solution)/shard_map/ppermute | solution.py:289
  121.4 8.4 %collective-permute-start.7 = (bf16[1,256,512]{2,1,0:T(8,128)(2,1)S(1)}, bf16[1,256,512]{2,1,0:T(8,128)(2,1)}, u32[]{:S(2)}, u32[]{:S(2)}) collective-permute-start(bf16[1,256,512]{2,1,0:T(8,128)(2,1)S(1)} %get-tuple-element.16), channel_id=1, source_target_pairs={{0,6},{1,7},{2,0},{3,1},{4,2},{5,3},{6,4},{7,5},{8,14},{9,15},{10,... | collective-permute-start | bytes 786440 | tf_op jit(solution)/shard_map/ppermute | solution.py:289
  123.1 8.9 %copy-start.4 = (bf16[512,512]{1,0:T(8,128)(2,1)S(1)}, bf16[512,512]{1,0:T(8,128)(2,1)}, u32[]{:S(2)}) copy-start(bf16[512,512]{1,0:T(8,128)(2,1)} %copy-done.1) | copy-start | bytes 1572868
  138.7 3.8 %collective-permute-start.8 = (bf16[2,256,512]{2,1,0:T(8,128)(2,1)S(1)}, bf16[2,256,512]{2,1,0:T(8,128)(2,1)S(1)}, u32[]{:S(2)}, u32[]{:S(2)}) collective-permute-start(bf16[2,256,512]{2,1,0:T(8,128)(2,1)S(1)} %slice.47), channel_id=1, source_target_pairs={{0,1},{1,0},{2,3},{3,2},{4,5},{5,4},{6,7},{7,6},{8,9},{9,8},{10,11... | collective-permute-start | bytes 1572872 | tf_op jit(solution)/shard_map/ppermute | solution.py:286
  139.7 14.8 %collective-permute-start.9 = (bf16[2,256,512]{2,1,0:T(8,128)(2,1)S(1)}, bf16[2,256,512]{2,1,0:T(8,128)(2,1)S(1)}, u32[]{:S(2)}, u32[]{:S(2)}) collective-permute-start(bf16[2,256,512]{2,1,0:T(8,128)(2,1)S(1)} %get-tuple-element.13), channel_id=1, source_target_pairs={{0,2},{1,3},{2,4},{3,5},{4,6},{5,7},{6,0},{7,1},{8,10},{9,11},{10,... | collective-permute-start | bytes 1572872 | tf_op jit(solution)/shard_map/ppermute | solution.py:289
  140.8 13.8 %collective-permute-start.10 = (bf16[2,256,512]{2,1,0:T(8,128)(2,1)S(1)}, bf16[2,256,512]{2,1,0:T(8,128)(2,1)S(1)}, u32[]{:S(2)}, u32[]{:S(2)}) collective-permute-start(bf16[2,256,512]{2,1,0:T(8,128)(2,1)S(1)} %get-tuple-element.14), channel_id=1, source_target_pairs={{0,6},{1,7},{2,0},{3,1},{4,2},{5,3},{6,4},{7,5},{8,14},{9,15},{10,... | collective-permute-start | bytes 1572872 | tf_op jit(solution)/shard_map/ppermute | solution.py:289
Sparse Core Ops, SparseCore 0:
  37.7 47.6 all-gather.1

commit v2 on v0

v2 whole, which is shorter than its diff:
```python
import jax
import jax.numpy as jnp
from jax import lax
from jax.experimental import pallas as pl
from jax.experimental.pallas import tpu as pltpu
from jax.sharding import PartitionSpec as P

reach = 2
across = 4


def in_hbm(*values):
    return [pltpu.with_memory_space_constraint(value, pltpu.HBM) for value in values]


def far_kernel(cols_ref, *rest):
    parts = rest[:-9]
    coupling_ref, rows_ref, out_ref, moments, gathered, spread, part_sem, result, out_sem = rest[-9:]
    slots = cols_ref.shape[0]
    rank = coupling_ref.shape[0]
    targets = out_ref.shape[0] // rank
    sizes = [part.shape[0] for part in parts]

    def part_copy(index):
        here = pl.ds(sum(sizes[:index]), sizes[index])
        return pltpu.make_async_copy(parts[index], moments.at[here, :], part_sem.at[index])

    for index in range(len(parts)):
        part_copy(index).start()
    couplings = coupling_ref[...]
    rows = rows_ref[...]
    for target in range(targets):
        spread[target * rank : (target + 1) * rank, :] = jnp.where(
            rows == target, couplings, jnp.zeros_like(couplings)
        )
    for index in range(len(parts)):
        part_copy(index).wait()

    def pick(slot, carry):
        source = pl.multiple_of(cols_ref[slot] * rank, rank)
        place = pl.multiple_of(slot * rank, rank)
        gathered[pl.ds(place, rank), :] = moments[pl.ds(source, rank), :]
        return carry

    lax.fori_loop(0, slots, pick, 0, unroll=4)
    incoming = jnp.dot(spread[...], gathered[...], preferred_element_type=jnp.float32)
    result[...] = incoming.astype(jnp.bfloat16)
    copy = pltpu.make_async_copy(result, out_ref, out_sem)
    copy.start()
    copy.wait()


def far_incoming(far_cols, moment_parts, coupling_rows, slot_rows, targets):
    rank, width = coupling_rows.shape
    depth = sum(part.shape[0] for part in moment_parts)
    excitations = moment_parts[0].shape[1]
    shape = (targets * rank, excitations)
    anywhere = pl.BlockSpec(memory_space=pltpu.HBM)
    return pl.pallas_call(
        far_kernel,
        grid_spec=pltpu.PrefetchScalarGridSpec(
            num_scalar_prefetch=1,
            grid=(1,),
            in_specs=[anywhere] * len(moment_parts)
            + [
                pl.BlockSpec(coupling_rows.shape, lambda i, *_: (0, 0)),
                pl.BlockSpec(slot_rows.shape, lambda i, *_: (0, 0)),
            ],
            out_specs=anywhere,
            scratch_shapes=[
                pltpu.VMEM((depth, excitations), jnp.bfloat16),
                pltpu.VMEM((width, excitations), jnp.bfloat16),
                pltpu.VMEM((targets * rank, width), jnp.bfloat16),
                pltpu.SemaphoreType.DMA((len(moment_parts),)),
                pltpu.VMEM(shape, jnp.bfloat16),
                pltpu.SemaphoreType.DMA,
            ],
        ),
        out_shape=pltpu.HBM(shape, jnp.bfloat16),
        compiler_params=pltpu.CompilerParams(vmem_limit_bytes=12 * 2**20),
        cost_estimate=pl.CostEstimate(
            flops=2 * targets * rank * width * excitations,
            bytes_accessed=8 * 2**20,
            transcendentals=0,
        ),
        name="far_incoming",
    )(far_cols, *moment_parts, coupling_rows, slot_rows)


def near_terms(place, targets, blocks, parts, columns, splits, window, partial=None):
    count = targets.shape[0]
    size = blocks.shape[1]
    part_rows, excitations = parts[0].shape
    per_target = len(columns)
    depth = per_target * size
    ahead = min(4, count)
    finishing = partial is not None
    starts = [sum(splits[:index]) for index in range(len(splits))]

    def kernel(place_ref, target_ref, blocks_ref, *rest):
        rest = list(rest)
        part_refs = [rest.pop(0) for _ in parts]
        if finishing:
            partial_ref = rest.pop(0)
        out_refs = [rest.pop(0) for _ in splits]
        held, sources, result, held_sem, source_sem, result_sem = [rest.pop(0) for _ in range(6)]
        if finishing:
            running, running_sem = rest

        def source_copy(index):
            return pltpu.make_async_copy(
                part_refs[index],
                sources.at[pl.ds(index * part_rows, part_rows), :],
                source_sem.at[index],
            )

        def running_copy(step):
            return pltpu.make_async_copy(
                partial_ref.at[target_ref[step]], running.at[step], running_sem.at[step]
            )

        def begin(step):
            first = target_ref[step] * window
            for index, column in enumerate(columns):
                slot = jnp.maximum(place_ref[first + column], 0)
                pltpu.make_async_copy(
                    blocks_ref.at[slot], held.at[step * per_target + index], held_sem.at[step]
                ).start()
            if finishing:
                running_copy(step).start()

        def work(step):
            first = target_ref[step] * window
            pltpu.make_async_copy(
                blocks_ref.at[pl.ds(0, per_target)],
                held.at[pl.ds(step * per_target, per_target)],
                held_sem.at[step],
            ).wait()
            if finishing:
                running_copy(step).wait()
            total = None
            for index, column in enumerate(columns):
                here = jnp.where(
                    place_ref[first + column] >= 0, step * per_target + index, count * per_target
                )
                product = jnp.dot(
                    held[here],
                    sources[index * size : (index + 1) * size, :],
                    preferred_element_type=jnp.float32,
                )
                total = product if total is None else total + product
            if finishing:
                total = total + running[step].astype(jnp.float32)
            result[step] = total.astype(result.dtype)

        begin(0)
        for index in range(len(parts)):
            source_copy(index).start()
        for step in range(1, ahead):
            begin(step)
        held[count * per_target] = jnp.zeros((size, size), held.dtype)
        for index in range(len(parts)):
            source_copy(index).wait()

        def result_copy(index, step):
            return pltpu.make_async_copy(
                result.at[step], out_refs[index].at[step - starts[index]], result_sem.at[step]
            )

        for index in range(len(splits)):
            first, last = starts[index], starts[index] + splits[index]

            def both(step, carry):
                begin(step + ahead)
                return only(step, carry)

            def only(step, carry):
                work(step)
                result_copy(index, step).start()
                return carry

            middle = min(max(first, count - ahead), last)
            lax.fori_loop(first, middle, both, 0)
            lax.fori_loop(middle, last, only, 0)
        for index in range(len(splits)):

            def end(step, carry):
                result_copy(index, step).wait()
                return carry

            lax.fori_loop(starts[index], starts[index] + splits[index], end, 0)

    anywhere = pl.BlockSpec(memory_space=pltpu.HBM)
    extras = (partial,) if finishing else ()
    scratch = [
        pltpu.VMEM((count * per_target + 1, size, size), jnp.bfloat16),
        pltpu.VMEM((depth, excitations), jnp.bfloat16),
        pltpu.VMEM((count, size, excitations), jnp.bfloat16),
        pltpu.SemaphoreType.DMA((count,)),
        pltpu.SemaphoreType.DMA((len(parts),)),
        pltpu.SemaphoreType.DMA((count,)),
    ]
    if finishing:
        scratch += [
            pltpu.VMEM((count, size, excitations), jnp.bfloat16),
            pltpu.SemaphoreType.DMA((count,)),
        ]
    return pl.pallas_call(
        kernel,
        grid_spec=pltpu.PrefetchScalarGridSpec(
            num_scalar_prefetch=2,
            grid=(1,),
            in_specs=[anywhere] * (1 + len(parts) + len(extras)),
            out_specs=[anywhere] * len(splits),
            scratch_shapes=scratch,
        ),
        out_shape=[
            pltpu.HBM((split, size, excitations), jnp.bfloat16) for split in splits
        ],
        compiler_params=pltpu.CompilerParams(
            vmem_limit_bytes=2 * size * (count * per_target * size + (depth + 2 * count * size) * 2)
            + 4 * 2**20
        ),
        cost_estimate=pl.CostEstimate(
            flops=2 * count * size * depth * excitations,
            bytes_accessed=2 * (count * size * depth + depth * excitations),
            transcendentals=0,
        ),
        name="near_rest" if finishing else "near_first",
    )(place, targets, *in_hbm(blocks), *parts, *in_hbm(*extras))


def finish_kernel(*rest):
    kept_ref, got_ref, below_late, above_late, below_early, above_early, *far_refs = rest[:-2]
    basis_ref, out_ref = rest[-2:]
    owned = out_ref.shape[0]
    rank = far_refs[0].shape[0] // owned
    sides = [[below_late, above_early], [below_early, above_late]]
    for cluster in range(owned):
        rows = slice(cluster * rank, (cluster + 1) * rank)
        incoming = far_refs[0][rows, :].astype(jnp.float32)
        for far_ref in far_refs[1:]:
            incoming = incoming + far_ref[rows, :].astype(jnp.float32)
        high = incoming.astype(jnp.bfloat16)
        left = incoming - high.astype(jnp.float32)
        middle = left.astype(jnp.bfloat16)
        low = (left - middle.astype(jnp.float32)).astype(jnp.bfloat16)
        total = jnp.dot(
            basis_ref[cluster],
            jnp.concatenate([high, middle, low]),
            preferred_element_type=jnp.float32,
        )
        for part in (kept_ref[cluster], got_ref[cluster], sides[cluster][0][0], sides[cluster][1][0]):
            total = total + part.astype(jnp.float32)
        out_ref[cluster] = total.astype(out_ref.dtype)


def finish(kept, got, late, early, far_parts, basis):
    operands = [kept, got, *late, *early, *far_parts, basis]
    whole = pl.BlockSpec(memory_space=pltpu.VMEM)
    return pl.pallas_call(
        finish_kernel,
        in_specs=[whole] * len(operands),
        out_specs=whole,
        out_shape=jax.ShapeDtypeStruct(kept.shape, jnp.bfloat16),
        compiler_params=pltpu.CompilerParams(vmem_limit_bytes=16 * 2**20),
        cost_estimate=pl.CostEstimate(
            flops=2 * kept.size * basis.shape[2],
            bytes_accessed=2 * 5 * kept.size,
            transcendentals=0,
        ),
        name="finish",
    )(*operands)


def add(*terms):
    total = terms[0].astype(jnp.float32)
    for term in terms[1:]:
        total = total + term.astype(jnp.float32)
    return total.astype(jnp.bfloat16)


def shards(
    charges,
    send_order,
    near_rows,
    near_cols,
    near_count,
    near_blocks,
    far_rows,
    far_cols,
    far_count,
    couplings,
    row_basis,
    col_basis,
):
    row_count = lax.axis_size("row")
    col_count = lax.axis_size("col")
    device_count = row_count * col_count
    panels, excitations = charges.shape
    segment = panels // device_count
    owned, rank, leaf = col_basis.shape
    targets = row_basis.shape[0]
    window = (2 * reach + 1) * owned
    row = lax.axis_index("row")
    col = lax.axis_index("col")

    outgoing = charges.at[send_order[0]].get(mode="promise_in_bounds")
    incoming = lax.all_to_all(
        outgoing.reshape(device_count, segment, excitations),
        ("row", "col"),
        split_axis=0,
        concat_axis=0,
        tiled=True,
    )
    slab = incoming.reshape(panels, excitations)
    (
        slab,
        near_rows,
        near_cols,
        near_count,
        far_rows,
        far_cols,
        far_count,
        couplings,
        row_basis,
    ) = lax.optimization_barrier(
        (
            slab,
            near_rows,
            near_cols,
            near_count,
            far_rows,
            far_cols,
            far_count,
            couplings,
            row_basis,
        )
    )
    def row_shift(value, step):
        return lax.ppermute(value, "row", [(i, (i + step) % row_count) for i in range(row_count)])

    def line_shift(value, step):
        return lax.ppermute(
            value,
            "row",
            [(i, i // across * across + (i + step) % across) for i in range(row_count)],
        )

    def other_core(value):
        return lax.ppermute(value, "col", [(i, i ^ 1) for i in range(col_count)])

    def chip_shift(value, step):
        return lax.ppermute(
            value, "col", [(i, (i + 2 * step) % col_count) for i in range(col_count)]
        )

    below = row_shift(slab, 1)
    above = row_shift(slab, -1)
    slots = jnp.arange(near_rows.shape[1], dtype=jnp.int32)
    pair = near_rows[0] * window + near_cols[0] - (row - reach) * owned
    pair = jnp.where(slots < near_count[0], pair, -1)
    wanted = jnp.arange(targets * window, dtype=jnp.int32)
    place = jnp.max(jnp.where(pair[None, :] == wanted[:, None], slots[None, :], -1), axis=1)

    far_slots = far_rows.shape[1]
    far_target = jnp.where(
        jnp.arange(far_slots, dtype=jnp.int32) < far_count[0], far_rows[0], -1
    )
    coupling_rows = couplings[0].transpose(1, 0, 2).reshape(rank, far_slots * rank)
    own_basis = lax.dynamic_slice_in_dim(row_basis, col * owned, owned, 0)
    own_basis = jnp.tile(own_basis.transpose(0, 2, 1), (1, 1, 3))
    far_row = far_cols[0] // owned
    far_line = (far_row // across - row // across) % (row_count // across)
    far_place = (far_row - row) % across
    far_source = (far_line * across + far_place) * owned + far_cols[0] % owned

    chips = col_count // 2
    chip, core = col // 2, col % 2
    each = jnp.arange(owned, dtype=jnp.int32)

    def clusters(chip_step, which):
        return (((chip + chip_step) % chips) * 2 + which) * owned + each

    def order(*chip_steps):
        return jnp.concatenate(
            [clusters(step, 1 - core) for step in chip_steps]
            + [clusters(step, core) for step in chip_steps]
        )

    far_chip = (far_target // (2 * owned) - chip) % chips
    far_core = (far_target // owned + 1 - core) % 2
    far_place = (far_core * chips + far_chip) * owned + far_target % owned
    far_place = jnp.where(far_target >= 0, far_place, -1)
    slot_rows = jnp.repeat(far_place, rank)[None, :]

    blocks = near_blocks[0]
    everyone = jnp.arange(targets, dtype=jnp.int32)
    middle = list(range(reach * owned, (reach + 1) * owned))
    inner = [column for column in range(owned, window - owned) if column not in middle]
    outer = list(range(owned)) + list(range(window - owned, window))
    (partial,) = near_terms(place, everyone, blocks, [slab], middle, [targets], window)
    slab, below, above, partial = lax.optimization_barrier((slab, below, above, partial))
    moments = (
        jnp.einsum(
            "gkb,gbr->gkr",
            col_basis,
            slab.reshape(owned, leaf, excitations),
            preferred_element_type=jnp.float32,
        )
        .astype(jnp.bfloat16)
        .reshape(owned * rank, excitations)
    )
    of_line = jnp.concatenate([moments] + [line_shift(moments, -step) for step in range(1, across)])

    below_more = row_shift(below, 1)
    above_more = row_shift(above, -1)
    (partial,) = near_terms(
        place, everyone, blocks, [below, above], inner, [targets], window, partial
    )

    def rest(*chip_steps):
        return near_terms(
            place,
            order(*chip_steps),
            blocks,
            [below_more, above_more],
            outer,
            [owned * len(chip_steps)] + [owned] * len(chip_steps),
            window,
            partial,
        )

    of_line, partial = lax.optimization_barrier((of_line, partial))
    next_line = row_shift(of_line, -across)
    last_line = row_shift(of_line, across)
    sent, kept = rest(2)
    sent, next_line, last_line = lax.optimization_barrier((sent, next_line, last_line))
    half = of_line.shape[0] // 2
    second_line = [row_shift(next_line[:half], -across), row_shift(last_line[half:], across)]
    opposite = add(kept, other_core(sent))
    opposite, place = lax.optimization_barrier((opposite, place))
    from_below = chip_shift(opposite[:1], 1)
    from_above = chip_shift(opposite[1:], -1)
    sent, kept_up, kept_down = rest(1, -1)
    sent, from_below, from_above, second_line = lax.optimization_barrier(
        (sent, from_below, from_above, second_line)
    )
    got = other_core(sent)
    kept_up, second_line = lax.optimization_barrier((kept_up, second_line))
    incoming = far_incoming(
        far_source,
        [of_line, next_line, *second_line, last_line],
        coupling_rows,
        slot_rows,
        targets,
    )
    incoming, got = lax.optimization_barrier((incoming, got))
    early = [add(kept_up[1:], got[1:2]), add(kept_down[:1], got[owned : owned + 1])]
    late = [add(kept_up[:1], got[:1], from_below), add(kept_down[1:], got[owned + 1 :], from_above)]
    early, late, place, incoming = lax.optimization_barrier((early, late, place, incoming))
    side_early = [chip_shift(early[0], 1), chip_shift(early[1], -1)]
    far_half = incoming.shape[0] // 2
    far_got = other_core(incoming[:far_half])
    sent, kept = rest(0)
    sent, far_got, side_early, late = lax.optimization_barrier((sent, far_got, side_early, late))
    side_late = [chip_shift(late[0], 1), chip_shift(late[1], -1)]
    far = add(incoming[far_half:], far_got).reshape(chips, owned * rank, excitations)
    far_parts = [far[0]] + [chip_shift(far[step], step) for step in range(1, chips)]
    got = other_core(sent)
    return finish(kept, got, side_late, side_early, far_parts, own_basis).reshape(
        panels, excitations
    )


def solution(mesh):
    placed = (
        P(("row", "col"), None),
        P(("row", "col"), None),
        P(("row", "col"), None),
        P(("row", "col"), None),
        P(("row", "col")),
        P(("row", "col"), None, None, None),
        P(("row", "col"), None),
        P(("row", "col"), None),
        P(("row", "col")),
        P(("row", "col"), None, None, None),
        P("row", None, None),
        P(("row", "col"), None, None),
    )
    return jax.shard_map(
        shards, mesh=mesh, in_specs=placed, out_specs=P(("row", "col"), None), check_vma=False
    )
```

time: 619 us -> 128 us (0.21)
  waiting for transfers between devices: 351 us -> 27 us
  other arithmetic: 102 us -> 4.06 us
  local copies, waits for them, and re-layouts: 70.1 us -> 8.23 us
  matrix products: 52.9 us -> 0.18 us
  starting transfers between devices: 0.08 us -> 47.8 us
  Pallas kernels: 0 us -> 38 us
  blocking collectives: 24.8 us -> 0 us
  between operations: 14.6 us -> 1.76 us
    reduce_scatter x1 -> x0, waiting for transfers between devices: 255 us -> none  [shards(): lax.psum_scatter((near_part + expanded).astype(jnp.bfloat16), 'col', scat...]
    all_gather x2 -> x0, waiting for transfers between devices: 95 us -> none  [the longest x1 60.1 us: shards(): lax.all_gather(own_slab, 'row', axis=0, tiled=True)]
    scatter-add x10 -> x0, other arithmetic: 92.5 us -> none  [the longest x9 83.6 us: near_step(): return running.at[slot_rows].add(product)]
    dot_general x12 -> x1, matrix products: 52.9 us -> 0.18 us  [shards(): jnp.einsum('gkb,gbr->gkr', col_basis, slab.reshape(owned, leaf, excitatio...]
    gather x12 -> x1, local copies, waits for them, and re-layouts: 52.5 us -> 1.96 us  [shards(): outgoing = charges.at[send_order[0]].get(mode='promise_in_bounds')]
    pallas_call x0 -> x7, Pallas kernels: none -> 38 us  [the longest x5 33.3 us: near_terms(): pl.pallas_call(kernel, grid_spec=pltpu.PrefetchScalarGridSpec(num_scalar_...]
    ppermute x0 -> x24, starting transfers between devices: none -> 36.3 us  [the longest x8 13.8 us: row_shift(): lax.ppermute(value, 'row', [(i, (i + step) % row_count) for i in range(ro...]
    all_to_all x1 -> x0, blocking collectives: 24.8 us -> none  [shards(): lax.all_to_all(outgoing.reshape(device_count, segment, excitations), ('ro...]
  transfers between devices with their start and end apart: 3 -> 25, of which waited for: 3 -> 9; matrix products, arithmetic and copies ran while one was open for 2% -> 3% of each run, Pallas kernels for 0% -> 29%
where the time goes in v2:
time: 128 us; the launch traced here: 127 us
  starting transfers between devices  47.8 us (37%)
  Pallas kernels  38 us (30%)
  waiting for transfers between devices  27 us (21%)
  local copies, waits for them, and re-layouts  8.23 us (6%)
  other arithmetic  4.06 us (3%)
  between operations  1.76 us (1%)
    pallas_call x5, Pallas kernels, near_terms(): pl.pallas_call(kernel, grid_spec=pltpu.PrefetchScalarGridSpec(num_scalar_...  33.3 us
    ppermute x8, starting transfers between devices, row_shift(): lax.ppermute(value, 'row', [(i, (i + step) % row_count) for i in range(ro...  13.8 us
    all_to_all x1, waiting for transfers between devices, shards(): lax.all_to_all(outgoing.reshape(device_count, segment, excitations), ('ro...  12.8 us
    ppermute x9, starting transfers between devices, chip_shift(): lax.ppermute(value, 'col', [(i, (i + 2 * step) % col_count) for i in rang...  12.4 us
    all_to_all x1, starting transfers between devices, shards(): lax.all_to_all(outgoing.reshape(device_count, segment, excitations), ('ro...  11.5 us
    ppermute x4, starting transfers between devices, other_core(): return lax.ppermute(value, 'col', [(i, i ^ 1) for i in range(col_count)])  8.22 us
    ppermute x9, waiting for transfers between devices, chip_shift(): lax.ppermute(value, 'col', [(i, (i + 2 * step) % col_count) for i in rang...  7.44 us
    ppermute x8, waiting for transfers between devices, row_shift(): lax.ppermute(value, 'row', [(i, (i + step) % row_count) for i in range(ro...  4.99 us
  transfers between devices with their start and end apart: 25, of which 9 were waited for; matrix products, arithmetic and copies ran while one was open for 3% of the time, Pallas kernels for 29%

profile of v2, /device:TPU:1, one launch (start us, length us, event | category | flops | bytes accessed | tf_op | source)
XLA Modules:
  0.0 127.1 jit_solution(1586207308093624882)
XLA Ops:
  0.0 0.7 compare_select_fusion
  0.8 0.3 copy-done
  1.1 2.0 %gather_fusion = bf16[512,512]{1,0:T(8,128)(2,1)S(1)} fusion(bf16[512,512]{1,0:T(8,128)(2,1)S(1)} %copy-done, s32[1024]{0:T(1024)S(1)} %pad_clamp_fusion), kind=kCustom, calls=%fused_computation | custom fusion | bytes 1050624 | tf_op jit(solution)/shard_map/gather | solution.py:308
  3.0 0.9 reshape.66
  3.9 11.5 %all-to-all-start = ((bf16[128,4,512]{2,1,0:T(4,128)(2,1)}), bf16[128,4,512]{2,1,0:T(4,128)(2,1)S(1)}, u32[]{:S(2)}, u32[]{:S(2)}) async-start(bf16[128,4,512]{2,1,0:T(4,128)(2,1)} %reshape.66), calls=%async_computation | async-start | bytes 1048576 | tf_op jit(solution)/shard_map/all_to_all | solution.py:309
  16.1 12.8 %all-to-all-done = bf16[128,4,512]{2,1,0:T(4,128)(2,1)S(1)} async-done(((bf16[128,4,512]{2,1,0:T(4,128)(2,1)}), bf16[128,4,512]{2,1,0:T(4,128)(2,1)S(1)}, u32[]{:S(2)}, u32[]{:S(2)}) %all-to-all-start) | async-done | bytes 524320 | tf_op jit(solution)/shard_map/all_to_all | solution.py:309
  29.0 0.1 reshape.67.rest_0_
  29.1 0.3 collective-permute-start
  29.4 4.5 %collective-permute-start.1 = (bf16[512,512]{1,0:T(8,128)(2,1)S(1)}, bf16[512,512]{1,0:T(8,128)(2,1)S(1)}, u32[]{:S(2)}, u32[]{:S(2)}) collective-permute-start(bf16[512,512]{1,0:T(8,128)(2,1)S(1)} %reshape.67.rest_0_), channel_id=1, source_target_pairs={{0,120},{8,0},{16,8},{24,16},{32,24},{40,32},{48,40},{56,48},{64,5... | collective-permute-start | bytes 1572872 | tf_op jit(solution)/shard_map/ppermute | solution.py:341
  34.0 0.1 select_reduce_fusion.place_ref
  34.1 0.0 copy-start.5
  34.1 7.5 %near_first.1.rest_2_ = bf16[16,256,512]{2,1,0:T(8,128)(2,1)} custom-call(s32[160]{0:T(256)S(1)} %select_reduce_fusion.place_ref, s32[16]{0:T(128)S(1)} %iota.39.target_ref, bf16[160,256,256]{2,1,0:T(8,128)(2,1)} %bitcast.40, bf16[512,512]{1,0:T(8,128)(2,1)S(1)} %reshape.67.rest_0_), custom_call_target="tpu_custom_call" | custom-call | flops 2147483648 | bytes 4718592 | tf_op jit(solution)/shard_map/near_first/pallas_call | solution.py:208
  41.6 3.2 %collective-permute-done.rest_0_ = bf16[512,512]{1,0:T(8,128)(2,1)S(1)} collective-permute-done((bf16[512,512]{1,0:T(8,128)(2,1)S(1)}, bf16[512,512]{1,0:T(8,128)(2,1)S(1)}, u32[]{:S(2)}, u32[]{:S(2)}) %collective-permute-start) | collective-permute-done | bytes 524320 | tf_op jit(solution)/shard_map/ppermute | solution.py:341
  44.8 0.2 convolution_convert_fusion
  45.0 1.3 %collective-permute-start.4 = (bf16[64,512]{1,0:T(8,128)(2,1)S(1)}, bf16[64,512]{1,0:T(8,128)(2,1)S(1)}, u32[]{:S(2)}, u32[]{:S(2)}) collective-permute-start(bf16[64,512]{1,0:T(8,128)(2,1)S(1)} %bitcast.47), channel_id=1, source_target_pairs={{0,24},{8,0},{16,8},{24,16},{32,56},{40,32},{48,40},{56,48},{64,88... | collective-permute-start | bytes 196616 | tf_op jit(solution)/shard_map/ppermute | solution.py:344
  46.3 0.7 collective-permute-start.6
  47.0 2.0 %collective-permute-start.2 = (bf16[512,512]{1,0:T(8,128)(2,1)S(1)}, bf16[512,512]{1,0:T(8,128)(2,1)S(1)}, u32[]{:S(2)}, u32[]{:S(2)}) collective-permute-start(bf16[512,512]{1,0:T(8,128)(2,1)S(1)} %collective-permute-done.rest_0_), channel_id=1, source_target_pairs={{0,8},{8,16},{16,24},{24,32},{32,40},{40,48},{48,56},{56,64},{64,7... | collective-permute-start | bytes 1572872 | tf_op jit(solution)/shard_map/ppermute | solution.py:341
  48.9 3.3 %collective-permute-start.3 = (bf16[512,512]{1,0:T(8,128)(2,1)S(1)}, bf16[512,512]{1,0:T(8,128)(2,1)S(1)}, u32[]{:S(2)}, u32[]{:S(2)}) collective-permute-start(bf16[512,512]{1,0:T(8,128)(2,1)S(1)} %collective-permute-done.1.rest_1_), channel_id=1, source_target_pairs={{0,120},{8,0},{16,8},{24,16},{32,24},{40,32},{48,40},{56,48},{64,5... | collective-permute-start | bytes 1572872 | tf_op jit(solution)/shard_map/ppermute | solution.py:341
  52.3 10.3 %near_rest.4.rest_2_ = bf16[16,256,512]{2,1,0:T(8,128)(2,1)} custom-call(s32[160]{0:T(256)S(1)} %select_reduce_fusion.place_ref, s32[16]{0:T(128)S(1)} %iota.40.target_ref, bf16[160,256,256]{2,1,0:T(8,128)(2,1)} %bitcast.41, bf16[512,512]{1,0:T(8,128)(2,1)S(1)} %collective-permute-done.rest_0_, bf16[512,512]{1,0:T(8,128)(2,1)S(1)} %collective-permute-done.1.rest_1_, ...), custom_call_target="tpu_custom_call" | custom-call | flops 4294967296 | bytes 9437184 | tf_op jit(solution)/shard_map/near_rest/pallas_call | solution.py:208
  62.7 2.0 %collective-permute-start.7 = (bf16[256,512]{1,0:T(8,128)(2,1)S(1)}, bf16[256,512]{1,0:T(8,128)(2,1)S(1)}, u32[]{:S(2)}, u32[]{:S(2)}) collective-permute-start(bf16[256,512]{1,0:T(8,128)(2,1)S(1)} %pad_maximum_fusion.rest_0_), channel_id=1, source_target_pairs={{0,96},{8,104},{16,112},{24,120},{32,0},{40,8},{48,16},{56,24},{64... | collective-permute-start | bytes 786440 | tf_op jit(solution)/shard_map/ppermute | solution.py:341
  64.7 0.1 pad_add_fusion.target_ref
  64.8 0.4 collective-permute-done.2.rest_0_
  65.2 4.6 %near_rest.5 = (bf16[2,256,512]{2,1,0:T(8,128)(2,1)}, bf16[2,256,512]{2,1,0:T(8,128)(2,1)}) custom-call(s32[160]{0:T(256)S(1)} %select_reduce_fusion.place_ref, s32[4]{0:T(128)S(1)} %pad_add_fusion.target_ref, bf16[160,256,256]{2,1,0:T(8,128)(2,1)} %bitcast.42, bf16[512,512]{1,0:T(8,128)(2,1)S(1)} %collective-permute-done.2.rest_0_, ...), custom_call_target="tpu_custom_call" | custom-call | flops 1073741824 | bytes 3145728 | tf_op jit(solution)/shard_map/near_rest/pallas_call | solution.py:208
  69.8 1.3 %collective-permute-done.8.rest_4_ = bf16[256,512]{1,0:T(8,128)(2,1)S(1)} collective-permute-done((bf16[256,512]{1,0:T(8,128)(2,1)S(1)}, bf16[256,512]{1,0:T(8,128)(2,1)S(1)}, u32[]{:S(2)}, u32[]{:S(2)}) %collective-permute-start.8) | collective-permute-done | bytes 262176 | tf_op jit(solution)/shard_map/ppermute | solution.py:341
  71.1 4.6 %collective-permute-start.9 = (bf16[2,256,512]{2,1,0:T(8,128)(2,1)}, bf16[2,256,512]{2,1,0:T(8,128)(2,1)S(1)}, u32[]{:S(2)}, u32[]{:S(2)}) collective-permute-start(bf16[2,256,512]{2,1,0:T(8,128)(2,1)} %get-tuple-element.66), channel_id=1, source_target_pairs={{0,1},{1,0},{2,3},{3,2},{4,5},{5,4},{6,7},{7,6},{8,9},{9,8},{10,11... | collective-permute-start | bytes 1572872 | tf_op jit(solution)/shard_map/ppermute | solution.py:351
  75.8 1.7 %collective-permute-done.9 = bf16[2,256,512]{2,1,0:T(8,128)(2,1)S(1)} collective-permute-done((bf16[2,256,512]{2,1,0:T(8,128)(2,1)}, bf16[2,256,512]{2,1,0:T(8,128)(2,1)S(1)}, u32[]{:S(2)}, u32[]{:S(2)}) %collective-permute-start.9) | collective-permute-done | bytes 524320 | tf_op jit(solution)/shard_map/ppermute | solution.py:351
  77.5 1.2 add_convert_fusion
  78.8 0.6 collective-permute-start.10
  79.3 2.2 %collective-permute-start.11 = (bf16[1,256,512]{2,1,0:T(8,128)(2,1)S(1)}, bf16[1,256,512]{2,1,0:T(8,128)(2,1)}, u32[]{:S(2)}, u32[]{:S(2)}) collective-permute-start(bf16[1,256,512]{2,1,0:T(8,128)(2,1)S(1)} %get-tuple-element.109), channel_id=1, source_target_pairs={{0,6},{1,7},{2,0},{3,1},{4,2},{5,3},{6,4},{7,5},{8,14},{9,15},{10,... | collective-permute-start | bytes 786440 | tf_op jit(solution)/shard_map/ppermute | solution.py:354
  81.5 0.1 pad_add_fusion.1.target_ref
  81.6 0.2 collective-permute-start.12
  81.8 0.0 copy-start.8
  81.8 0.0 copy-start.9
  81.8 1.4 %collective-permute-start.13 = (bf16[128,512]{1,0:T(8,128)(2,1)S(1)}, bf16[128,512]{1,0:T(8,128)(2,1)S(1)}, u32[]{:S(2)}, u32[]{:S(2)}) collective-permute-start(bf16[128,512]{1,0:T(8,128)(2,1)S(1)} %slice.61), channel_id=1, source_target_pairs={{0,32},{8,40},{16,48},{24,56},{32,64},{40,72},{48,80},{56,88},{64,... | collective-permute-start | bytes 393224 | tf_op jit(solution)/shard_map/ppermute | solution.py:341
  83.2 6.5 %near_rest.6 = (bf16[4,256,512]{2,1,0:T(8,128)(2,1)}, bf16[2,256,512]{2,1,0:T(8,128)(2,1)}, bf16[2,256,512]{2,1,0:T(8,128)(2,1)}) custom-call(s32[160]{0:T(256)S(1)} %select_reduce_fusion.place_ref, s32[8]{0:T(128)S(1)} %pad_add_fusion.1.target_ref, bf16[160,256,256]{2,1,0:T(8,128)(2,1)} %bitcast.43, bf16[512,512]{1,0:T(8,128)(2,1)S(1)} %collective-permute-done.2.rest_0_, ...), custom_call_target="tpu_custom_call" | custom-call | flops 2147483648 | bytes 5242880 | tf_op jit(solution)/shard_map/near_rest/pallas_call | solution.py:208
  89.8 2.2 %collective-permute-start.14 = (bf16[4,256,512]{2,1,0:T(8,128)(2,1)}, bf16[4,256,512]{2,1,0:T(8,128)(2,1)}, u32[]{:S(2)}, u32[]{:S(2)}) collective-permute-start(bf16[4,256,512]{2,1,0:T(8,128)(2,1)} %get-tuple-element.82), channel_id=1, source_target_pairs={{0,1},{1,0},{2,3},{3,2},{4,5},{5,4},{6,7},{7,6},{8,9},{9,8},{10,11... | collective-permute-start | bytes 3145736 | tf_op jit(solution)/shard_map/ppermute | solution.py:351
  92.7 0.1 broadcast_in_dim.29
  92.8 0.1 broadcast_in_dim_reshape.3.rest_6_
  92.9 1.2 copy.17
  94.1 0.5 reshape.70.rest_5_
  94.7 0.0 copy-start.2
  94.7 3.5 %far_incoming.1 = bf16[512,512]{1,0:T(8,128)(2,1)} custom-call(s32[64]{0:T(128)S(1)} %fusion.1.cols_ref, bf16[256,512]{1,0:T(8,128)(2,1)S(1)} %pad_maximum_fusion.rest_0_, bf16[256,512]{1,0:T(8,128)(2,1)S(1)} %collective-permute-done.7.rest_1_, bf16[128,512]{1,0:T(8,128)(2,1)S(1)} %collective-permute-done.12.rest_2_, ...), custom_call_target="tpu_custom_call" | custom-call | flops 1073741824 | bytes 8388608 | tf_op jit(solution)/shard_map/far_incoming/pallas_call | solution.py:59
  98.2 1.6 %add_convert_fusion.2 = (bf16[1,256,512]{2,1,0:T(8,128)(2,1)S(1)}, bf16[1,256,512]{2,1,0:T(8,128)(2,1)S(1)}, bf16[1,256,512]{2,1,0:T(8,128)(2,1)S(1)}, bf16[1,256,512]{2,1,0:T(8,128)(2,1)S(1)}) fusion(bf16[1,256,512]{2,1,0:T(8,128)(2,1)} %collective-permute-done.11, bf16[4,256,512]{2,1,0:T(8,128)(2,1)} %collective-permute-done.14, ...), kind=kLoop, calls=%fused_computation.4 | loop fusion | flops 2621440 | bytes 3670016 | tf_op jit(solution)/shard_map/convert_element_type | solution.py:280
  99.8 1.0 slice.70
  100.8 0.1 collective-permute-start.15
  100.9 0.1 collective-permute-start.16
  101.0 2.7 %collective-permute-start.17 = (bf16[1,256,512]{2,1,0:T(8,128)(2,1)S(1)}, bf16[1,256,512]{2,1,0:T(8,128)(2,1)S(1)}, u32[]{:S(2)}, u32[]{:S(2)}) collective-permute-start(bf16[1,256,512]{2,1,0:T(8,128)(2,1)S(1)} %get-tuple-element.93), channel_id=1, source_target_pairs={{0,6},{1,7},{2,0},{3,1},{4,2},{5,3},{6,4},{7,5},{8,14},{9,15},{10,... | collective-permute-start | bytes 786440 | tf_op jit(solution)/shard_map/ppermute | solution.py:354
  103.7 0.1 pad_add_fusion.2.target_ref
  103.7 4.4 %near_rest.7 = (bf16[2,256,512]{2,1,0:T(8,128)(2,1)}, bf16[2,256,512]{2,1,0:T(8,128)(2,1)}) custom-call(s32[160]{0:T(256)S(1)} %select_reduce_fusion.place_ref, s32[4]{0:T(128)S(1)} %pad_add_fusion.2.target_ref, bf16[160,256,256]{2,1,0:T(8,128)(2,1)} %bitcast.44, bf16[512,512]{1,0:T(8,128)(2,1)S(1)} %collective-permute-done.2.rest_0_, ...), custom_call_target="tpu_custom_call" | custom-call | flops 1073741824 | bytes 3145728 | tf_op jit(solution)/shard_map/near_rest/pallas_call | solution.py:208
  108.1 1.5 %collective-permute-done.16.rest_4_ = bf16[1,256,512]{2,1,0:T(8,128)(2,1)S(1)} collective-permute-done((bf16[1,256,512]{2,1,0:T(8,128)(2,1)S(1)}, bf16[1,256,512]{2,1,0:T(8,128)(2,1)S(1)}, u32[]{:S(2)}, u32[]{:S(2)}) %collective-permute-start.16) | collective-permute-done | bytes 262176 | tf_op jit(solution)/shard_map/ppermute | solution.py:354
  109.6 1.3 collective-permute-start.18
  110.9 0.1 add_convert_fusion.1
  111.0 0.1 collective-permute-start.19
  111.1 2.7 %collective-permute-start.20 = (bf16[1,256,512]{2,1,0:T(8,128)(2,1)S(1)}, bf16[1,256,512]{2,1,0:T(8,128)(2,1)S(1)}, u32[]{:S(2)}, u32[]{:S(2)}) collective-permute-start(bf16[1,256,512]{2,1,0:T(8,128)(2,1)S(1)} %get-tuple-element.98), channel_id=1, source_target_pairs={{0,6},{1,7},{2,0},{3,1},{4,2},{5,3},{6,4},{7,5},{8,14},{9,15},{10,... | collective-permute-start | bytes 786440 | tf_op jit(solution)/shard_map/ppermute | solution.py:354
  113.8 0.1 collective-permute-start.21
  113.9 2.5 %collective-permute-start.22 = (bf16[64,512]{1,0:T(8,128)(2,1)S(1)}, bf16[64,512]{1,0:T(8,128)(2,1)S(1)}, u32[]{:S(2)}, u32[]{:S(2)}) collective-permute-start(bf16[64,512]{1,0:T(8,128)(2,1)S(1)} %get-tuple-element.112), channel_id=1, source_target_pairs={{0,4},{1,5},{2,6},{3,7},{4,0},{5,1},{6,2},{7,3},{8,12},{9,13},{10,... | collective-permute-start | bytes 196616 | tf_op jit(solution)/shard_map/ppermute | solution.py:354
  116.5 5.1 %collective-permute-done.21.rest_7_ = bf16[64,512]{1,0:T(8,128)(2,1)S(1)} collective-permute-done((bf16[64,512]{1,0:T(8,128)(2,1)S(1)}, bf16[64,512]{1,0:T(8,128)(2,1)S(1)}, u32[]{:S(2)}, u32[]{:S(2)}) %collective-permute-start.21) | collective-permute-done | bytes 65568 | tf_op jit(solution)/shard_map/ppermute | solution.py:354
  121.6 1.5 %collective-permute-start.23 = (bf16[64,512]{1,0:T(8,128)(2,1)S(1)}, bf16[64,512]{1,0:T(8,128)(2,1)S(1)}, u32[]{:S(2)}, u32[]{:S(2)}) collective-permute-start(bf16[64,512]{1,0:T(8,128)(2,1)S(1)} %get-tuple-element.111), channel_id=1, source_target_pairs={{0,6},{1,7},{2,0},{3,1},{4,2},{5,3},{6,4},{7,5},{8,14},{9,15},{10,... | collective-permute-start | bytes 196616 | tf_op jit(solution)/shard_map/ppermute | solution.py:354
  123.1 0.8 dynamic-slice_bitcast_fusion
  123.8 0.1 copy.18.rest_10_
  124.0 0.2 collective-permute-done.22.rest_8_
  124.2 0.5 collective-permute-done.23.rest_9_
  124.8 1.0 copy-done.1
  125.8 1.3 finish.1
  (48 shorter events, 0.3 us)
Async XLA Ops:
  0.0 1.1 copy-start
  0.0 33.9 %copy-start.7 = (s32[1,160]{1,0:T(1,128)S(1)}, s32[1,160]{1,0:T(1,128)}, u32[]{:S(2)}) copy-start(s32[1,160]{1,0:T(1,128)} %param.14) | copy-start | bytes 1924
  0.0 33.9 %copy-start.6 = (s32[1,160]{1,0:T(1,128)S(1)}, s32[1,160]{1,0:T(1,128)}, u32[]{:S(2)}) copy-start(s32[1,160]{1,0:T(1,128)} %param.15) | copy-start | bytes 1924
  3.9 25.0 %all-to-all-start = ((bf16[128,4,512]{2,1,0:T(4,128)(2,1)}), bf16[128,4,512]{2,1,0:T(4,128)(2,1)S(1)}, u32[]{:S(2)}, u32[]{:S(2)}) async-start(bf16[128,4,512]{2,1,0:T(4,128)(2,1)} %reshape.66), calls=%async_computation | async-start | bytes 1048576 | tf_op jit(solution)/shard_map/all_to_all | solution.py:309
  29.1 15.7 %collective-permute-start = (bf16[512,512]{1,0:T(8,128)(2,1)S(1)}, bf16[512,512]{1,0:T(8,128)(2,1)S(1)}, u32[]{:S(2)}, u32[]{:S(2)}) collective-permute-start(bf16[512,512]{1,0:T(8,128)(2,1)S(1)} %reshape.67.rest_0_), channel_id=1, source_target_pairs={{0,8},{8,16},{16,24},{24,32},{32,40},{40,48},{48,56},{56,64},{64,7... | collective-permute-start | bytes 1572872 | tf_op jit(solution)/shard_map/ppermute | solution.py:341
  29.4 15.4 %collective-permute-start.1 = (bf16[512,512]{1,0:T(8,128)(2,1)S(1)}, bf16[512,512]{1,0:T(8,128)(2,1)S(1)}, u32[]{:S(2)}, u32[]{:S(2)}) collective-permute-start(bf16[512,512]{1,0:T(8,128)(2,1)S(1)} %reshape.67.rest_0_), channel_id=1, source_target_pairs={{0,120},{8,0},{16,8},{24,16},{32,24},{40,32},{48,40},{56,48},{64,5... | collective-permute-start | bytes 1572872 | tf_op jit(solution)/shard_map/ppermute | solution.py:341
  34.1 10.7 %copy-start.5 = (bf16[2,32,256]{2,1,0:T(8,128)(2,1)S(1)}, bf16[2,32,256]{2,1,0:T(8,128)(2,1)}, u32[]{:S(2)}) copy-start(bf16[2,32,256]{2,1,0:T(8,128)(2,1)} %param.23) | copy-start | bytes 98308
  45.0 17.6 %collective-permute-start.4 = (bf16[64,512]{1,0:T(8,128)(2,1)S(1)}, bf16[64,512]{1,0:T(8,128)(2,1)S(1)}, u32[]{:S(2)}, u32[]{:S(2)}) collective-permute-start(bf16[64,512]{1,0:T(8,128)(2,1)S(1)} %bitcast.47), channel_id=1, source_target_pairs={{0,24},{8,0},{16,8},{24,16},{32,56},{40,32},{48,40},{56,48},{64,88... | collective-permute-start | bytes 196616 | tf_op jit(solution)/shard_map/ppermute | solution.py:344
  46.3 16.3 %collective-permute-start.5 = (bf16[64,512]{1,0:T(8,128)(2,1)S(1)}, bf16[64,512]{1,0:T(8,128)(2,1)S(1)}, u32[]{:S(2)}, u32[]{:S(2)}) collective-permute-start(bf16[64,512]{1,0:T(8,128)(2,1)S(1)} %bitcast.48), channel_id=1, source_target_pairs={{0,16},{8,24},{16,0},{24,8},{32,48},{40,56},{48,32},{56,40},{64,80... | collective-permute-start | bytes 196616 | tf_op jit(solution)/shard_map/ppermute | solution.py:344
  46.3 16.3 %collective-permute-start.6 = (bf16[64,512]{1,0:T(8,128)(2,1)S(1)}, bf16[64,512]{1,0:T(8,128)(2,1)S(1)}, u32[]{:S(2)}, u32[]{:S(2)}) collective-permute-start(bf16[64,512]{1,0:T(8,128)(2,1)S(1)} %bitcast.49), channel_id=1, source_target_pairs={{0,8},{8,16},{16,24},{24,0},{32,40},{40,48},{48,56},{56,32},{64,72... | collective-permute-start | bytes 196616 | tf_op jit(solution)/shard_map/ppermute | solution.py:344
  47.0 18.2 %collective-permute-start.2 = (bf16[512,512]{1,0:T(8,128)(2,1)S(1)}, bf16[512,512]{1,0:T(8,128)(2,1)S(1)}, u32[]{:S(2)}, u32[]{:S(2)}) collective-permute-start(bf16[512,512]{1,0:T(8,128)(2,1)S(1)} %collective-permute-done.rest_0_), channel_id=1, source_target_pairs={{0,8},{8,16},{16,24},{24,32},{32,40},{40,48},{48,56},{56,64},{64,7... | collective-permute-start | bytes 1572872 | tf_op jit(solution)/shard_map/ppermute | solution.py:341
  48.9 16.2 %collective-permute-start.3 = (bf16[512,512]{1,0:T(8,128)(2,1)S(1)}, bf16[512,512]{1,0:T(8,128)(2,1)S(1)}, u32[]{:S(2)}, u32[]{:S(2)}) collective-permute-start(bf16[512,512]{1,0:T(8,128)(2,1)S(1)} %collective-permute-done.1.rest_1_), channel_id=1, source_target_pairs={{0,120},{8,0},{16,8},{24,16},{32,24},{40,32},{48,40},{56,48},{64,5... | collective-permute-start | bytes 1572872 | tf_op jit(solution)/shard_map/ppermute | solution.py:341
  62.7 7.1 %collective-permute-start.7 = (bf16[256,512]{1,0:T(8,128)(2,1)S(1)}, bf16[256,512]{1,0:T(8,128)(2,1)S(1)}, u32[]{:S(2)}, u32[]{:S(2)}) collective-permute-start(bf16[256,512]{1,0:T(8,128)(2,1)S(1)} %pad_maximum_fusion.rest_0_), channel_id=1, source_target_pairs={{0,96},{8,104},{16,112},{24,120},{32,0},{40,8},{48,16},{56,24},{64... | collective-permute-start | bytes 786440 | tf_op jit(solution)/shard_map/ppermute | solution.py:341
  64.7 6.4 %collective-permute-start.8 = (bf16[256,512]{1,0:T(8,128)(2,1)S(1)}, bf16[256,512]{1,0:T(8,128)(2,1)S(1)}, u32[]{:S(2)}, u32[]{:S(2)}) collective-permute-start(bf16[256,512]{1,0:T(8,128)(2,1)S(1)} %pad_maximum_fusion.rest_0_), channel_id=1, source_target_pairs={{0,32},{8,40},{16,48},{24,56},{32,64},{40,72},{48,80},{56,88},{64,... | collective-permute-start | bytes 786440 | tf_op jit(solution)/shard_map/ppermute | solution.py:341
  71.1 6.4 %collective-permute-start.9 = (bf16[2,256,512]{2,1,0:T(8,128)(2,1)}, bf16[2,256,512]{2,1,0:T(8,128)(2,1)S(1)}, u32[]{:S(2)}, u32[]{:S(2)}) collective-permute-start(bf16[2,256,512]{2,1,0:T(8,128)(2,1)} %get-tuple-element.66), channel_id=1, source_target_pairs={{0,1},{1,0},{2,3},{3,2},{4,5},{5,4},{6,7},{7,6},{8,9},{9,8},{10,11... | collective-permute-start | bytes 1572872 | tf_op jit(solution)/shard_map/ppermute | solution.py:351
  78.8 11.0 %collective-permute-start.10 = (bf16[1,256,512]{2,1,0:T(8,128)(2,1)S(1)}, bf16[1,256,512]{2,1,0:T(8,128)(2,1)S(1)}, u32[]{:S(2)}, u32[]{:S(2)}) collective-permute-start(bf16[1,256,512]{2,1,0:T(8,128)(2,1)S(1)} %get-tuple-element.110), channel_id=1, source_target_pairs={{0,2},{1,3},{2,4},{3,5},{4,6},{5,7},{6,0},{7,1},{8,10},{9,11},{10,... | collective-permute-start | bytes 786440 | tf_op jit(solution)/shard_map/ppermute | solution.py:354
  79.3 10.5 %collective-permute-start.11 = (bf16[1,256,512]{2,1,0:T(8,128)(2,1)S(1)}, bf16[1,256,512]{2,1,0:T(8,128)(2,1)}, u32[]{:S(2)}, u32[]{:S(2)}) collective-permute-start(bf16[1,256,512]{2,1,0:T(8,128)(2,1)S(1)} %get-tuple-element.109), channel_id=1, source_target_pairs={{0,6},{1,7},{2,0},{3,1},{4,2},{5,3},{6,4},{7,5},{8,14},{9,15},{10,... | collective-permute-start | bytes 786440 | tf_op jit(solution)/shard_map/ppermute | solution.py:354
  81.6 8.1 %collective-permute-start.12 = (bf16[128,512]{1,0:T(8,128)(2,1)S(1)}, bf16[128,512]{1,0:T(8,128)(2,1)S(1)}, u32[]{:S(2)}, u32[]{:S(2)}) collective-permute-start(bf16[128,512]{1,0:T(8,128)(2,1)S(1)} %slice.60), channel_id=1, source_target_pairs={{0,96},{8,104},{16,112},{24,120},{32,0},{40,8},{48,16},{56,24},{64... | collective-permute-start | bytes 393224 | tf_op jit(solution)/shard_map/ppermute | solution.py:341
  81.8 10.9 %copy-start.8 = (s32[1,64]{1,0:T(1,128)S(1)}, s32[1,64]{1,0:T(1,128)}, u32[]{:S(2)}) copy-start(s32[1,64]{1,0:T(1,128)} %param.18) | copy-start | bytes 772
  81.8 12.8 %copy-start.9 = (s32[1,64]{1,0:T(1,128)S(1)}, s32[1,64]{1,0:T(1,128)}, u32[]{:S(2)}) copy-start(s32[1,64]{1,0:T(1,128)} %param.19) | copy-start | bytes 772
  81.8 7.9 %collective-permute-start.13 = (bf16[128,512]{1,0:T(8,128)(2,1)S(1)}, bf16[128,512]{1,0:T(8,128)(2,1)S(1)}, u32[]{:S(2)}, u32[]{:S(2)}) collective-permute-start(bf16[128,512]{1,0:T(8,128)(2,1)S(1)} %slice.61), channel_id=1, source_target_pairs={{0,32},{8,40},{16,48},{24,56},{32,64},{40,72},{48,80},{56,88},{64,... | collective-permute-start | bytes 393224 | tf_op jit(solution)/shard_map/ppermute | solution.py:341
  89.8 8.4 %collective-permute-start.14 = (bf16[4,256,512]{2,1,0:T(8,128)(2,1)}, bf16[4,256,512]{2,1,0:T(8,128)(2,1)}, u32[]{:S(2)}, u32[]{:S(2)}) collective-permute-start(bf16[4,256,512]{2,1,0:T(8,128)(2,1)} %get-tuple-element.82), channel_id=1, source_target_pairs={{0,1},{1,0},{2,3},{3,2},{4,5},{5,4},{6,7},{7,6},{8,9},{9,8},{10,11... | collective-permute-start | bytes 3145736 | tf_op jit(solution)/shard_map/ppermute | solution.py:351
  94.7 3.6 %copy-start.2 = (bf16[2,256,512]{2,1,0:T(8,128)(2,1)S(1)}, bf16[2,256,512]{2,1,0:T(8,128)(2,1)}, u32[]{:S(2)}) copy-start(bf16[2,256,512]{2,1,0:T(8,128)(2,1)} %get-tuple-element.75) | copy-start | bytes 1572868
  94.7 3.6 %copy-start.3 = (bf16[2,256,512]{2,1,0:T(8,128)(2,1)S(1)}, bf16[2,256,512]{2,1,0:T(8,128)(2,1)}, u32[]{:S(2)}) copy-start(bf16[2,256,512]{2,1,0:T(8,128)(2,1)} %get-tuple-element.84) | copy-start | bytes 1572868
  100.8 7.3 %collective-permute-start.15 = (bf16[256,512]{1,0:T(8,128)(2,1)S(1)}, bf16[256,512]{1,0:T(8,128)(2,1)S(1)}, u32[]{:S(2)}, u32[]{:S(2)}) collective-permute-start(bf16[256,512]{1,0:T(8,128)(2,1)S(1)} %slice.70), channel_id=1, source_target_pairs={{0,1},{1,0},{2,3},{3,2},{4,5},{5,4},{6,7},{7,6},{8,9},{9,8},{10,11... | collective-permute-start | bytes 786440 | tf_op jit(solution)/shard_map/ppermute | solution.py:351
  100.9 8.7 %collective-permute-start.16 = (bf16[1,256,512]{2,1,0:T(8,128)(2,1)S(1)}, bf16[1,256,512]{2,1,0:T(8,128)(2,1)S(1)}, u32[]{:S(2)}, u32[]{:S(2)}) collective-permute-start(bf16[1,256,512]{2,1,0:T(8,128)(2,1)S(1)} %get-tuple-element.92), channel_id=1, source_target_pairs={{0,2},{1,3},{2,4},{3,5},{4,6},{5,7},{6,0},{7,1},{8,10},{9,11},{10,... | collective-permute-start | bytes 786440 | tf_op jit(solution)/shard_map/ppermute | solution.py:354
  101.0 8.7 %collective-permute-start.17 = (bf16[1,256,512]{2,1,0:T(8,128)(2,1)S(1)}, bf16[1,256,512]{2,1,0:T(8,128)(2,1)S(1)}, u32[]{:S(2)}, u32[]{:S(2)}) collective-permute-start(bf16[1,256,512]{2,1,0:T(8,128)(2,1)S(1)} %get-tuple-element.93), channel_id=1, source_target_pairs={{0,6},{1,7},{2,0},{3,1},{4,2},{5,3},{6,4},{7,5},{8,14},{9,15},{10,... | collective-permute-start | bytes 786440 | tf_op jit(solution)/shard_map/ppermute | solution.py:354
  103.7 7.2 %copy-start.4 = (bf16[512,512]{1,0:T(8,128)(2,1)S(1)}, bf16[512,512]{1,0:T(8,128)(2,1)}, u32[]{:S(2)}) copy-start(bf16[512,512]{1,0:T(8,128)(2,1)} %far_incoming.1) | copy-start | bytes 1572868
  109.6 15.1 %collective-permute-start.18 = (bf16[2,256,512]{2,1,0:T(8,128)(2,1)}, bf16[2,256,512]{2,1,0:T(8,128)(2,1)S(1)}, u32[]{:S(2)}, u32[]{:S(2)}) collective-permute-start(bf16[2,256,512]{2,1,0:T(8,128)(2,1)} %get-tuple-element.96), channel_id=1, source_target_pairs={{0,1},{1,0},{2,3},{3,2},{4,5},{5,4},{6,7},{7,6},{8,9},{9,8},{10,11... | collective-permute-start | bytes 1572872 | tf_op jit(solution)/shard_map/ppermute | solution.py:351
  111.0 13.7 %collective-permute-start.19 = (bf16[1,256,512]{2,1,0:T(8,128)(2,1)S(1)}, bf16[1,256,512]{2,1,0:T(8,128)(2,1)S(1)}, u32[]{:S(2)}, u32[]{:S(2)}) collective-permute-start(bf16[1,256,512]{2,1,0:T(8,128)(2,1)S(1)} %get-tuple-element.97), channel_id=1, source_target_pairs={{0,2},{1,3},{2,4},{3,5},{4,6},{5,7},{6,0},{7,1},{8,10},{9,11},{10,... | collective-permute-start | bytes 786440 | tf_op jit(solution)/shard_map/ppermute | solution.py:354
  111.1 13.7 %collective-permute-start.20 = (bf16[1,256,512]{2,1,0:T(8,128)(2,1)S(1)}, bf16[1,256,512]{2,1,0:T(8,128)(2,1)S(1)}, u32[]{:S(2)}, u32[]{:S(2)}) collective-permute-start(bf16[1,256,512]{2,1,0:T(8,128)(2,1)S(1)} %get-tuple-element.98), channel_id=1, source_target_pairs={{0,6},{1,7},{2,0},{3,1},{4,2},{5,3},{6,4},{7,5},{8,14},{9,15},{10,... | collective-permute-start | bytes 786440 | tf_op jit(solution)/shard_map/ppermute | solution.py:354
  113.8 7.8 %collective-permute-start.21 = (bf16[64,512]{1,0:T(8,128)(2,1)S(1)}, bf16[64,512]{1,0:T(8,128)(2,1)S(1)}, u32[]{:S(2)}, u32[]{:S(2)}) collective-permute-start(bf16[64,512]{1,0:T(8,128)(2,1)S(1)} %get-tuple-element.113), channel_id=1, source_target_pairs={{0,2},{1,3},{2,4},{3,5},{4,6},{5,7},{6,0},{7,1},{8,10},{9,11},{10,... | collective-permute-start | bytes 196616 | tf_op jit(solution)/shard_map/ppermute | solution.py:354
  113.9 10.3 %collective-permute-start.22 = (bf16[64,512]{1,0:T(8,128)(2,1)S(1)}, bf16[64,512]{1,0:T(8,128)(2,1)S(1)}, u32[]{:S(2)}, u32[]{:S(2)}) collective-permute-start(bf16[64,512]{1,0:T(8,128)(2,1)S(1)} %get-tuple-element.112), channel_id=1, source_target_pairs={{0,4},{1,5},{2,6},{3,7},{4,0},{5,1},{6,2},{7,3},{8,12},{9,13},{10,... | collective-permute-start | bytes 196616 | tf_op jit(solution)/shard_map/ppermute | solution.py:354
  121.6 3.1 %collective-permute-start.23 = (bf16[64,512]{1,0:T(8,128)(2,1)S(1)}, bf16[64,512]{1,0:T(8,128)(2,1)S(1)}, u32[]{:S(2)}, u32[]{:S(2)}) collective-permute-start(bf16[64,512]{1,0:T(8,128)(2,1)S(1)} %get-tuple-element.111), channel_id=1, source_target_pairs={{0,6},{1,7},{2,0},{3,1},{4,2},{5,3},{6,4},{7,5},{8,14},{9,15},{10,... | collective-permute-start | bytes 196616 | tf_op jit(solution)/shard_map/ppermute | solution.py:354
  124.7 1.0 copy-start.1

commit v3 on v2

v3 whole, which is shorter than its diff:
```python
import jax
import jax.numpy as jnp
from jax import lax
from jax.experimental import pallas as pl
from jax.experimental.pallas import tpu as pltpu
from jax.sharding import PartitionSpec as P

reach = 2


def in_hbm(*values):
    return [pltpu.with_memory_space_constraint(value, pltpu.HBM) for value in values]


def far_incoming(cols_ref, moments, coupling_ref, rows_ref, gathered, spread, arrived):
    slots = cols_ref.shape[0]
    rank = coupling_ref.shape[0]
    couplings = coupling_ref[...]
    rows = rows_ref[...]
    for target in range(spread.shape[0] // rank):
        spread[target * rank : (target + 1) * rank, :] = jnp.where(
            rows == target, couplings, jnp.zeros_like(couplings)
        )
    arrived()

    def pick(slot, carry):
        source = pl.multiple_of(cols_ref[slot] * rank, rank)
        here = pl.multiple_of(slot * rank, rank)
        gathered[pl.ds(here, rank), :] = moments[pl.ds(source, rank), :]
        return carry

    lax.fori_loop(0, slots, pick, 0, unroll=4)
    return jnp.dot(spread[...], gathered[...], preferred_element_type=jnp.float32)


def near_terms(place, targets, blocks, parts, columns, splits, window, partial=None, far=None):
    count = targets.shape[0]
    size = blocks.shape[1]
    part_rows, excitations = parts[0].shape
    per_target = len(columns)
    depth = per_target * size
    ahead = min(4, count)
    finishing = partial is not None
    far_cols, moment_parts, *coupling = far or (None, [])
    moment_sizes = [part.shape[0] for part in moment_parts]
    starts = [sum(splits[:index]) for index in range(len(splits))]

    def kernel(place_ref, target_ref, *rest):
        rest = list(rest)
        if far:
            cols_ref = rest.pop(0)
        blocks_ref = rest.pop(0)
        part_refs = [rest.pop(0) for _ in parts]
        if finishing:
            partial_ref = rest.pop(0)
        if far:
            moment_refs = [rest.pop(0) for _ in moment_parts]
            coupling_ref, rows_ref = rest.pop(0), rest.pop(0)
        out_refs = [rest.pop(0) for _ in splits]
        if far:
            far_ref = rest.pop(0)
        held, sources, result, held_sem, source_sem, result_sem = [rest.pop(0) for _ in range(6)]
        if finishing:
            running, running_sem = rest.pop(0), rest.pop(0)
        if far:
            moments, gathered, spread, moment_sem = rest

        def source_copy(index):
            return pltpu.make_async_copy(
                part_refs[index],
                sources.at[pl.ds(index * part_rows, part_rows), :],
                source_sem.at[index],
            )

        def running_copy(step):
            return pltpu.make_async_copy(
                partial_ref.at[target_ref[step]], running.at[step], running_sem.at[step]
            )

        def moment_copy(index):
            here = pl.ds(sum(moment_sizes[:index]), moment_sizes[index])
            return pltpu.make_async_copy(
                moment_refs[index], moments.at[here, :], moment_sem.at[index]
            )

        def far_copies():
            return (
                pltpu.make_async_copy(
                    result.at[count], out_refs[0].at[splits[0]], result_sem.at[count]
                ),
                pltpu.make_async_copy(
                    result.at[count + 1], far_ref.at[0], result_sem.at[count + 1]
                ),
            )

        def moments_arrived():
            for index in range(len(moment_parts)):
                moment_copy(index).wait()

        def begin(step):
            first = target_ref[step] * window
            for index, column in enumerate(columns):
                slot = jnp.maximum(place_ref[first + column], 0)
                pltpu.make_async_copy(
                    blocks_ref.at[slot], held.at[step * per_target + index], held_sem.at[step]
                ).start()
            if finishing:
                running_copy(step).start()

        def work(step):
            first = target_ref[step] * window
            pltpu.make_async_copy(
                blocks_ref.at[pl.ds(0, per_target)],
                held.at[pl.ds(step * per_target, per_target)],
                held_sem.at[step],
            ).wait()
            if finishing:
                running_copy(step).wait()
            total = None
            for index, column in enumerate(columns):
                here = jnp.where(
                    place_ref[first + column] >= 0, step * per_target + index, count * per_target
                )
                product = jnp.dot(
                    held[here],
                    sources[index * size : (index + 1) * size, :],
                    preferred_element_type=jnp.float32,
                )
                total = product if total is None else total + product
            if finishing:
                total = total + running[step].astype(jnp.float32)
            result[step] = total.astype(result.dtype)

        begin(0)
        for index in range(len(parts)):
            source_copy(index).start()
        for index in range(len(moment_parts)):
            moment_copy(index).start()
        for step in range(1, ahead):
            begin(step)
        held[count * per_target] = jnp.zeros((size, size), held.dtype)
        if far:
            incoming = far_incoming(
                cols_ref, moments, coupling_ref, rows_ref, gathered, spread, moments_arrived
            )
            result[count] = incoming[:size].astype(result.dtype)
            result[count + 1] = incoming[size:].astype(result.dtype)
            for copy in far_copies():
                copy.start()
        for index in range(len(parts)):
            source_copy(index).wait()

        def result_copy(index, step):
            return pltpu.make_async_copy(
                result.at[step], out_refs[index].at[step - starts[index]], result_sem.at[step]
            )

        for index in range(len(splits)):
            first, last = starts[index], starts[index] + splits[index]

            def both(step, carry):
                begin(step + ahead)
                return only(step, carry)

            def only(step, carry):
                work(step)
                result_copy(index, step).start()
                return carry

            middle = min(max(first, count - ahead), last)
            lax.fori_loop(first, middle, both, 0)
            lax.fori_loop(middle, last, only, 0)
        for index in range(len(splits)):

            def end(step, carry):
                result_copy(index, step).wait()
                return carry

            lax.fori_loop(starts[index], starts[index] + splits[index], end, 0)
        if far:
            for copy in far_copies():
                copy.wait()

    anywhere = pl.BlockSpec(memory_space=pltpu.HBM)
    extras = (partial,) if finishing else ()
    more = 2 if far else 0
    scratch = [
        pltpu.VMEM((count * per_target + 1, size, size), jnp.bfloat16),
        pltpu.VMEM((depth, excitations), jnp.bfloat16),
        pltpu.VMEM((count + more, size, excitations), jnp.bfloat16),
        pltpu.SemaphoreType.DMA((count,)),
        pltpu.SemaphoreType.DMA((len(parts),)),
        pltpu.SemaphoreType.DMA((count + more,)),
    ]
    if finishing:
        scratch += [
            pltpu.VMEM((count, size, excitations), jnp.bfloat16),
            pltpu.SemaphoreType.DMA((count,)),
        ]
    shapes = [(split, size, excitations) for split in splits]
    coupling_specs = [pl.BlockSpec(item.shape, lambda i, *_: (0, 0)) for item in coupling]
    if far:
        shapes[0] = (splits[0] + 1, size, excitations)
        shapes.append((1, size, excitations))
        scratch += [
            pltpu.VMEM((sum(moment_sizes), excitations), jnp.bfloat16),
            pltpu.VMEM((coupling[0].shape[1], excitations), jnp.bfloat16),
            pltpu.VMEM((2 * size, coupling[0].shape[1]), jnp.bfloat16),
            pltpu.SemaphoreType.DMA((len(moment_parts),)),
        ]
    return pl.pallas_call(
        kernel,
        grid_spec=pltpu.PrefetchScalarGridSpec(
            num_scalar_prefetch=3 if far else 2,
            grid=(1,),
            in_specs=[anywhere] * (1 + len(parts) + len(extras) + len(moment_parts))
            + coupling_specs,
            out_specs=[anywhere] * len(shapes),
            scratch_shapes=scratch,
        ),
        out_shape=[pltpu.HBM(shape, jnp.bfloat16) for shape in shapes],
        compiler_params=pltpu.CompilerParams(
            vmem_limit_bytes=2 * size * (count * per_target * size + (depth + 2 * count * size) * 2)
            + (14 if far else 4) * 2**20
        ),
        cost_estimate=pl.CostEstimate(
            flops=2 * count * size * depth * excitations,
            bytes_accessed=2 * (count * size * depth + depth * excitations),
            transcendentals=0,
        ),
        name="near_rest" if finishing else "near_first",
    )(
        place,
        targets,
        *([far_cols] if far else []),
        *in_hbm(blocks),
        *parts,
        *in_hbm(*extras),
        *moment_parts,
        *coupling,
    )


def finish_kernel(
    kept_ref, got_ref, below_late, above_late, below_early, above_early, far_ref, basis_ref, out_ref
):
    owned, size, _ = out_ref.shape
    rank = basis_ref.shape[2] // 3
    sides = [[below_late, above_early], [below_early, above_late]]
    relayed = [below_late, above_late]
    for cluster in range(owned):
        rows = slice(size + cluster * rank, size + (cluster + 1) * rank)
        incoming = far_ref[cluster * rank : (cluster + 1) * rank, :].astype(jnp.float32)
        incoming = incoming + below_early[rows, :].astype(jnp.float32)
        incoming = incoming + above_early[rows, :].astype(jnp.float32)
        incoming = incoming + relayed[cluster][size : size + rank, :].astype(jnp.float32)
        high = incoming.astype(jnp.bfloat16)
        left = incoming - high.astype(jnp.float32)
        middle = left.astype(jnp.bfloat16)
        low = (left - middle.astype(jnp.float32)).astype(jnp.bfloat16)
        total = jnp.dot(
            basis_ref[cluster],
            jnp.concatenate([high, middle, low]),
            preferred_element_type=jnp.float32,
        )
        total = total + kept_ref[cluster].astype(jnp.float32)
        total = total + got_ref[cluster].astype(jnp.float32)
        for side in sides[cluster]:
            total = total + side[0:size, :].astype(jnp.float32)
        out_ref[cluster] = total.astype(out_ref.dtype)


def finish(kept, got, late, early, far, basis):
    operands = [kept, got, *late, *early, far, basis]
    whole = pl.BlockSpec(memory_space=pltpu.VMEM)
    return pl.pallas_call(
        finish_kernel,
        in_specs=[whole] * len(operands),
        out_specs=whole,
        out_shape=jax.ShapeDtypeStruct(kept.shape, jnp.bfloat16),
        compiler_params=pltpu.CompilerParams(vmem_limit_bytes=16 * 2**20),
        cost_estimate=pl.CostEstimate(
            flops=2 * kept.size * basis.shape[2],
            bytes_accessed=2 * 5 * kept.size,
            transcendentals=0,
        ),
        name="finish",
    )(*operands)


def add(*terms):
    total = terms[0].astype(jnp.float32)
    for term in terms[1:]:
        total = total + term.astype(jnp.float32)
    return total.astype(jnp.bfloat16)


def shards(
    charges,
    send_order,
    near_rows,
    near_cols,
    near_count,
    near_blocks,
    far_rows,
    far_cols,
    far_count,
    couplings,
    row_basis,
    col_basis,
):
    row_count = lax.axis_size("row")
    col_count = lax.axis_size("col")
    device_count = row_count * col_count
    panels, excitations = charges.shape
    segment = panels // device_count
    owned, rank, leaf = col_basis.shape
    targets = row_basis.shape[0]
    window = (2 * reach + 1) * owned
    row = lax.axis_index("row")
    col = lax.axis_index("col")

    outgoing = charges.at[send_order[0]].get(mode="promise_in_bounds")
    incoming = lax.all_to_all(
        outgoing.reshape(device_count, segment, excitations),
        ("row", "col"),
        split_axis=0,
        concat_axis=0,
        tiled=True,
    )
    slab = incoming.reshape(panels, excitations)
    (
        slab,
        near_rows,
        near_cols,
        near_count,
        far_rows,
        far_cols,
        far_count,
        couplings,
        row_basis,
    ) = lax.optimization_barrier(
        (
            slab,
            near_rows,
            near_cols,
            near_count,
            far_rows,
            far_cols,
            far_count,
            couplings,
            row_basis,
        )
    )
    def row_shift(value, step):
        return lax.ppermute(value, "row", [(i, (i + step) % row_count) for i in range(row_count)])

    def other_core(value):
        return lax.ppermute(value, "col", [(i, i ^ 1) for i in range(col_count)])

    def chip_shift(value, step):
        return lax.ppermute(
            value, "col", [(i, (i + 2 * step) % col_count) for i in range(col_count)]
        )

    below = row_shift(slab, 1)
    above = row_shift(slab, -1)
    moments = (
        jnp.einsum(
            "gkb,gbr->gkr",
            col_basis,
            slab.reshape(owned, leaf, excitations),
            preferred_element_type=jnp.float32,
        )
        .astype(jnp.bfloat16)
        .reshape(owned * rank, excitations)
    )
    slots = jnp.arange(near_rows.shape[1], dtype=jnp.int32)
    pair = near_rows[0] * window + near_cols[0] - (row - reach) * owned
    pair = jnp.where(slots < near_count[0], pair, -1)
    wanted = jnp.arange(targets * window, dtype=jnp.int32)
    place = jnp.max(jnp.where(pair[None, :] == wanted[:, None], slots[None, :], -1), axis=1)

    far_slots = far_rows.shape[1]
    far_target = jnp.where(
        jnp.arange(far_slots, dtype=jnp.int32) < far_count[0], far_rows[0], -1
    )
    coupling_rows = couplings[0].transpose(1, 0, 2).reshape(rank, far_slots * rank)
    own_basis = lax.dynamic_slice_in_dim(row_basis, col * owned, owned, 0)
    own_basis = jnp.tile(own_basis.transpose(0, 2, 1), (1, 1, 3))
    far_source = far_cols[0]

    chips = col_count // 2
    chip, core = col // 2, col % 2
    each = jnp.arange(owned, dtype=jnp.int32)

    def clusters(chip_step, which):
        return (((chip + chip_step) % chips) * 2 + which) * owned + each

    def order(*chip_steps):
        return jnp.concatenate(
            [clusters(step, 1 - core) for step in chip_steps]
            + [clusters(step, core) for step in chip_steps]
        )

    far_chip = (far_target // (2 * owned) - chip) % chips
    far_core = (far_target // owned + 1 - core) % 2
    far_place = (far_core * chips + far_chip) * owned + far_target % owned
    far_place = jnp.where(far_target >= 0, far_place, -1)
    slot_rows = jnp.repeat(far_place, rank)[None, :]

    blocks = near_blocks[0]
    everyone = jnp.arange(targets, dtype=jnp.int32)
    middle = list(range(reach * owned, (reach + 1) * owned))
    inner = [column for column in range(owned, window - owned) if column not in middle]
    outer = list(range(owned)) + list(range(window - owned, window))
    (partial,) = near_terms(place, everyone, blocks, [slab], middle, [targets], window)
    below, above, partial, coupling_rows, slot_rows, far_source, own_basis = (
        lax.optimization_barrier(
            (below, above, partial, coupling_rows, slot_rows, far_source, own_basis)
        )
    )
    below_more = row_shift(below, 1)
    above_more = row_shift(above, -1)
    (partial,) = near_terms(
        place, everyone, blocks, [below, above], inner, [targets], window, partial
    )

    def rest(*chip_steps, far=None):
        return near_terms(
            place,
            order(*chip_steps),
            blocks,
            [below_more, above_more],
            outer,
            [owned * len(chip_steps)] + [owned] * len(chip_steps),
            window,
            partial,
            far,
        )

    moments, partial, below_more, above_more = lax.optimization_barrier(
        (moments, partial, below_more, above_more)
    )
    all_moments = lax.all_to_all(
        jnp.tile(moments, (row_count, 1)), "row", split_axis=0, concat_axis=0, tiled=True
    )
    sent, kept = rest(2)
    sent, all_moments = lax.optimization_barrier((sent, all_moments))
    got = other_core(sent)
    opposite = [add(kept[index], got[index]) for index in range(owned)]
    opposite, place = lax.optimization_barrier((opposite, place))
    from_below = chip_shift(opposite[0], 1)
    from_above = chip_shift(opposite[1], -1)
    sent, kept_up, kept_down, kept_far = rest(
        1, -1, far=(far_source, [all_moments], coupling_rows, slot_rows)
    )
    sent, from_below, from_above = lax.optimization_barrier((sent, from_below, from_above))
    got = other_core(sent)
    far = add(kept_far[0], got[2 * owned]).reshape(chips, owned * rank, excitations)
    early = [
        jnp.concatenate([add(kept_up[1], got[1]), far[1], far[2, :rank]]),
        jnp.concatenate([add(kept_down[0], got[owned]), far[chips - 1], far[2, rank:]]),
    ]
    early, place, own_far = lax.optimization_barrier((early, place, far[0]))
    early = [chip_shift(early[0], 1), chip_shift(early[1], -1)]
    sent, kept = rest(0)
    sent, early = lax.optimization_barrier((sent, early))
    passed = [side[leaf + owned * rank :] for side in early]
    late = [
        jnp.concatenate([add(kept_up[0], got[0], from_below), passed[0]]),
        jnp.concatenate([add(kept_down[1], got[owned + 1], from_above), passed[1]]),
    ]
    late = [chip_shift(late[0], 1), chip_shift(late[1], -1)]
    got = other_core(sent)
    return finish(kept, got, late, early, own_far, own_basis).reshape(panels, excitations)


def solution(mesh):
    placed = (
        P(("row", "col"), None),
        P(("row", "col"), None),
        P(("row", "col"), None),
        P(("row", "col"), None),
        P(("row", "col")),
        P(("row", "col"), None, None, None),
        P(("row", "col"), None),
        P(("row", "col"), None),
        P(("row", "col")),
        P(("row", "col"), None, None, None),
        P("row", None, None),
        P(("row", "col"), None, None),
    )
    return jax.shard_map(
        shards, mesh=mesh, in_specs=placed, out_specs=P(("row", "col"), None), check_vma=False
    )
```

time: 128 us -> 133 us (1.039)
  waiting for transfers between devices: 27 us -> 43.3 us
  starting transfers between devices: 47.8 us -> 38 us
  other arithmetic: 4.06 us -> 6.91 us
  Pallas kernels: 38 us -> 35.4 us
    all_to_all x0 -> x1, waiting for transfers between devices: none -> 8.99 us  [shards(): lax.all_to_all(jnp.tile(moments, (row_count, 1)), 'row', split_axis=0, co...]
    ppermute x8 -> x4, starting transfers between devices: 13.8 us -> 6.38 us  [row_shift(): lax.ppermute(value, 'row', [(i, (i + step) % row_count) for i in range(ro...]
    all_to_all x0 -> x1, starting transfers between devices: none -> 4.95 us  [shards(): lax.all_to_all(jnp.tile(moments, (row_count, 1)), 'row', split_axis=0, co...]
    ppermute x9 -> x6, waiting for transfers between devices: 7.44 us -> 11.9 us  [chip_shift(): lax.ppermute(value, 'col', [(i, (i + 2 * step) % col_count) for i in rang...]
    ppermute x9 -> x6, starting transfers between devices: 12.4 us -> 8.16 us  [chip_shift(): lax.ppermute(value, 'col', [(i, (i + 2 * step) % col_count) for i in rang...]
    pallas_call x1 -> x0, Pallas kernels: 3.48 us -> none  [far_incoming(): pl.pallas_call(far_kernel, grid_spec=pltpu.PrefetchScalarGridSpec(num_sca...]
    ppermute x4 -> x3, waiting for transfers between devices: 1.75 us -> 4.53 us  [other_core(): return lax.ppermute(value, 'col', [(i, i ^ 1) for i in range(col_count)])]
    ppermute x3 -> x0, starting transfers between devices: 1.94 us -> none  [line_shift(): lax.ppermute(value, 'row', [(i, i // across * across + (i + step) % acros...]
  transfers between devices with their start and end apart: 25 -> 15, of which waited for: 9 -> 9; matrix products, arithmetic and copies ran while one was open for 3% -> 4% of each run, Pallas kernels for 29% -> 26%
where the time goes in v3:
time: 133 us
  waiting for transfers between devices  43.3 us (33%)
  starting transfers between devices  38 us (29%)
  Pallas kernels  35.4 us (27%)
  local copies, waits for them, and re-layouts  7.06 us (5%)
  other arithmetic  6.91 us (5%)
  between operations  1.71 us (1%)
    pallas_call x5, Pallas kernels, near_terms(): pl.pallas_call(kernel, grid_spec=pltpu.PrefetchScalarGridSpec(num_scalar_...  34.1 us
    all_to_all x1, waiting for transfers between devices, shards(): lax.all_to_all(outgoing.reshape(device_count, segment, excitations), ('ro...  12.2 us
    ppermute x6, waiting for transfers between devices, chip_shift(): lax.ppermute(value, 'col', [(i, (i + 2 * step) % col_count) for i in rang...  11.9 us
    all_to_all x1, starting transfers between devices, shards(): lax.all_to_all(outgoing.reshape(device_count, segment, excitations), ('ro...  11.5 us
    all_to_all x1, waiting for transfers between devices, shards(): lax.all_to_all(jnp.tile(moments, (row_count, 1)), 'row', split_axis=0, co...  8.99 us
    ppermute x6, starting transfers between devices, chip_shift(): lax.ppermute(value, 'col', [(i, (i + 2 * step) % col_count) for i in rang...  8.16 us
    ppermute x3, starting transfers between devices, other_core(): return lax.ppermute(value, 'col', [(i, i ^ 1) for i in range(col_count)])  7.04 us
    ppermute x4, starting transfers between devices, row_shift(): lax.ppermute(value, 'row', [(i, (i + step) % row_count) for i in range(ro...  6.38 us
  transfers between devices with their start and end apart: 15, of which 9 were waited for; matrix products, arithmetic and copies ran while one was open for 4% of the time, Pallas kernels for 26%

profile of v3, /device:TPU:1, one launch (start us, length us, event | category | flops | bytes accessed | tf_op | source)
XLA Modules:
  0.0 132.6 jit_solution(4087870036376787250)
XLA Ops:
  0.0 0.7 compare_select_fusion
  0.8 0.3 copy-done
  1.1 2.0 %gather_fusion = bf16[512,512]{1,0:T(8,128)(2,1)S(1)} fusion(bf16[512,512]{1,0:T(8,128)(2,1)S(1)} %copy-done, s32[1024]{0:T(1024)S(1)} %pad_clamp_fusion), kind=kCustom, calls=%fused_computation | custom fusion | bytes 1050624 | tf_op jit(solution)/shard_map/gather | solution.py:323
  3.0 0.9 reshape.106
  4.0 11.5 %all-to-all-start = ((bf16[128,4,512]{2,1,0:T(4,128)(2,1)}), bf16[128,4,512]{2,1,0:T(4,128)(2,1)S(1)}, u32[]{:S(2)}, u32[]{:S(2)}) async-start(bf16[128,4,512]{2,1,0:T(4,128)(2,1)} %reshape.106), calls=%async_computation | async-start | bytes 1048576 | tf_op jit(solution)/shard_map/all_to_all | solution.py:324
  16.8 0.0 copy-start.12
  16.8 0.0 copy-start.13
  16.8 12.2 %all-to-all-done = bf16[128,4,512]{2,1,0:T(4,128)(2,1)S(1)} async-done(((bf16[128,4,512]{2,1,0:T(4,128)(2,1)}), bf16[128,4,512]{2,1,0:T(4,128)(2,1)S(1)}, u32[]{:S(2)}, u32[]{:S(2)}) %all-to-all-start) | async-done | bytes 524320 | tf_op jit(solution)/shard_map/all_to_all | solution.py:324
  29.0 0.1 reshape.107.rest_1_
  29.1 1.1 collective-permute-start.1
  30.2 0.4 collective-permute-start
  30.7 0.1 broadcast_in_dim.32
  30.7 0.1 broadcast_in_dim_reshape.3.rest_7_
  30.8 0.0 copy-done.6
  30.8 0.3 copy.17
  31.1 0.5 reshape.110.rest_6_
  31.7 0.8 dynamic-slice_bitcast_fusion
  32.4 0.1 select_reduce_fusion.place_ref
  32.6 0.0 copy-start.11
  32.6 7.5 %near_first.1.rest_3_ = bf16[16,256,512]{2,1,0:T(8,128)(2,1)} custom-call(s32[160]{0:T(256)S(1)} %select_reduce_fusion.place_ref, s32[16]{0:T(128)S(1)} %iota.40.target_ref, bf16[160,256,256]{2,1,0:T(8,128)(2,1)} %bitcast.58, bf16[512,512]{1,0:T(8,128)(2,1)S(1)} %reshape.107.rest_1_), custom_call_target="tpu_custom_call" | custom-call | flops 2147483648 | bytes 4718592 | tf_op jit(solution)/shard_map/near_first/pallas_call | solution.py:211
  40.0 1.5 %collective-permute-done.1.rest_2_ = bf16[512,512]{1,0:T(8,128)(2,1)S(1)} collective-permute-done((bf16[512,512]{1,0:T(8,128)(2,1)S(1)}, bf16[512,512]{1,0:T(8,128)(2,1)S(1)}, u32[]{:S(2)}, u32[]{:S(2)}) %collective-permute-start.1) | collective-permute-done | bytes 524320 | tf_op jit(solution)/shard_map/ppermute | solution.py:356
  41.5 4.2 %collective-permute-done.rest_1_ = bf16[512,512]{1,0:T(8,128)(2,1)S(1)} collective-permute-done((bf16[512,512]{1,0:T(8,128)(2,1)S(1)}, bf16[512,512]{1,0:T(8,128)(2,1)S(1)}, u32[]{:S(2)}, u32[]{:S(2)}) %collective-permute-start) | collective-permute-done | bytes 524320 | tf_op jit(solution)/shard_map/ppermute | solution.py:356
  45.8 0.1 collective-permute-start.2
  45.8 4.8 %collective-permute-start.3 = (bf16[512,512]{1,0:T(8,128)(2,1)S(1)}, bf16[512,512]{1,0:T(8,128)(2,1)S(1)}, u32[]{:S(2)}, u32[]{:S(2)}) collective-permute-start(bf16[512,512]{1,0:T(8,128)(2,1)S(1)} %collective-permute-done.1.rest_2_), channel_id=1, source_target_pairs={{0,120},{8,0},{16,8},{24,16},{32,24},{40,32},{48,40},{56,48},{64,5... | collective-permute-start | bytes 1572872 | tf_op jit(solution)/shard_map/ppermute | solution.py:356
  50.6 0.2 convolution_convert_fusion
  50.8 10.5 %near_rest.4.rest_3_.rest_4_ = bf16[16,256,512]{2,1,0:T(8,128)(2,1)} custom-call(s32[160]{0:T(256)S(1)} %select_reduce_fusion.place_ref, s32[16]{0:T(128)S(1)} %iota.39.target_ref, bf16[160,256,256]{2,1,0:T(8,128)(2,1)} %bitcast.59, bf16[512,512]{1,0:T(8,128)(2,1)S(1)} %collective-permute-done.rest_1_, bf16[512,512]{1,0:T(8,128)(2,1)S(1)} %collective-permute-done.1.rest_2_, ...), custom_call_target="tpu_custom_call" | custom-call | flops 4294967296 | bytes 9437184 | tf_op jit(solution)/shard_map/near_rest/pallas_call | solution.py:211
  61.3 0.0 collective-permute-done.2.rest_1_.rest_2_
  61.4 0.0 collective-permute-done.3.rest_2_.rest_3_
  61.4 1.1 tile.8
  62.5 4.9 %all-to-all-start.1 = ((bf16[16,64,512]{2,1,0:T(8,128)(2,1)}), bf16[16,64,512]{2,1,0:T(8,128)(2,1)S(1)}, u32[]{:S(2)}, u32[]{:S(2)}) async-start(bf16[16,64,512]{2,1,0:T(8,128)(2,1)} %tile.8), calls=%async_computation.1 | async-start | bytes 2097152 | tf_op jit(solution)/shard_map/all_to_all | solution.py:445
  67.5 0.1 pad_add_fusion.target_ref
  67.6 4.6 %near_rest.5 = (bf16[2,256,512]{2,1,0:T(8,128)(2,1)}, bf16[2,256,512]{2,1,0:T(8,128)(2,1)}) custom-call(s32[160]{0:T(256)S(1)} %select_reduce_fusion.place_ref, s32[4]{0:T(128)S(1)} %pad_add_fusion.target_ref, bf16[160,256,256]{2,1,0:T(8,128)(2,1)} %bitcast.60, bf16[512,512]{1,0:T(8,128)(2,1)S(1)} %collective-permute-done.2.rest_1_.rest_2_, ...), custom_call_target="tpu_custom_call" | custom-call | flops 1073741824 | bytes 3145728 | tf_op jit(solution)/shard_map/near_rest/pallas_call | solution.py:211
  72.2 0.0 copy-start.2
  72.2 9.0 %all-to-all-done.1 = bf16[16,64,512]{2,1,0:T(8,128)(2,1)S(1)} async-done(((bf16[16,64,512]{2,1,0:T(8,128)(2,1)}), bf16[16,64,512]{2,1,0:T(8,128)(2,1)S(1)}, u32[]{:S(2)}, u32[]{:S(2)}) %all-to-all-start.1) | async-done | bytes 1048608 | tf_op jit(solution)/shard_map/all_to_all | solution.py:445
  81.2 4.8 %collective-permute-start.4 = (bf16[2,256,512]{2,1,0:T(8,128)(2,1)}, bf16[2,256,512]{2,1,0:T(8,128)(2,1)S(1)}, u32[]{:S(2)}, u32[]{:S(2)}) collective-permute-start(bf16[2,256,512]{2,1,0:T(8,128)(2,1)} %get-tuple-element.66), channel_id=1, source_target_pairs={{0,1},{1,0},{2,3},{3,2},{4,5},{5,4},{6,7},{7,6},{8,9},{9,8},{10,11... | collective-permute-start | bytes 1572872 | tf_op jit(solution)/shard_map/ppermute | solution.py:359
  86.0 1.7 %collective-permute-done.4 = bf16[2,256,512]{2,1,0:T(8,128)(2,1)S(1)} collective-permute-done((bf16[2,256,512]{2,1,0:T(8,128)(2,1)}, bf16[2,256,512]{2,1,0:T(8,128)(2,1)S(1)}, u32[]{:S(2)}, u32[]{:S(2)}) %collective-permute-start.4) | collective-permute-done | bytes 524320 | tf_op jit(solution)/shard_map/ppermute | solution.py:359
  87.8 1.2 fusion.3
  88.9 1.6 %collective-permute-start.5 = (bf16[256,512]{1,0:T(8,128)(2,1)S(1)}, bf16[256,512]{1,0:T(8,128)(2,1)S(1)}, u32[]{:S(2)}, u32[]{:S(2)}) collective-permute-start(bf16[256,512]{1,0:T(8,128)(2,1)S(1)} %get-tuple-element.74), channel_id=1, source_target_pairs={{0,2},{1,3},{2,4},{3,5},{4,6},{5,7},{6,0},{7,1},{8,10},{9,11},{10,... | collective-permute-start | bytes 786440 | tf_op jit(solution)/shard_map/ppermute | solution.py:362
  90.6 1.1 collective-permute-start.6
  91.7 0.1 pad_add_fusion.1.target_ref
  91.8 7.0 %near_rest.6 = (bf16[5,256,512]{2,1,0:T(8,128)(2,1)}, bf16[2,256,512]{2,1,0:T(8,128)(2,1)}, bf16[2,256,512]{2,1,0:T(8,128)(2,1)}, bf16[1,256,512]{2,1,0:T(8,128)(2,1)}) custom-call(s32[160]{0:T(256)S(1)} %select_reduce_fusion.place_ref, s32[8]{0:T(128)S(1)} %pad_add_fusion.1.target_ref, s32[64]{0:T(128)S(1)} %bitcast.57, bf16[160,256,256]{2,1,0:T(8,128)(2,1)} %bitcast.61, ...), custom_call_target="tpu_custom_call" | custom-call | flops 2147483648 | bytes 5242880 | tf_op jit(solution)/shard_map/near_rest/pallas_call | solution.py:211
  98.7 0.0 collective-permute-done.5
  98.7 0.0 collective-permute-done.6
  98.8 0.7 copy-done.7
  99.4 0.9 collective-permute-start.7
  100.4 0.1 pad_add_fusion.2.target_ref
  100.5 2.8 %collective-permute-done.7 = bf16[5,256,512]{2,1,0:T(8,128)(2,1)S(1)} collective-permute-done((bf16[5,256,512]{2,1,0:T(8,128)(2,1)}, bf16[5,256,512]{2,1,0:T(8,128)(2,1)S(1)}, u32[]{:S(2)}, u32[]{:S(2)}) %collective-permute-start.7) | collective-permute-done | bytes 1310752 | tf_op jit(solution)/shard_map/ppermute | solution.py:359
  103.2 1.8 %fusion.5 = (bf16[256,512]{1,0:T(8,128)(2,1)S(1)}, bf16[1,256,512]{2,1,0:T(8,128)(2,1)S(1)}, bf16[256,512]{1,0:T(8,128)(2,1)S(1)}) fusion(bf16[5,256,512]{2,1,0:T(8,128)(2,1)S(1)} %collective-permute-done.7, bf16[2,256,512]{2,1,0:T(8,128)(2,1)} %get-tuple-element.78, bf16[1,256,512]{2,1,0:T(8,128)(2,1)} %get-tuple-element.77, ...), kind=kLoop, calls=%fused_computation.18 | loop fusion | flops 1572864 | bytes 2359296 | tf_op jit(solution)/shard_map/convert_element_type | solution.py:295
  105.2 0.4 collective-permute-start.8
  105.6 2.3 %collective-permute-start.9 = (bf16[352,512]{1,0:T(8,128)(2,1)S(1)}, bf16[352,512]{1,0:T(8,128)(2,1)S(1)}, u32[]{:S(2)}, u32[]{:S(2)}) collective-permute-start(bf16[352,512]{1,0:T(8,128)(2,1)S(1)} %pad_maximum_fusion.1), channel_id=1, source_target_pairs={{0,6},{1,7},{2,0},{3,1},{4,2},{5,3},{6,4},{7,5},{8,14},{9,15},{10,... | collective-permute-start | bytes 1081352 | tf_op jit(solution)/shard_map/ppermute | solution.py:362
  108.0 4.5 %near_rest.7 = (bf16[2,256,512]{2,1,0:T(8,128)(2,1)}, bf16[2,256,512]{2,1,0:T(8,128)(2,1)}) custom-call(s32[160]{0:T(256)S(1)} %select_reduce_fusion.place_ref, s32[4]{0:T(128)S(1)} %pad_add_fusion.2.target_ref, bf16[160,256,256]{2,1,0:T(8,128)(2,1)} %bitcast.62, bf16[512,512]{1,0:T(8,128)(2,1)S(1)} %collective-permute-done.2.rest_1_.rest_2_, ...), custom_call_target="tpu_custom_call" | custom-call | flops 1073741824 | bytes 3145728 | tf_op jit(solution)/shard_map/near_rest/pallas_call | solution.py:211
  112.5 1.3 fusion
  113.8 2.3 %collective-permute-done.8.below_early = bf16[352,512]{1,0:T(8,128)(2,1)S(1)} collective-permute-done((bf16[352,512]{1,0:T(8,128)(2,1)S(1)}, bf16[352,512]{1,0:T(8,128)(2,1)S(1)}, u32[]{:S(2)}, u32[]{:S(2)}) %collective-permute-start.8) | collective-permute-done | bytes 360480 | tf_op jit(solution)/shard_map/ppermute | solution.py:362
  116.1 0.0 collective-permute-done.9.above_early
  116.1 1.3 collective-permute-start.10
  117.4 0.7 pad_maximum_fusion.3
  118.1 2.7 %collective-permute-start.12 = (bf16[288,512]{1,0:T(8,128)(2,1)}, bf16[288,512]{1,0:T(8,128)(2,1)S(1)}, u32[]{:S(2)}, u32[]{:S(2)}) collective-permute-start(bf16[288,512]{1,0:T(8,128)(2,1)} %pad_maximum_fusion.3), channel_id=1, source_target_pairs={{0,6},{1,7},{2,0},{3,1},{4,2},{5,3},{6,4},{7,5},{8,14},{9,15},{10,... | collective-permute-start | bytes 884744 | tf_op jit(solution)/shard_map/ppermute | solution.py:362
  120.8 0.7 pad_maximum_fusion.2
  121.5 0.0 collective-permute-start.11
  121.5 0.1 copy.18.basis_ref
  121.7 5.9 %collective-permute-done.12.above_late = bf16[288,512]{1,0:T(8,128)(2,1)S(1)} collective-permute-done((bf16[288,512]{1,0:T(8,128)(2,1)}, bf16[288,512]{1,0:T(8,128)(2,1)S(1)}, u32[]{:S(2)}, u32[]{:S(2)}) %collective-permute-start.12) | collective-permute-done | bytes 294944 | tf_op jit(solution)/shard_map/ppermute | solution.py:362
  127.6 3.7 %collective-permute-done.11.below_late = bf16[288,512]{1,0:T(8,128)(2,1)S(1)} collective-permute-done((bf16[288,512]{1,0:T(8,128)(2,1)}, bf16[288,512]{1,0:T(8,128)(2,1)S(1)}, u32[]{:S(2)}, u32[]{:S(2)}) %collective-permute-start.11) | collective-permute-done | bytes 294944 | tf_op jit(solution)/shard_map/ppermute | solution.py:362
  131.3 0.0 collective-permute-done.10.got_ref
  131.3 1.3 finish.1
  (39 shorter events, 0.2 us)
Async XLA Ops:
  0.0 1.1 copy-start
  3.9 26.7 %copy-start.14 = (s32[1,64]{1,0:T(1,128)S(1)}, s32[1,64]{1,0:T(1,128)}, u32[]{:S(2)}) copy-start(s32[1,64]{1,0:T(1,128)} %param.18) | copy-start | bytes 772
  4.0 26.9 %copy-start.6 = (bf16[1,64,32,32]{1,3,2,0:T(8,128)(2,1)S(1)}, bf16[1,64,32,32]{1,3,2,0:T(8,128)(2,1)}, u32[]{:S(2)}) copy-start(bf16[1,64,32,32]{1,3,2,0:T(8,128)(2,1)} %param.21) | copy-start | bytes 393220
  4.0 25.0 %all-to-all-start = ((bf16[128,4,512]{2,1,0:T(4,128)(2,1)}), bf16[128,4,512]{2,1,0:T(4,128)(2,1)S(1)}, u32[]{:S(2)}, u32[]{:S(2)}) async-start(bf16[128,4,512]{2,1,0:T(4,128)(2,1)} %reshape.106), calls=%async_computation | async-start | bytes 1048576 | tf_op jit(solution)/shard_map/all_to_all | solution.py:324
  16.8 15.7 %copy-start.12 = (s32[1,160]{1,0:T(1,128)S(1)}, s32[1,160]{1,0:T(1,128)}, u32[]{:S(2)}) copy-start(s32[1,160]{1,0:T(1,128)} %param.15) | copy-start | bytes 1924
  16.8 15.6 %copy-start.13 = (s32[1,160]{1,0:T(1,128)S(1)}, s32[1,160]{1,0:T(1,128)}, u32[]{:S(2)}) copy-start(s32[1,160]{1,0:T(1,128)} %param.14) | copy-start | bytes 1924
  29.1 12.4 %collective-permute-start.1 = (bf16[512,512]{1,0:T(8,128)(2,1)S(1)}, bf16[512,512]{1,0:T(8,128)(2,1)S(1)}, u32[]{:S(2)}, u32[]{:S(2)}) collective-permute-start(bf16[512,512]{1,0:T(8,128)(2,1)S(1)} %reshape.107.rest_1_), channel_id=1, source_target_pairs={{0,120},{8,0},{16,8},{24,16},{32,24},{40,32},{48,40},{56,48},{64,5... | collective-permute-start | bytes 1572872 | tf_op jit(solution)/shard_map/ppermute | solution.py:356
  30.2 15.5 %collective-permute-start = (bf16[512,512]{1,0:T(8,128)(2,1)S(1)}, bf16[512,512]{1,0:T(8,128)(2,1)S(1)}, u32[]{:S(2)}, u32[]{:S(2)}) collective-permute-start(bf16[512,512]{1,0:T(8,128)(2,1)S(1)} %reshape.107.rest_1_), channel_id=1, source_target_pairs={{0,8},{8,16},{16,24},{24,32},{32,40},{40,48},{48,56},{56,64},{64,7... | collective-permute-start | bytes 1572872 | tf_op jit(solution)/shard_map/ppermute | solution.py:356
  32.6 18.0 %copy-start.11 = (bf16[2,32,256]{2,1,0:T(8,128)(2,1)S(1)}, bf16[2,32,256]{2,1,0:T(8,128)(2,1)}, u32[]{:S(2)}) copy-start(bf16[2,32,256]{2,1,0:T(8,128)(2,1)} %param.23) | copy-start | bytes 98308
  45.8 15.6 %collective-permute-start.2 = (bf16[512,512]{1,0:T(8,128)(2,1)S(1)}, bf16[512,512]{1,0:T(8,128)(2,1)S(1)}, u32[]{:S(2)}, u32[]{:S(2)}) collective-permute-start(bf16[512,512]{1,0:T(8,128)(2,1)S(1)} %collective-permute-done.rest_1_), channel_id=1, source_target_pairs={{0,8},{8,16},{16,24},{24,32},{32,40},{40,48},{48,56},{56,64},{64,7... | collective-permute-start | bytes 1572872 | tf_op jit(solution)/shard_map/ppermute | solution.py:356
  45.8 15.5 %collective-permute-start.3 = (bf16[512,512]{1,0:T(8,128)(2,1)S(1)}, bf16[512,512]{1,0:T(8,128)(2,1)S(1)}, u32[]{:S(2)}, u32[]{:S(2)}) collective-permute-start(bf16[512,512]{1,0:T(8,128)(2,1)S(1)} %collective-permute-done.1.rest_2_), channel_id=1, source_target_pairs={{0,120},{8,0},{16,8},{24,16},{32,24},{40,32},{48,40},{56,48},{64,5... | collective-permute-start | bytes 1572872 | tf_op jit(solution)/shard_map/ppermute | solution.py:356
  62.5 18.7 %all-to-all-start.1 = ((bf16[16,64,512]{2,1,0:T(8,128)(2,1)}), bf16[16,64,512]{2,1,0:T(8,128)(2,1)S(1)}, u32[]{:S(2)}, u32[]{:S(2)}) async-start(bf16[16,64,512]{2,1,0:T(8,128)(2,1)} %tile.8), calls=%async_computation.1 | async-start | bytes 2097152 | tf_op jit(solution)/shard_map/all_to_all | solution.py:445
  72.2 19.6 %copy-start.2 = (s32[1,64]{1,0:T(1,128)S(1)}, s32[1,64]{1,0:T(1,128)}, u32[]{:S(2)}) copy-start(s32[1,64]{1,0:T(1,128)} %param.19) | copy-start | bytes 772
  81.2 6.6 %collective-permute-start.4 = (bf16[2,256,512]{2,1,0:T(8,128)(2,1)}, bf16[2,256,512]{2,1,0:T(8,128)(2,1)S(1)}, u32[]{:S(2)}, u32[]{:S(2)}) collective-permute-start(bf16[2,256,512]{2,1,0:T(8,128)(2,1)} %get-tuple-element.66), channel_id=1, source_target_pairs={{0,1},{1,0},{2,3},{3,2},{4,5},{5,4},{6,7},{7,6},{8,9},{9,8},{10,11... | collective-permute-start | bytes 1572872 | tf_op jit(solution)/shard_map/ppermute | solution.py:359
  88.9 9.8 %collective-permute-start.5 = (bf16[256,512]{1,0:T(8,128)(2,1)S(1)}, bf16[256,512]{1,0:T(8,128)(2,1)S(1)}, u32[]{:S(2)}, u32[]{:S(2)}) collective-permute-start(bf16[256,512]{1,0:T(8,128)(2,1)S(1)} %get-tuple-element.74), channel_id=1, source_target_pairs={{0,2},{1,3},{2,4},{3,5},{4,6},{5,7},{6,0},{7,1},{8,10},{9,11},{10,... | collective-permute-start | bytes 786440 | tf_op jit(solution)/shard_map/ppermute | solution.py:362
  90.6 8.2 %collective-permute-start.6 = (bf16[256,512]{1,0:T(8,128)(2,1)S(1)}, bf16[256,512]{1,0:T(8,128)(2,1)S(1)}, u32[]{:S(2)}, u32[]{:S(2)}) collective-permute-start(bf16[256,512]{1,0:T(8,128)(2,1)S(1)} %get-tuple-element.75), channel_id=1, source_target_pairs={{0,6},{1,7},{2,0},{3,1},{4,2},{5,3},{6,4},{7,5},{8,14},{9,15},{10,... | collective-permute-start | bytes 786440 | tf_op jit(solution)/shard_map/ppermute | solution.py:362
  98.7 0.7 copy-start.7
  99.4 5.6 %copy-start.9 = (bf16[256,512]{1,0:T(8,128)(2,1)}, bf16[256,512]{1,0:T(8,128)(2,1)S(1)}, u32[]{:S(2)}) copy-start(bf16[256,512]{1,0:T(8,128)(2,1)S(1)} %collective-permute-done.6) | copy-start | bytes 786436
  99.4 3.8 %collective-permute-start.7 = (bf16[5,256,512]{2,1,0:T(8,128)(2,1)}, bf16[5,256,512]{2,1,0:T(8,128)(2,1)S(1)}, u32[]{:S(2)}, u32[]{:S(2)}) collective-permute-start(bf16[5,256,512]{2,1,0:T(8,128)(2,1)} %get-tuple-element.76), channel_id=1, source_target_pairs={{0,1},{1,0},{2,3},{3,2},{4,5},{5,4},{6,7},{7,6},{8,9},{9,8},{10,11... | collective-permute-start | bytes 3932168 | tf_op jit(solution)/shard_map/ppermute | solution.py:359
  103.2 1.8 %copy-start.3 = (bf16[5,256,512]{2,1,0:T(8,128)(2,1)}, bf16[5,256,512]{2,1,0:T(8,128)(2,1)S(1)}, u32[]{:S(2)}) copy-start(bf16[5,256,512]{2,1,0:T(8,128)(2,1)S(1)} %collective-permute-done.7) | copy-start | bytes 3932164
  105.2 7.3 %copy-start.4 = (bf16[2,256,512]{2,1,0:T(8,128)(2,1)S(1)}, bf16[2,256,512]{2,1,0:T(8,128)(2,1)}, u32[]{:S(2)}) copy-start(bf16[2,256,512]{2,1,0:T(8,128)(2,1)} %get-tuple-element.72) | copy-start | bytes 1572868
  105.2 7.3 %copy-start.5 = (bf16[2,256,512]{2,1,0:T(8,128)(2,1)S(1)}, bf16[2,256,512]{2,1,0:T(8,128)(2,1)}, u32[]{:S(2)}) copy-start(bf16[2,256,512]{2,1,0:T(8,128)(2,1)} %get-tuple-element.78) | copy-start | bytes 1572868
  105.2 7.3 %copy-start.8 = (bf16[256,512]{1,0:T(8,128)(2,1)S(1)}, bf16[256,512]{1,0:T(8,128)(2,1)}, u32[]{:S(2)}) copy-start(bf16[256,512]{1,0:T(8,128)(2,1)} %copy-done.7) | copy-start | bytes 786436
  105.2 7.3 %copy-start.10 = (bf16[256,512]{1,0:T(8,128)(2,1)S(1)}, bf16[256,512]{1,0:T(8,128)(2,1)}, u32[]{:S(2)}) copy-start(bf16[256,512]{1,0:T(8,128)(2,1)} %copy-done.9) | copy-start | bytes 786436
  105.2 10.9 %collective-permute-start.8 = (bf16[352,512]{1,0:T(8,128)(2,1)S(1)}, bf16[352,512]{1,0:T(8,128)(2,1)S(1)}, u32[]{:S(2)}, u32[]{:S(2)}) collective-permute-start(bf16[352,512]{1,0:T(8,128)(2,1)S(1)} %pad_maximum_fusion), channel_id=1, source_target_pairs={{0,2},{1,3},{2,4},{3,5},{4,6},{5,7},{6,0},{7,1},{8,10},{9,11},{10,... | collective-permute-start | bytes 1081352 | tf_op jit(solution)/shard_map/ppermute | solution.py:362
  105.6 10.5 %collective-permute-start.9 = (bf16[352,512]{1,0:T(8,128)(2,1)S(1)}, bf16[352,512]{1,0:T(8,128)(2,1)S(1)}, u32[]{:S(2)}, u32[]{:S(2)}) collective-permute-start(bf16[352,512]{1,0:T(8,128)(2,1)S(1)} %pad_maximum_fusion.1), channel_id=1, source_target_pairs={{0,6},{1,7},{2,0},{3,1},{4,2},{5,3},{6,4},{7,5},{8,14},{9,15},{10,... | collective-permute-start | bytes 1081352 | tf_op jit(solution)/shard_map/ppermute | solution.py:362
  112.5 18.8 %copy-start.1 = (bf16[2,256,512]{2,1,0:T(8,128)(2,1)S(1)}, bf16[2,256,512]{2,1,0:T(8,128)(2,1)}, u32[]{:S(2)}) copy-start(bf16[2,256,512]{2,1,0:T(8,128)(2,1)} %get-tuple-element.80.kept_ref) | copy-start | bytes 1572868
  116.1 15.1 %collective-permute-start.10 = (bf16[2,256,512]{2,1,0:T(8,128)(2,1)}, bf16[2,256,512]{2,1,0:T(8,128)(2,1)S(1)}, u32[]{:S(2)}, u32[]{:S(2)}) collective-permute-start(bf16[2,256,512]{2,1,0:T(8,128)(2,1)} %get-tuple-element.84), channel_id=1, source_target_pairs={{0,1},{1,0},{2,3},{3,2},{4,5},{5,4},{6,7},{7,6},{8,9},{9,8},{10,11... | collective-permute-start | bytes 1572872 | tf_op jit(solution)/shard_map/ppermute | solution.py:359
  118.1 9.4 %collective-permute-start.12 = (bf16[288,512]{1,0:T(8,128)(2,1)}, bf16[288,512]{1,0:T(8,128)(2,1)S(1)}, u32[]{:S(2)}, u32[]{:S(2)}) collective-permute-start(bf16[288,512]{1,0:T(8,128)(2,1)} %pad_maximum_fusion.3), channel_id=1, source_target_pairs={{0,6},{1,7},{2,0},{3,1},{4,2},{5,3},{6,4},{7,5},{8,14},{9,15},{10,... | collective-permute-start | bytes 884744 | tf_op jit(solution)/shard_map/ppermute | solution.py:362
  121.5 9.7 %collective-permute-start.11 = (bf16[288,512]{1,0:T(8,128)(2,1)}, bf16[288,512]{1,0:T(8,128)(2,1)S(1)}, u32[]{:S(2)}, u32[]{:S(2)}) collective-permute-start(bf16[288,512]{1,0:T(8,128)(2,1)} %pad_maximum_fusion.2), channel_id=1, source_target_pairs={{0,2},{1,3},{2,4},{3,5},{4,6},{5,7},{6,0},{7,1},{8,10},{9,11},{10,... | collective-permute-start | bytes 884744 | tf_op jit(solution)/shard_map/ppermute | solution.py:362

commit v4 on v3

--- a/solution.py
+++ b/solution.py
@@ -6,6 +6,7 @@
 from jax.sharding import PartitionSpec as P
 
 reach = 2
+across = 4
 
 
 def in_hbm(*values):
@@ -355,6 +356,13 @@
     def row_shift(value, step):
         return lax.ppermute(value, "row", [(i, (i + step) % row_count) for i in range(row_count)])
 
+    def line_shift(value, step):
+        return lax.ppermute(
+            value,
+            "row",
+            [(i, i // across * across + (i + step) % across) for i in range(row_count)],
+        )
+
     def other_core(value):
         return lax.ppermute(value, "col", [(i, i ^ 1) for i in range(col_count)])
 
@@ -365,6 +373,50 @@
 
     below = row_shift(slab, 1)
     above = row_shift(slab, -1)
+    slots = jnp.arange(near_rows.shape[1], dtype=jnp.int32)
+    pair = near_rows[0] * window + near_cols[0] - (row - reach) * owned
+    pair = jnp.where(slots < near_count[0], pair, -1)
+    wanted = jnp.arange(targets * window, dtype=jnp.int32)
+    place = jnp.max(jnp.where(pair[None, :] == wanted[:, None], slots[None, :], -1), axis=1)
+
+    far_slots = far_rows.shape[1]
+    far_target = jnp.where(
+        jnp.arange(far_slots, dtype=jnp.int32) < far_count[0], far_rows[0], -1
+    )
+    coupling_rows = couplings[0].transpose(1, 0, 2).reshape(rank, far_slots * rank)
+    own_basis = lax.dynamic_slice_in_dim(row_basis, col * owned, owned, 0)
+    own_basis = jnp.tile(own_basis.transpose(0, 2, 1), (1, 1, 3))
+    far_row = far_cols[0] // owned
+    far_line = (far_row // across - row // across) % (row_count // across)
+    far_place = (far_row - row) % across
+    far_source = (far_line * across + far_place) * owned + far_cols[0] % owned
+
+    chips = col_count // 2
+    chip, core = col // 2, col % 2
+    each = jnp.arange(owned, dtype=jnp.int32)
+
+    def clusters(chip_step, which):
+        return (((chip + chip_step) % chips) * 2 + which) * owned + each
+
+    def order(*chip_steps):
+        return jnp.concatenate(
+            [clusters(step, 1 - core) for step in chip_steps]
+            + [clusters(step, core) for step in chip_steps]
+        )
+
+    far_chip = (far_target // (2 * owned) - chip) % chips
+    far_core = (far_target // owned + 1 - core) % 2
+    far_place = (far_core * chips + far_chip) * owned + far_target % owned
+    far_place = jnp.where(far_target >= 0, far_place, -1)
+    slot_rows = jnp.repeat(far_place, rank)[None, :]
+
+    blocks = near_blocks[0]
+    everyone = jnp.arange(targets, dtype=jnp.int32)
+    middle = list(range(reach * owned, (reach + 1) * owned))
+    inner = [column for column in range(owned, window - owned) if column not in middle]
+    outer = list(range(owned)) + list(range(window - owned, window))
+    (partial,) = near_terms(place, everyone, blocks, [slab], middle, [targets], window)
+    slab, partial = lax.optimization_barrier((slab, partial))
     moments = (
         jnp.einsum(
             "gkb,gbr->gkr",
@@ -375,49 +427,10 @@
         .astype(jnp.bfloat16)
         .reshape(owned * rank, excitations)
     )
-    slots = jnp.arange(near_rows.shape[1], dtype=jnp.int32)
-    pair = near_rows[0] * window + near_cols[0] - (row - reach) * owned
-    pair = jnp.where(slots < near_count[0], pair, -1)
-    wanted = jnp.arange(targets * window, dtype=jnp.int32)
-    place = jnp.max(jnp.where(pair[None, :] == wanted[:, None], slots[None, :], -1), axis=1)
-
-    far_slots = far_rows.shape[1]
-    far_target = jnp.where(
-        jnp.arange(far_slots, dtype=jnp.int32) < far_count[0], far_rows[0], -1
-    )
-    coupling_rows = couplings[0].transpose(1, 0, 2).reshape(rank, far_slots * rank)
-    own_basis = lax.dynamic_slice_in_dim(row_basis, col * owned, owned, 0)
-    own_basis = jnp.tile(own_basis.transpose(0, 2, 1), (1, 1, 3))
-    far_source = far_cols[0]
-
-    chips = col_count // 2
-    chip, core = col // 2, col % 2
-    each = jnp.arange(owned, dtype=jnp.int32)
-
-    def clusters(chip_step, which):
-        return (((chip + chip_step) % chips) * 2 + which) * owned + each
-
-    def order(*chip_steps):
-        return jnp.concatenate(
-            [clusters(step, 1 - core) for step in chip_steps]
-            + [clusters(step, core) for step in chip_steps]
-        )
-
-    far_chip = (far_target // (2 * owned) - chip) % chips
-    far_core = (far_target // owned + 1 - core) % 2
-    far_place = (far_core * chips + far_chip) * owned + far_target % owned
-    far_place = jnp.where(far_target >= 0, far_place, -1)
-    slot_rows = jnp.repeat(far_place, rank)[None, :]
-
-    blocks = near_blocks[0]
-    everyone = jnp.arange(targets, dtype=jnp.int32)
-    middle = list(range(reach * owned, (reach + 1) * owned))
-    inner = [column for column in range(owned, window - owned) if column not in middle]
-    outer = list(range(owned)) + list(range(window - owned, window))
-    (partial,) = near_terms(place, everyone, blocks, [slab], middle, [targets], window)
-    below, above, partial, coupling_rows, slot_rows, far_source, own_basis = (
+    of_line = [moments] + [line_shift(moments, -step) for step in range(1, across)]
+    below, above, partial, of_line, coupling_rows, slot_rows, far_source, own_basis = (
         lax.optimization_barrier(
-            (below, above, partial, coupling_rows, slot_rows, far_source, own_basis)
+            (below, above, partial, of_line, coupling_rows, slot_rows, far_source, own_basis)
         )
     )
     below_more = row_shift(below, 1)
@@ -439,21 +452,21 @@
             far,
         )
 
-    moments, partial, below_more, above_more = lax.optimization_barrier(
-        (moments, partial, below_more, above_more)
-    )
-    all_moments = lax.all_to_all(
-        jnp.tile(moments, (row_count, 1)), "row", split_axis=0, concat_axis=0, tiled=True
-    )
+    of_line, partial = lax.optimization_barrier((jnp.concatenate(of_line), partial))
+    next_line = row_shift(of_line, -across)
+    last_line = row_shift(of_line, across)
     sent, kept = rest(2)
-    sent, all_moments = lax.optimization_barrier((sent, all_moments))
+    sent, next_line, last_line = lax.optimization_barrier((sent, next_line, last_line))
+    half = of_line.shape[0] // 2
+    second_line = [row_shift(next_line[:half], -across), row_shift(last_line[half:], across)]
     got = other_core(sent)
     opposite = [add(kept[index], got[index]) for index in range(owned)]
-    opposite, place = lax.optimization_barrier((opposite, place))
+    opposite, place, second_line = lax.optimization_barrier((opposite, place, second_line))
     from_below = chip_shift(opposite[0], 1)
     from_above = chip_shift(opposite[1], -1)
+    moment_parts = [of_line, next_line, *second_line, last_line]
     sent, kept_up, kept_down, kept_far = rest(
-        1, -1, far=(far_source, [all_moments], coupling_rows, slot_rows)
+        1, -1, far=(far_source, moment_parts, coupling_rows, slot_rows)
     )
     sent, from_below, from_above = lax.optimization_barrier((sent, from_below, from_above))
     got = other_core(sent)

time: 133 us -> 132 us (level)
  starting transfers between devices: 38 us -> 41 us
  waiting for transfers between devices: 43.3 us -> 40.4 us
    all_to_all x1 -> x0, waiting for transfers between devices: 8.99 us -> none  [shards(): lax.all_to_all(jnp.tile(moments, (row_count, 1)), 'row', split_axis=0, co...]
    ppermute x4 -> x8, waiting for transfers between devices: 5.71 us -> 13.5 us  [row_shift(): lax.ppermute(value, 'row', [(i, (i + step) % row_count) for i in range(ro...]
    ppermute x4 -> x8, starting transfers between devices: 6.38 us -> 12.7 us  [row_shift(): lax.ppermute(value, 'row', [(i, (i + step) % row_count) for i in range(ro...]
    all_to_all x1 -> x0, starting transfers between devices: 4.95 us -> none  [shards(): lax.all_to_all(jnp.tile(moments, (row_count, 1)), 'row', split_axis=0, co...]
    ppermute x0 -> x3, starting transfers between devices: none -> 2.18 us  [line_shift(): lax.ppermute(value, 'row', [(i, i // across * across + (i + step) % acros...]
    ppermute x3, waiting for transfers between devices: 4.53 us -> 2.9 us  [other_core(): return lax.ppermute(value, 'col', [(i, i ^ 1) for i in range(col_count)])]
  transfers between devices with their start and end apart: 15 -> 21, of which waited for: 9 -> 10; matrix products, arithmetic and copies ran while one was open for 4% -> 4% of each run, Pallas kernels for 26% -> 20%
where the time goes in v4:
time: 132 us
  starting transfers between devices  41 us (31%)
  waiting for transfers between devices  40.4 us (31%)
  Pallas kernels  35.5 us (27%)
  local copies, waits for them, and re-layouts  6.62 us (5%)
  other arithmetic  6.32 us (5%)
  between operations  1.76 us (1%)
    pallas_call x5, Pallas kernels, near_terms(): pl.pallas_call(kernel, grid_spec=pltpu.PrefetchScalarGridSpec(num_scalar_...  34.2 us
    ppermute x8, waiting for transfers between devices, row_shift(): lax.ppermute(value, 'row', [(i, (i + step) % row_count) for i in range(ro...  13.5 us
    ppermute x8, starting transfers between devices, row_shift(): lax.ppermute(value, 'row', [(i, (i + step) % row_count) for i in range(ro...  12.7 us
    all_to_all x1, waiting for transfers between devices, shards(): lax.all_to_all(outgoing.reshape(device_count, segment, excitations), ('ro...  12.2 us
    ppermute x6, waiting for transfers between devices, chip_shift(): lax.ppermute(value, 'col', [(i, (i + 2 * step) % col_count) for i in rang...  11.8 us
    all_to_all x1, starting transfers between devices, shards(): lax.all_to_all(outgoing.reshape(device_count, segment, excitations), ('ro...  11.5 us
    ppermute x6, starting transfers between devices, chip_shift(): lax.ppermute(value, 'col', [(i, (i + 2 * step) % col_count) for i in rang...  8.16 us
    ppermute x3, starting transfers between devices, other_core(): return lax.ppermute(value, 'col', [(i, i ^ 1) for i in range(col_count)])  6.45 us
  transfers between devices with their start and end apart: 21, of which 10 were waited for; matrix products, arithmetic and copies ran while one was open for 4% of the time, Pallas kernels for 20%

profile of v4, /device:TPU:1, one launch (start us, length us, event | category | flops | bytes accessed | tf_op | source)
XLA Modules:
  0.0 131.8 jit_solution(8300358787865043090)
XLA Ops:
  0.0 0.7 compare_select_fusion
  0.8 0.3 copy-done
  1.1 2.0 %gather_fusion = bf16[512,512]{1,0:T(8,128)(2,1)S(1)} fusion(bf16[512,512]{1,0:T(8,128)(2,1)S(1)} %copy-done, s32[1024]{0:T(1024)S(1)} %pad_clamp_fusion), kind=kCustom, calls=%fused_computation | custom fusion | bytes 1050624 | tf_op jit(solution)/shard_map/gather | solution.py:324
  3.0 0.9 reshape.99
  4.0 11.5 %all-to-all-start = ((bf16[128,4,512]{2,1,0:T(4,128)(2,1)}), bf16[128,4,512]{2,1,0:T(4,128)(2,1)S(1)}, u32[]{:S(2)}, u32[]{:S(2)}) async-start(bf16[128,4,512]{2,1,0:T(4,128)(2,1)} %reshape.99), calls=%async_computation | async-start | bytes 1048576 | tf_op jit(solution)/shard_map/all_to_all | solution.py:325
  16.8 12.2 %all-to-all-done = bf16[128,4,512]{2,1,0:T(4,128)(2,1)S(1)} async-done(((bf16[128,4,512]{2,1,0:T(4,128)(2,1)}), bf16[128,4,512]{2,1,0:T(4,128)(2,1)S(1)}, u32[]{:S(2)}, u32[]{:S(2)}) %all-to-all-start) | async-done | bytes 524320 | tf_op jit(solution)/shard_map/all_to_all | solution.py:325
  29.0 0.1 reshape.100.rest_1_
  29.1 0.1 select_reduce_fusion.place_ref
  29.3 0.0 copy-start.9
  29.3 0.0 copy-start.12
  29.3 0.0 copy-start.6
  29.3 7.5 %near_first.1.rest_3_ = bf16[16,256,512]{2,1,0:T(8,128)(2,1)} custom-call(s32[160]{0:T(256)S(1)} %select_reduce_fusion.place_ref, s32[16]{0:T(128)S(1)} %iota.39.target_ref, bf16[160,256,256]{2,1,0:T(8,128)(2,1)} %bitcast.67, bf16[512,512]{1,0:T(8,128)(2,1)S(1)} %reshape.100.rest_1_), custom_call_target="tpu_custom_call" | custom-call | flops 2147483648 | bytes 4718592 | tf_op jit(solution)/shard_map/near_first/pallas_call | solution.py:212
  36.8 0.0 copy-start.13
  36.8 0.2 convolution_convert_fusion
  37.0 1.0 collective-permute-start.2
  38.0 1.1 collective-permute-start.3
  39.1 0.1 collective-permute-start.4
  39.1 1.5 %collective-permute-start = (bf16[512,512]{1,0:T(8,128)(2,1)S(1)}, bf16[512,512]{1,0:T(8,128)(2,1)S(1)}, u32[]{:S(2)}, u32[]{:S(2)}) collective-permute-start(bf16[512,512]{1,0:T(8,128)(2,1)S(1)} %reshape.100.rest_1_), channel_id=1, source_target_pairs={{0,8},{8,16},{16,24},{24,32},{32,40},{40,48},{48,56},{56,64},{64,7... | collective-permute-start | bytes 1572872 | tf_op jit(solution)/shard_map/ppermute | solution.py:357
  40.6 3.3 %collective-permute-start.1 = (bf16[512,512]{1,0:T(8,128)(2,1)S(1)}, bf16[512,512]{1,0:T(8,128)(2,1)S(1)}, u32[]{:S(2)}, u32[]{:S(2)}) collective-permute-start(bf16[512,512]{1,0:T(8,128)(2,1)S(1)} %reshape.100.rest_1_), channel_id=1, source_target_pairs={{0,120},{8,0},{16,8},{24,16},{32,24},{40,32},{48,40},{56,48},{64,5... | collective-permute-start | bytes 1572872 | tf_op jit(solution)/shard_map/ppermute | solution.py:357
  44.0 0.1 broadcast_in_dim.32
  44.0 0.1 broadcast_in_dim_reshape.3.rest_11_
  44.1 0.3 copy.17
  44.4 0.5 reshape.103.rest_10_
  45.0 0.8 dynamic-slice_bitcast_fusion
  45.8 0.0 collective-permute-done.2
  45.8 0.0 collective-permute-done.4
  45.8 10.0 %collective-permute-done.rest_1_ = bf16[512,512]{1,0:T(8,128)(2,1)S(1)} collective-permute-done((bf16[512,512]{1,0:T(8,128)(2,1)S(1)}, bf16[512,512]{1,0:T(8,128)(2,1)S(1)}, u32[]{:S(2)}, u32[]{:S(2)}) %collective-permute-start) | collective-permute-done | bytes 524320 | tf_op jit(solution)/shard_map/ppermute | solution.py:357
  55.8 0.0 collective-permute-done.1.rest_2_
  55.8 0.6 tile.4
  56.4 4.8 %collective-permute-start.6 = (bf16[512,512]{1,0:T(8,128)(2,1)S(1)}, bf16[512,512]{1,0:T(8,128)(2,1)S(1)}, u32[]{:S(2)}, u32[]{:S(2)}) collective-permute-start(bf16[512,512]{1,0:T(8,128)(2,1)S(1)} %collective-permute-done.1.rest_2_), channel_id=1, source_target_pairs={{0,120},{8,0},{16,8},{24,16},{32,24},{40,32},{48,40},{56,48},{64,5... | collective-permute-start | bytes 1572872 | tf_op jit(solution)/shard_map/ppermute | solution.py:357
  61.2 10.2 %near_rest.4.rest_3_.rest_4_ = bf16[16,256,512]{2,1,0:T(8,128)(2,1)} custom-call(s32[160]{0:T(256)S(1)} %select_reduce_fusion.place_ref, s32[16]{0:T(128)S(1)} %iota.41.target_ref, bf16[160,256,256]{2,1,0:T(8,128)(2,1)} %bitcast.68, bf16[512,512]{1,0:T(8,128)(2,1)S(1)} %collective-permute-done.rest_1_, bf16[512,512]{1,0:T(8,128)(2,1)S(1)} %collective-permute-done.1.rest_2_, ...), custom_call_target="tpu_custom_call" | custom-call | flops 4294967296 | bytes 9437184 | tf_op jit(solution)/shard_map/near_rest/pallas_call | solution.py:212
  71.4 0.1 collective-permute-start.7
  71.5 1.5 %collective-permute-start.8 = (bf16[256,512]{1,0:T(8,128)(2,1)S(1)}, bf16[256,512]{1,0:T(8,128)(2,1)S(1)}, u32[]{:S(2)}, u32[]{:S(2)}) collective-permute-start(bf16[256,512]{1,0:T(8,128)(2,1)S(1)} %pad_maximum_fusion.4.rest_5_), channel_id=1, source_target_pairs={{0,32},{8,40},{16,48},{24,56},{32,64},{40,72},{48,80},{56,88},{64,... | collective-permute-start | bytes 786440 | tf_op jit(solution)/shard_map/ppermute | solution.py:357
  72.9 0.1 pad_add_fusion.target_ref
  73.0 4.8 %near_rest.5 = (bf16[2,256,512]{2,1,0:T(8,128)(2,1)}, bf16[2,256,512]{2,1,0:T(8,128)(2,1)}) custom-call(s32[160]{0:T(256)S(1)} %select_reduce_fusion.place_ref, s32[4]{0:T(128)S(1)} %pad_add_fusion.target_ref, bf16[160,256,256]{2,1,0:T(8,128)(2,1)} %bitcast.69, bf16[512,512]{1,0:T(8,128)(2,1)S(1)} %collective-permute-done.5.rest_1_.rest_2_, ...), custom_call_target="tpu_custom_call" | custom-call | flops 1073741824 | bytes 3145728 | tf_op jit(solution)/shard_map/near_rest/pallas_call | solution.py:212
  77.8 0.2 collective-permute-done.8.rest_9_
  78.0 3.7 %collective-permute-start.9 = (bf16[2,256,512]{2,1,0:T(8,128)(2,1)}, bf16[2,256,512]{2,1,0:T(8,128)(2,1)S(1)}, u32[]{:S(2)}, u32[]{:S(2)}) collective-permute-start(bf16[2,256,512]{2,1,0:T(8,128)(2,1)} %get-tuple-element.77), channel_id=1, source_target_pairs={{0,1},{1,0},{2,3},{3,2},{4,5},{5,4},{6,7},{7,6},{8,9},{9,8},{10,11... | collective-permute-start | bytes 1572872 | tf_op jit(solution)/shard_map/ppermute | solution.py:367
  81.7 0.1 collective-permute-start.10
  81.8 1.5 %collective-permute-start.11 = (bf16[128,512]{1,0:T(8,128)(2,1)S(1)}, bf16[128,512]{1,0:T(8,128)(2,1)S(1)}, u32[]{:S(2)}, u32[]{:S(2)}) collective-permute-start(bf16[128,512]{1,0:T(8,128)(2,1)S(1)} %slice.83), channel_id=1, source_target_pairs={{0,32},{8,40},{16,48},{24,56},{32,64},{40,72},{48,80},{56,88},{64,... | collective-permute-start | bytes 393224 | tf_op jit(solution)/shard_map/ppermute | solution.py:357
  83.3 0.1 collective-permute-done.9
  83.4 1.2 fusion.3
  84.6 2.3 %collective-permute-done.10.rest_7_ = bf16[128,512]{1,0:T(8,128)(2,1)S(1)} collective-permute-done((bf16[128,512]{1,0:T(8,128)(2,1)S(1)}, bf16[128,512]{1,0:T(8,128)(2,1)S(1)}, u32[]{:S(2)}, u32[]{:S(2)}) %collective-permute-start.10) | collective-permute-done | bytes 131104 | tf_op jit(solution)/shard_map/ppermute | solution.py:357
  86.9 1.1 collective-permute-done.11.rest_8_
  88.0 0.1 collective-permute-start.12
  88.0 2.6 %collective-permute-start.13 = (bf16[256,512]{1,0:T(8,128)(2,1)S(1)}, bf16[256,512]{1,0:T(8,128)(2,1)S(1)}, u32[]{:S(2)}, u32[]{:S(2)}) collective-permute-start(bf16[256,512]{1,0:T(8,128)(2,1)S(1)} %get-tuple-element.89), channel_id=1, source_target_pairs={{0,6},{1,7},{2,0},{3,1},{4,2},{5,3},{6,4},{7,5},{8,14},{9,15},{10,... | collective-permute-start | bytes 786440 | tf_op jit(solution)/shard_map/ppermute | solution.py:370
  90.6 0.1 pad_add_fusion.1.target_ref
  90.7 7.3 %near_rest.6 = (bf16[5,256,512]{2,1,0:T(8,128)(2,1)}, bf16[2,256,512]{2,1,0:T(8,128)(2,1)}, bf16[2,256,512]{2,1,0:T(8,128)(2,1)}, bf16[1,256,512]{2,1,0:T(8,128)(2,1)}) custom-call(s32[160]{0:T(256)S(1)} %select_reduce_fusion.place_ref, s32[8]{0:T(128)S(1)} %pad_add_fusion.1.target_ref, s32[64]{0:T(128)S(1)} %fusion.9.rest_0_, ...), custom_call_target="tpu_custom_call" | custom-call | flops 2147483648 | bytes 5242880 | tf_op jit(solution)/shard_map/near_rest/pallas_call | solution.py:212
  98.1 0.7 copy-done.7
  98.7 1.6 %collective-permute-start.14 = (bf16[5,256,512]{2,1,0:T(8,128)(2,1)}, bf16[5,256,512]{2,1,0:T(8,128)(2,1)S(1)}, u32[]{:S(2)}, u32[]{:S(2)}) collective-permute-start(bf16[5,256,512]{2,1,0:T(8,128)(2,1)} %get-tuple-element.90), channel_id=1, source_target_pairs={{0,1},{1,0},{2,3},{3,2},{4,5},{5,4},{6,7},{7,6},{8,9},{9,8},{10,11... | collective-permute-start | bytes 3932168 | tf_op jit(solution)/shard_map/ppermute | solution.py:367
  100.3 0.1 pad_add_fusion.2.target_ref
  100.4 2.8 %collective-permute-done.14 = bf16[5,256,512]{2,1,0:T(8,128)(2,1)S(1)} collective-permute-done((bf16[5,256,512]{2,1,0:T(8,128)(2,1)}, bf16[5,256,512]{2,1,0:T(8,128)(2,1)S(1)}, u32[]{:S(2)}, u32[]{:S(2)}) %collective-permute-start.14) | collective-permute-done | bytes 1310752 | tf_op jit(solution)/shard_map/ppermute | solution.py:367
  103.2 1.8 %fusion.5 = (bf16[256,512]{1,0:T(8,128)(2,1)S(1)}, bf16[1,256,512]{2,1,0:T(8,128)(2,1)S(1)}, bf16[256,512]{1,0:T(8,128)(2,1)S(1)}) fusion(bf16[5,256,512]{2,1,0:T(8,128)(2,1)S(1)} %collective-permute-done.14, bf16[2,256,512]{2,1,0:T(8,128)(2,1)} %get-tuple-element.92, bf16[1,256,512]{2,1,0:T(8,128)(2,1)} %get-tuple-element.91, ...), kind=kLoop, calls=%fused_computation.18 | loop fusion | flops 1572864 | bytes 2359296 | tf_op jit(solution)/shard_map/convert_element_type | solution.py:296
  105.2 0.1 collective-permute-start.15
  105.3 2.7 %collective-permute-start.16 = (bf16[352,512]{1,0:T(8,128)(2,1)S(1)}, bf16[352,512]{1,0:T(8,128)(2,1)S(1)}, u32[]{:S(2)}, u32[]{:S(2)}) collective-permute-start(bf16[352,512]{1,0:T(8,128)(2,1)S(1)} %pad_maximum_fusion.1), channel_id=1, source_target_pairs={{0,6},{1,7},{2,0},{3,1},{4,2},{5,3},{6,4},{7,5},{8,14},{9,15},{10,... | collective-permute-start | bytes 1081352 | tf_op jit(solution)/shard_map/ppermute | solution.py:370
  107.9 4.5 %near_rest.7 = (bf16[2,256,512]{2,1,0:T(8,128)(2,1)}, bf16[2,256,512]{2,1,0:T(8,128)(2,1)}) custom-call(s32[160]{0:T(256)S(1)} %select_reduce_fusion.place_ref, s32[4]{0:T(128)S(1)} %pad_add_fusion.2.target_ref, bf16[160,256,256]{2,1,0:T(8,128)(2,1)} %bitcast.71, bf16[512,512]{1,0:T(8,128)(2,1)S(1)} %collective-permute-done.5.rest_1_.rest_2_, ...), custom_call_target="tpu_custom_call" | custom-call | flops 1073741824 | bytes 3145728 | tf_op jit(solution)/shard_map/near_rest/pallas_call | solution.py:212
  112.5 1.3 %fusion = (bf16[256,512]{1,0:T(8,128)(2,1)S(1)}, bf16[256,512]{1,0:T(8,128)(2,1)S(1)}) fusion(bf16[256,512]{1,0:T(8,128)(2,1)S(1)} %copy-done.8, bf16[5,256,512]{2,1,0:T(8,128)(2,1)} %copy-done.2, bf16[2,256,512]{2,1,0:T(8,128)(2,1)S(1)} %copy-done.4, bf16[256,512]{1,0:T(8,128)(2,1)S(1)} %collective-permute-done.12, bf16[2,256,512]{2,1,0:T(8,128)(2,1)S(1)} %copy-done.3), kind=kLoop, calls=%fused_computation.3 | loop fusion | flops 1572864 | bytes 2097152 | tf_op jit(solution)/shard_map/convert_element_type | solution.py:296
  113.9 2.2 %collective-permute-done.15.below_early = bf16[352,512]{1,0:T(8,128)(2,1)S(1)} collective-permute-done((bf16[352,512]{1,0:T(8,128)(2,1)S(1)}, bf16[352,512]{1,0:T(8,128)(2,1)S(1)}, u32[]{:S(2)}, u32[]{:S(2)}) %collective-permute-start.15) | collective-permute-done | bytes 360480 | tf_op jit(solution)/shard_map/ppermute | solution.py:370
  116.1 1.2 collective-permute-start.17
  117.3 2.7 %collective-permute-start.19 = (bf16[288,512]{1,0:T(8,128)(2,1)S(1)}, bf16[288,512]{1,0:T(8,128)(2,1)S(1)}, u32[]{:S(2)}, u32[]{:S(2)}) collective-permute-start(bf16[288,512]{1,0:T(8,128)(2,1)S(1)} %pad_maximum_fusion.3), channel_id=1, source_target_pairs={{0,6},{1,7},{2,0},{3,1},{4,2},{5,3},{6,4},{7,5},{8,14},{9,15},{10,... | collective-permute-start | bytes 884744 | tf_op jit(solution)/shard_map/ppermute | solution.py:370
  120.1 0.7 pad_maximum_fusion.2
  120.8 0.1 copy.18.basis_ref
  120.9 5.6 %collective-permute-done.19.above_late = bf16[288,512]{1,0:T(8,128)(2,1)S(1)} collective-permute-done((bf16[288,512]{1,0:T(8,128)(2,1)S(1)}, bf16[288,512]{1,0:T(8,128)(2,1)S(1)}, u32[]{:S(2)}, u32[]{:S(2)}) %collective-permute-start.19) | collective-permute-done | bytes 294944 | tf_op jit(solution)/shard_map/ppermute | solution.py:370
  126.5 4.0 %collective-permute-done.18.below_late = bf16[288,512]{1,0:T(8,128)(2,1)S(1)} collective-permute-done((bf16[288,512]{1,0:T(8,128)(2,1)}, bf16[288,512]{1,0:T(8,128)(2,1)S(1)}, u32[]{:S(2)}, u32[]{:S(2)}) %collective-permute-start.18) | collective-permute-done | bytes 294944 | tf_op jit(solution)/shard_map/ppermute | solution.py:370
  130.5 1.3 finish.1
  (52 shorter events, 0.3 us)
Async XLA Ops:
  0.0 1.1 copy-start
  3.9 25.1 %copy-start.10 = (s32[1,160]{1,0:T(1,128)S(1)}, s32[1,160]{1,0:T(1,128)}, u32[]{:S(2)}) copy-start(s32[1,160]{1,0:T(1,128)} %param.15) | copy-start | bytes 1924
  4.0 25.2 %copy-start.11 = (s32[1,160]{1,0:T(1,128)S(1)}, s32[1,160]{1,0:T(1,128)}, u32[]{:S(2)}) copy-start(s32[1,160]{1,0:T(1,128)} %param.14) | copy-start | bytes 1924
  4.0 25.0 %all-to-all-start = ((bf16[128,4,512]{2,1,0:T(4,128)(2,1)}), bf16[128,4,512]{2,1,0:T(4,128)(2,1)S(1)}, u32[]{:S(2)}, u32[]{:S(2)}) async-start(bf16[128,4,512]{2,1,0:T(4,128)(2,1)} %reshape.99), calls=%async_computation | async-start | bytes 1048576 | tf_op jit(solution)/shard_map/all_to_all | solution.py:325
  29.3 7.5 %copy-start.9 = (bf16[2,32,256]{2,1,0:T(8,128)(2,1)S(1)}, bf16[2,32,256]{2,1,0:T(8,128)(2,1)}, u32[]{:S(2)}) copy-start(bf16[2,32,256]{2,1,0:T(8,128)(2,1)} %param.23) | copy-start | bytes 98308
  29.3 14.7 %copy-start.12 = (s32[1,64]{1,0:T(1,128)S(1)}, s32[1,64]{1,0:T(1,128)}, u32[]{:S(2)}) copy-start(s32[1,64]{1,0:T(1,128)} %param.18) | copy-start | bytes 772
  29.3 14.8 %copy-start.6 = (bf16[1,64,32,32]{1,3,2,0:T(8,128)(2,1)S(1)}, bf16[1,64,32,32]{1,3,2,0:T(8,128)(2,1)}, u32[]{:S(2)}) copy-start(bf16[1,64,32,32]{1,3,2,0:T(8,128)(2,1)} %param.21) | copy-start | bytes 393220
  36.8 8.2 %copy-start.13 = (s32[1,64]{1,0:T(1,128)S(1)}, s32[1,64]{1,0:T(1,128)}, u32[]{:S(2)}) copy-start(s32[1,64]{1,0:T(1,128)} %param.19) | copy-start | bytes 772
  37.0 8.8 %collective-permute-start.2 = (bf16[64,512]{1,0:T(8,128)(2,1)S(1)}, bf16[64,512]{1,0:T(8,128)(2,1)S(1)}, u32[]{:S(2)}, u32[]{:S(2)}) collective-permute-start(bf16[64,512]{1,0:T(8,128)(2,1)S(1)} %bitcast.75), channel_id=1, source_target_pairs={{0,24},{8,0},{16,8},{24,16},{32,56},{40,32},{48,40},{56,48},{64,88... | collective-permute-start | bytes 196616 | tf_op jit(solution)/shard_map/ppermute | solution.py:360
  38.0 7.8 %collective-permute-start.3 = (bf16[64,512]{1,0:T(8,128)(2,1)S(1)}, bf16[64,512]{1,0:T(8,128)(2,1)S(1)}, u32[]{:S(2)}, u32[]{:S(2)}) collective-permute-start(bf16[64,512]{1,0:T(8,128)(2,1)S(1)} %bitcast.76), channel_id=1, source_target_pairs={{0,16},{8,24},{16,0},{24,8},{32,48},{40,56},{48,32},{56,40},{64,80... | collective-permute-start | bytes 196616 | tf_op jit(solution)/shard_map/ppermute | solution.py:360
  39.1 6.7 %collective-permute-start.4 = (bf16[64,512]{1,0:T(8,128)(2,1)S(1)}, bf16[64,512]{1,0:T(8,128)(2,1)S(1)}, u32[]{:S(2)}, u32[]{:S(2)}) collective-permute-start(bf16[64,512]{1,0:T(8,128)(2,1)S(1)} %bitcast.77), channel_id=1, source_target_pairs={{0,8},{8,16},{16,24},{24,0},{32,40},{40,48},{48,56},{56,32},{64,72... | collective-permute-start | bytes 196616 | tf_op jit(solution)/shard_map/ppermute | solution.py:360
  39.1 16.6 %collective-permute-start = (bf16[512,512]{1,0:T(8,128)(2,1)S(1)}, bf16[512,512]{1,0:T(8,128)(2,1)S(1)}, u32[]{:S(2)}, u32[]{:S(2)}) collective-permute-start(bf16[512,512]{1,0:T(8,128)(2,1)S(1)} %reshape.100.rest_1_), channel_id=1, source_target_pairs={{0,8},{8,16},{16,24},{24,32},{32,40},{40,48},{48,56},{56,64},{64,7... | collective-permute-start | bytes 1572872 | tf_op jit(solution)/shard_map/ppermute | solution.py:357
  40.6 15.1 %collective-permute-start.1 = (bf16[512,512]{1,0:T(8,128)(2,1)S(1)}, bf16[512,512]{1,0:T(8,128)(2,1)S(1)}, u32[]{:S(2)}, u32[]{:S(2)}) collective-permute-start(bf16[512,512]{1,0:T(8,128)(2,1)S(1)} %reshape.100.rest_1_), channel_id=1, source_target_pairs={{0,120},{8,0},{16,8},{24,16},{32,24},{40,32},{48,40},{56,48},{64,5... | collective-permute-start | bytes 1572872 | tf_op jit(solution)/shard_map/ppermute | solution.py:357
  56.4 16.6 %collective-permute-start.5 = (bf16[512,512]{1,0:T(8,128)(2,1)S(1)}, bf16[512,512]{1,0:T(8,128)(2,1)S(1)}, u32[]{:S(2)}, u32[]{:S(2)}) collective-permute-start(bf16[512,512]{1,0:T(8,128)(2,1)S(1)} %collective-permute-done.rest_1_), channel_id=1, source_target_pairs={{0,8},{8,16},{16,24},{24,32},{32,40},{40,48},{48,56},{56,64},{64,7... | collective-permute-start | bytes 1572872 | tf_op jit(solution)/shard_map/ppermute | solution.py:357
  56.4 16.6 %collective-permute-start.6 = (bf16[512,512]{1,0:T(8,128)(2,1)S(1)}, bf16[512,512]{1,0:T(8,128)(2,1)S(1)}, u32[]{:S(2)}, u32[]{:S(2)}) collective-permute-start(bf16[512,512]{1,0:T(8,128)(2,1)S(1)} %collective-permute-done.1.rest_2_), channel_id=1, source_target_pairs={{0,120},{8,0},{16,8},{24,16},{32,24},{40,32},{48,40},{56,48},{64,5... | collective-permute-start | bytes 1572872 | tf_op jit(solution)/shard_map/ppermute | solution.py:357
  71.4 6.4 %collective-permute-start.7 = (bf16[256,512]{1,0:T(8,128)(2,1)S(1)}, bf16[256,512]{1,0:T(8,128)(2,1)S(1)}, u32[]{:S(2)}, u32[]{:S(2)}) collective-permute-start(bf16[256,512]{1,0:T(8,128)(2,1)S(1)} %pad_maximum_fusion.4.rest_5_), channel_id=1, source_target_pairs={{0,96},{8,104},{16,112},{24,120},{32,0},{40,8},{48,16},{56,24},{64... | collective-permute-start | bytes 786440 | tf_op jit(solution)/shard_map/ppermute | solution.py:357
  71.5 6.5 %collective-permute-start.8 = (bf16[256,512]{1,0:T(8,128)(2,1)S(1)}, bf16[256,512]{1,0:T(8,128)(2,1)S(1)}, u32[]{:S(2)}, u32[]{:S(2)}) collective-permute-start(bf16[256,512]{1,0:T(8,128)(2,1)S(1)} %pad_maximum_fusion.4.rest_5_), channel_id=1, source_target_pairs={{0,32},{8,40},{16,48},{24,56},{32,64},{40,72},{48,80},{56,88},{64,... | collective-permute-start | bytes 786440 | tf_op jit(solution)/shard_map/ppermute | solution.py:357
  78.0 5.4 %collective-permute-start.9 = (bf16[2,256,512]{2,1,0:T(8,128)(2,1)}, bf16[2,256,512]{2,1,0:T(8,128)(2,1)S(1)}, u32[]{:S(2)}, u32[]{:S(2)}) collective-permute-start(bf16[2,256,512]{2,1,0:T(8,128)(2,1)} %get-tuple-element.77), channel_id=1, source_target_pairs={{0,1},{1,0},{2,3},{3,2},{4,5},{5,4},{6,7},{7,6},{8,9},{9,8},{10,11... | collective-permute-start | bytes 1572872 | tf_op jit(solution)/shard_map/ppermute | solution.py:367
  81.7 5.2 %collective-permute-start.10 = (bf16[128,512]{1,0:T(8,128)(2,1)S(1)}, bf16[128,512]{1,0:T(8,128)(2,1)S(1)}, u32[]{:S(2)}, u32[]{:S(2)}) collective-permute-start(bf16[128,512]{1,0:T(8,128)(2,1)S(1)} %slice.82), channel_id=1, source_target_pairs={{0,96},{8,104},{16,112},{24,120},{32,0},{40,8},{48,16},{56,24},{64... | collective-permute-start | bytes 393224 | tf_op jit(solution)/shard_map/ppermute | solution.py:357
  81.8 6.2 %collective-permute-start.11 = (bf16[128,512]{1,0:T(8,128)(2,1)S(1)}, bf16[128,512]{1,0:T(8,128)(2,1)S(1)}, u32[]{:S(2)}, u32[]{:S(2)}) collective-permute-start(bf16[128,512]{1,0:T(8,128)(2,1)S(1)} %slice.83), channel_id=1, source_target_pairs={{0,32},{8,40},{16,48},{24,56},{32,64},{40,72},{48,80},{56,88},{64,... | collective-permute-start | bytes 393224 | tf_op jit(solution)/shard_map/ppermute | solution.py:357
  88.0 10.1 %collective-permute-start.12 = (bf16[256,512]{1,0:T(8,128)(2,1)S(1)}, bf16[256,512]{1,0:T(8,128)(2,1)S(1)}, u32[]{:S(2)}, u32[]{:S(2)}) collective-permute-start(bf16[256,512]{1,0:T(8,128)(2,1)S(1)} %get-tuple-element.88), channel_id=1, source_target_pairs={{0,2},{1,3},{2,4},{3,5},{4,6},{5,7},{6,0},{7,1},{8,10},{9,11},{10,... | collective-permute-start | bytes 786440 | tf_op jit(solution)/shard_map/ppermute | solution.py:370
  88.0 10.0 %collective-permute-start.13 = (bf16[256,512]{1,0:T(8,128)(2,1)S(1)}, bf16[256,512]{1,0:T(8,128)(2,1)S(1)}, u32[]{:S(2)}, u32[]{:S(2)}) collective-permute-start(bf16[256,512]{1,0:T(8,128)(2,1)S(1)} %get-tuple-element.89), channel_id=1, source_target_pairs={{0,6},{1,7},{2,0},{3,1},{4,2},{5,3},{6,4},{7,5},{8,14},{9,15},{10,... | collective-permute-start | bytes 786440 | tf_op jit(solution)/shard_map/ppermute | solution.py:370
  98.0 0.7 copy-start.7
  98.7 4.4 %collective-permute-start.14 = (bf16[5,256,512]{2,1,0:T(8,128)(2,1)}, bf16[5,256,512]{2,1,0:T(8,128)(2,1)S(1)}, u32[]{:S(2)}, u32[]{:S(2)}) collective-permute-start(bf16[5,256,512]{2,1,0:T(8,128)(2,1)} %get-tuple-element.90), channel_id=1, source_target_pairs={{0,1},{1,0},{2,3},{3,2},{4,5},{5,4},{6,7},{7,6},{8,9},{9,8},{10,11... | collective-permute-start | bytes 3932168 | tf_op jit(solution)/shard_map/ppermute | solution.py:367
  103.2 1.9 %copy-start.2 = (bf16[5,256,512]{2,1,0:T(8,128)(2,1)}, bf16[5,256,512]{2,1,0:T(8,128)(2,1)S(1)}, u32[]{:S(2)}) copy-start(bf16[5,256,512]{2,1,0:T(8,128)(2,1)S(1)} %collective-permute-done.14) | copy-start | bytes 3932164
  105.1 7.3 %copy-start.3 = (bf16[2,256,512]{2,1,0:T(8,128)(2,1)S(1)}, bf16[2,256,512]{2,1,0:T(8,128)(2,1)}, u32[]{:S(2)}) copy-start(bf16[2,256,512]{2,1,0:T(8,128)(2,1)} %get-tuple-element.86) | copy-start | bytes 1572868
  105.2 7.3 %copy-start.4 = (bf16[2,256,512]{2,1,0:T(8,128)(2,1)S(1)}, bf16[2,256,512]{2,1,0:T(8,128)(2,1)}, u32[]{:S(2)}) copy-start(bf16[2,256,512]{2,1,0:T(8,128)(2,1)} %get-tuple-element.92) | copy-start | bytes 1572868
  105.2 7.3 %copy-start.8 = (bf16[256,512]{1,0:T(8,128)(2,1)S(1)}, bf16[256,512]{1,0:T(8,128)(2,1)}, u32[]{:S(2)}) copy-start(bf16[256,512]{1,0:T(8,128)(2,1)} %copy-done.7) | copy-start | bytes 786436
  105.2 10.9 %collective-permute-start.15 = (bf16[352,512]{1,0:T(8,128)(2,1)S(1)}, bf16[352,512]{1,0:T(8,128)(2,1)S(1)}, u32[]{:S(2)}, u32[]{:S(2)}) collective-permute-start(bf16[352,512]{1,0:T(8,128)(2,1)S(1)} %pad_maximum_fusion), channel_id=1, source_target_pairs={{0,2},{1,3},{2,4},{3,5},{4,6},{5,7},{6,0},{7,1},{8,10},{9,11},{10,... | collective-permute-start | bytes 1081352 | tf_op jit(solution)/shard_map/ppermute | solution.py:370
  105.3 10.8 %collective-permute-start.16 = (bf16[352,512]{1,0:T(8,128)(2,1)S(1)}, bf16[352,512]{1,0:T(8,128)(2,1)S(1)}, u32[]{:S(2)}, u32[]{:S(2)}) collective-permute-start(bf16[352,512]{1,0:T(8,128)(2,1)S(1)} %pad_maximum_fusion.1), channel_id=1, source_target_pairs={{0,6},{1,7},{2,0},{3,1},{4,2},{5,3},{6,4},{7,5},{8,14},{9,15},{10,... | collective-permute-start | bytes 1081352 | tf_op jit(solution)/shard_map/ppermute | solution.py:370
  112.5 8.3 %copy-start.5 = (bf16[2,256,3,32]{1,3,2,0:T(8,128)(2,1)S(1)}, bf16[2,256,3,32]{1,3,2,0:T(8,128)(2,1)}, u32[]{:S(2)}) copy-start(bf16[2,256,3,32]{1,3,2,0:T(8,128)(2,1)} %tile.4) | copy-start | bytes 294916
  112.5 18.0 %copy-start.1 = (bf16[2,256,512]{2,1,0:T(8,128)(2,1)S(1)}, bf16[2,256,512]{2,1,0:T(8,128)(2,1)}, u32[]{:S(2)}) copy-start(bf16[2,256,512]{2,1,0:T(8,128)(2,1)} %get-tuple-element.94.kept_ref) | copy-start | bytes 1572868
  116.1 14.5 %collective-permute-start.17 = (bf16[2,256,512]{2,1,0:T(8,128)(2,1)}, bf16[2,256,512]{2,1,0:T(8,128)(2,1)S(1)}, u32[]{:S(2)}, u32[]{:S(2)}) collective-permute-start(bf16[2,256,512]{2,1,0:T(8,128)(2,1)} %get-tuple-element.98), channel_id=1, source_target_pairs={{0,1},{1,0},{2,3},{3,2},{4,5},{5,4},{6,7},{7,6},{8,9},{9,8},{10,11... | collective-permute-start | bytes 1572872 | tf_op jit(solution)/shard_map/ppermute | solution.py:367
  117.3 9.2 %collective-permute-start.19 = (bf16[288,512]{1,0:T(8,128)(2,1)S(1)}, bf16[288,512]{1,0:T(8,128)(2,1)S(1)}, u32[]{:S(2)}, u32[]{:S(2)}) collective-permute-start(bf16[288,512]{1,0:T(8,128)(2,1)S(1)} %pad_maximum_fusion.3), channel_id=1, source_target_pairs={{0,6},{1,7},{2,0},{3,1},{4,2},{5,3},{6,4},{7,5},{8,14},{9,15},{10,... | collective-permute-start | bytes 884744 | tf_op jit(solution)/shard_map/ppermute | solution.py:370
  120.8 9.7 %collective-permute-start.18 = (bf16[288,512]{1,0:T(8,128)(2,1)}, bf16[288,512]{1,0:T(8,128)(2,1)S(1)}, u32[]{:S(2)}, u32[]{:S(2)}) collective-permute-start(bf16[288,512]{1,0:T(8,128)(2,1)} %pad_maximum_fusion.2), channel_id=1, source_target_pairs={{0,2},{1,3},{2,4},{3,5},{4,6},{5,7},{6,0},{7,1},{8,10},{9,11},{10,... | collective-permute-start | bytes 884744 | tf_op jit(solution)/shard_map/ppermute | solution.py:370
